TPU v7x, 32 devices: a whole 2x2x4 slice. The times are simulated.
32 devices in a mesh: dp: 2 (over y), seq: 4 (over x, core), fsdp: 4 (over z).
Axes of the slice: x: 2, y: 2, z: 4, core: 2. Of those that a mesh axis runs over, the one named last changes fastest.
Arguments:
- tokens: bfloat16 [8, 1024, 2048], P(('dp', 'fsdp'), 'seq'), may hold values from -6 to 6
- lengths: int32 [8, 4], P(('dp', 'fsdp')), may hold values from 1 to 769, 1024 in all within a row
- norm_gain: float32 [2048], replicated, may hold values from 0.5 to 1.5
- w_in: bfloat16 [2048, 8448], P(('dp', 'seq', 'fsdp')), may hold values from -0.125 to 0.125
- w_dt: bfloat16 [2048, 64], P(('dp', 'seq', 'fsdp')), may hold values from -0.25 to 0.25
- conv_w: float32 [4, 4352], replicated, may hold values from -3 to 3
- conv_b: float32 [4352], replicated, may hold values from -0.5 to 0.5
- dt_bias: float32 [64], replicated, may hold values from -5 to -3
- a_log: float32 [64], replicated, may hold values from -6 to 0
- skip: float32 [64], replicated, may hold values from 0.5 to 1.5
- gate_gain: float32 [4096], replicated, may hold values from 0.5 to 1.5
- w_out: bfloat16 [4096, 2048], P(('dp', 'seq', 'fsdp')), may hold values from -0.125 to 0.125
- cotangent: bfloat16 [4, 8, 1024, 2048], P(None, ('dp', 'fsdp'), 'seq'), may hold values from -6 to 6
Outputs:
- mixed: bfloat16 [4, 8, 1024, 2048], P(None, ('dp', 'fsdp'), 'seq')
- grad_tokens: bfloat16 [8, 1024, 2048], P(('dp', 'fsdp'), 'seq')
- grad_norm_gain: float32 [2048], replicated
- grad_w_in: float32 [2048, 8448], P(('dp', 'seq', 'fsdp'))
- grad_w_dt: float32 [2048, 64], P(('dp', 'seq', 'fsdp'))
- grad_conv_w: float32 [4, 4352], replicated
- grad_conv_b: float32 [4352], replicated
- grad_dt_bias: float32 [64], replicated
- grad_a_log: float32 [64], replicated
- grad_skip: float32 [64], replicated
- grad_gate_gain: float32 [4096], replicated
- grad_w_out: float32 [4096, 2048], P(('dp', 'seq', 'fsdp'))
Inputs may be any that keep to these rules, and one draw needn't show every extreme that they name: `lengths`: each row sums to 1024; each sequence holds one document of exactly 769 tokens.
All inputs are finite; a program needn't handle non-finite values.
Results may differ from a plain program's by a relative error of at most 0.014.
Values may be sent and summed in bfloat16 or wider, within the bound.
No kernel may reach another device: no remote copies, remote signals or barrier semaphores. Data moves between devices by JAX's collectives and lax.ppermute only.
A program may use at most 512 MiB of HBM per device.

v0:
```python
import functools

import jax
import jax.numpy as jnp
import numpy as np
from jax import lax
from jax.experimental import pallas as pl
from jax.experimental.pallas import tpu as pltpu
from jax.sharding import PartitionSpec as P

D = 2048
HEADS = 64
HEADDIM = 64
STATE = 128
CONV = 4
SPAN = 128
INNER = 4096
EPS = 1e-05
LEVELS = 4
BF = jnp.bfloat16
F32 = jnp.float32
HIGH = lax.Precision.HIGHEST
LANES = 128
HALO = 16
TILE = 256
VMEM_LIMIT = 48 * 1024 * 1024


def dot(a, b, dims=((1,), (0,)), precision=None):
    return lax.dot_general(a, b, (dims, ((), ())), preferred_element_type=F32, precision=precision)


def silu_slope(v):
    sig = jax.nn.sigmoid(v)
    return sig * (1.0 + v * (1.0 - sig))


def level_of(head):
    return 0 if head < 8 else 1 if head < 16 else 2 if head < 32 else 3


def swapped(value, axis, k, keep=None):
    pairs = [(i, i ^ k) for i in range(lax.axis_size(axis))]
    if keep is not None:
        pairs = [p for p in pairs if keep(*p)]
    return lax.ppermute(value, axis, pairs)


def after(value, *others):
    return lax.optimization_barrier((value,) + others)[0]


def together(*values):
    return lax.optimization_barrier(values)


def flattened(vectors):
    flat = jnp.concatenate(vectors)
    return jnp.pad(flat, (0, -flat.shape[0] % 1024)).reshape(-1, LANES)


def butterfly(value, axis):
    k = 1
    while k < lax.axis_size(axis):
        value = value + swapped(value, axis, k)
        k *= 2
    return value


def picked(array, index):
    return lax.dynamic_index_in_dim(array, index, 0, keepdims=False)


def seq_gather(block, here):
    return jnp.stack(reordered_by_xor([block] + [swapped(block, "seq", k) for k in range(1, 4)], here))


def reordered_by_xor(pieces, here):
    k = 1
    while k < len(pieces):
        flip = (here & k) > 0
        pieces = [jnp.where(flip, pieces[j ^ k], piece) for j, piece in enumerate(pieces)]
        k *= 2
    return pieces


def call(kernel, **kwargs):
    return pl.pallas_call(
        kernel,
        compiler_params=pltpu.CompilerParams(vmem_limit_bytes=VMEM_LIMIT),
        cost_estimate=pl.CostEstimate(flops=1, bytes_accessed=1, transcendentals=0),
        **kwargs,
    )


def filled(shape, moves):
    arrays, plan, rows = [], [], []
    block = tuple(size if index is None else 1 for size, index in zip(shape, moves[0][2]))
    for piece, lead, place in moves:
        at = next((i for i, a in enumerate(arrays) if a is piece), len(arrays))
        if at == len(arrays):
            arrays.append(piece)
        plan.append((at, lead))
        rows.append(jnp.stack([jnp.asarray(0 if n is None else n, jnp.int32) for n in place]))

    def kernel(index_ref, *refs):
        pieces, out = refs[:-1], refs[-1]
        for m, (at, lead) in enumerate(plan):

            @pl.when(pl.program_id(0) == m)
            def _():
                value = pieces[at][...] if lead is None else pieces[at][lead]
                out[...] = value.reshape(block)

    return call(
        kernel,
        grid_spec=pltpu.PrefetchScalarGridSpec(
            num_scalar_prefetch=1,
            grid=(len(plan),),
            in_specs=[
                pl.BlockSpec(a.shape, lambda i, t, n=a.ndim: (0,) * n) for a in arrays
            ],
            out_specs=pl.BlockSpec(
                block, lambda i, t: tuple(t[i, n] for n in range(len(shape)))
            ),
        ),
        out_shape=jax.ShapeDtypeStruct(shape, arrays[0].dtype),
        name="filled",
    )(jnp.stack(rows), *arrays)


def terms_kernel(ns, nf, at_ref, left_ref, right_ref, out_ref):
    value = dot(left_ref[...], right_ref[...]).astype(BF)
    rows = value.shape[0] // (ns * nf)
    for i in range(ns):
        for k in range(nf):
            out_ref[k, i] = value[(i * nf + k) * rows : (i * nf + k + 1) * rows]


def row_terms(turned, right, at, nd, ns, nf, first, columns):
    depth = turned.shape[1]
    rows = turned.shape[0] // nd
    wide = TILE if columns % TILE == 0 else LANES
    return call(
        functools.partial(terms_kernel, ns, nf),
        grid_spec=pltpu.PrefetchScalarGridSpec(
            num_scalar_prefetch=1,
            grid=(columns // wide,),
            in_specs=[
                pl.BlockSpec((rows, depth), lambda i, t: (t[0], 0)),
                pl.BlockSpec((depth, wide), lambda i, t: (0, i + first // wide)),
            ],
            out_specs=pl.BlockSpec((nf, ns, rows // (nf * ns), wide), lambda i, t: (0, 0, 0, i)),
        ),
        out_shape=jax.ShapeDtypeStruct((nf, ns, rows // (nf * ns), columns), BF),
        name="row_terms",
    )(at.astype(jnp.int32)[None], turned, right)


def small_back_kernel(
    width, pre_ref, dbc_ref, in_ref, mask_ref, weight_ref, ddt_ref, pre_dt_ref, out_ref, sum_ref, ext, dext
):
    rows = pre_ref.shape[0]
    ext[0:HALO] = jnp.zeros((HALO, LANES), F32)
    ext[HALO:] = in_ref[...].astype(F32)
    pre = pre_ref[...]
    sig = jax.nn.sigmoid(pre)
    dpre = dbc_ref[...] * (sig * (1.0 + pre * (1.0 - sig)))
    dext[0:rows] = dpre
    dext[rows:] = jnp.zeros((HALO, LANES), F32)
    total = dpre * weight_ref[CONV - 1 : CONV, :]
    for k in range(CONV):
        term = ext[pl.ds(HALO - CONV + 1 + k, rows), :]
        if k < CONV - 1:
            term = term * mask_ref[:, k : k + 1]
            later = dext[pl.ds(CONV - 1 - k, rows), :] * mask_ref[:, CONV - 1 + k : CONV + k]
            total = total + later * weight_ref[k : k + 1, :]
        sum_ref[k : k + 1, :] = jnp.sum(dpre * term, axis=0, keepdims=True)
    sum_ref[CONV : CONV + 1, :] = jnp.sum(dpre, axis=0, keepdims=True)
    draw = ddt_ref[...] * jax.nn.sigmoid(pre_dt_ref[...])
    sum_ref[CONV + 1 : CONV + 2, :] = jnp.sum(draw, axis=0, keepdims=True)
    out_ref[...] = (total + pltpu.roll(draw, width, axis=1)).astype(BF)


def small_back(width, pre, dbc, proj, masks, weight, ddt, pre_dt):
    rows = pre.shape[0]
    return call(
        functools.partial(small_back_kernel, width),
        out_shape=[
            jax.ShapeDtypeStruct((rows, LANES), BF),
            jax.ShapeDtypeStruct((8, LANES), F32),
        ],
        scratch_shapes=[pltpu.VMEM((HALO + rows, LANES), F32), pltpu.VMEM((rows + HALO, LANES), F32)],
        name="small_back",
    )(pre, dbc, proj, masks, weight, ddt, pre_dt)


def input_grad_kernel(blocks, dz_ref, ds_ref, dr_ref, wz_ref, wa_ref, wb_ref, out_ref):
    half = wb_ref.shape[1]
    columns = ((1,), (1,))
    total = dot(dz_ref[...], wz_ref[...], columns)
    total = total + dot(ds_ref[:, :half], wa_ref[:, :half], columns)
    total = total + dot(ds_ref[:, half:], wb_ref[...], columns)
    total = total + dot(dr_ref[...], wa_ref[:, half:], columns)
    total = total.astype(BF)
    tok = total.shape[0] // blocks
    for i in range(blocks):
        out_ref[i] = total[i * tok : (i + 1) * tok]


def input_grad(dz, ds, dr, wz, wa, wb, blocks, tok):
    def whole(a):
        return pl.BlockSpec(a.shape, lambda i: (0, 0))

    def rows(a):
        return pl.BlockSpec((TILE, a.shape[1]), lambda i: (i, 0))

    return call(
        functools.partial(input_grad_kernel, blocks),
        grid=(wz.shape[0] // TILE,),
        in_specs=[whole(dz), whole(ds), whole(dr), rows(wz), rows(wa), rows(wb)],
        out_specs=pl.BlockSpec((blocks, tok, TILE), lambda i: (0, 0, i)),
        out_shape=jax.ShapeDtypeStruct((blocks, tok, wz.shape[0]), BF),
        name="input_grad",
    )(dz, ds, dr, wz, wa, wb)


def assembled(here_ref, pieces, nd, full_ref):
    halves = len(pieces) // nd
    nf, ns, rows = pieces[0].shape[:3]
    for n, piece in enumerate(pieces):
        h, j = divmod(n, nd)
        for k in range(nf):
            for i in range(ns):
                block = ((here_ref[1] ^ j) * ns + i) * nf + k
                at = pl.multiple_of((block * halves + h) * rows, rows)
                full_ref[pl.ds(at, rows), :] = piece[k, i]


def project_kernel(nd, count, here_ref, xn_ref, *refs):
    pieces, (out_ref, full_ref) = refs[:count], refs[count:]
    if nd:
        assembled(here_ref, pieces, nd, full_ref)
    else:
        full_ref[...] = pieces[0][...]
    out_ref[...] = dot(xn_ref[...], full_ref[...]).astype(BF)


def gated_kernel(nd, count, starts, wide, here_ref, xn_ref, y_ref, gain_ref, *refs):
    pieces, (out_ref, full_ref, gated_ref, turned_ref, squares_ref, sums) = refs[:count], refs[count:]
    step = pl.program_id(0)

    @pl.when(step == 0)
    def _():
        sums[...] = jnp.zeros_like(sums)

    if nd:
        assembled(here_ref, pieces, nd, full_ref)
    else:
        full_ref[...] = pieces[0][...]
    value = dot(xn_ref[...], full_ref[...]).astype(BF)
    out_ref[...] = value
    where = tile_range(starts, wide, step)
    for c in range(0, wide, LANES):
        at = slice(c, c + LANES)
        z = value[:, at].astype(F32)
        q = y_ref[:, at] * (z * jax.nn.sigmoid(z))
        gated = (q * gain_ref[:, at]).astype(BF)
        gated_ref[:, at] = gated
        turned_ref[at, :] = gated.T
        sums[where] += q * q

    @pl.when(step == pl.num_programs(0) - 1)
    def _():
        lane = lax.broadcasted_iota(jnp.int32, sums.shape[1:], 1)
        total = jnp.zeros(sums.shape[1:], F32)
        for j in range(len(starts)):
            total = jnp.where(lane == j, jnp.sum(sums[j], axis=1, keepdims=True), total)
        squares_ref[...] = total.T[: squares_ref.shape[0]]


def projections(here, xn, pieces, nd, rows, columns, gate=None):
    if pieces[0].ndim == 2:
        nd = 0
    wide = TILE if columns % TILE == 0 else LANES
    if gate is not None:
        y, gain, starts, wide = gate
    tokens, depth = xn.shape
    outs = [pl.BlockSpec((tokens, wide), lambda i: (0, i)), pl.BlockSpec((depth, wide), lambda i: (0, i))]
    shapes = [jax.ShapeDtypeStruct((tokens, columns), BF), jax.ShapeDtypeStruct((depth, columns), BF)]
    ins = [pl.BlockSpec(memory_space=pltpu.SMEM), pl.BlockSpec((tokens, depth), lambda i: (0, 0))]
    operands = [here, xn]
    scratch = []
    kernel = functools.partial(project_kernel, nd, len(pieces))
    if gate is not None:
        kernel = functools.partial(gated_kernel, nd, len(pieces), starts, wide)
        operands += [y, gain]
        ins += [outs[0], pl.BlockSpec((1, wide), lambda i: (0, i))]
        outs += [
            outs[0],
            pl.BlockSpec((wide, tokens), lambda i: (i, 0)),
            pl.BlockSpec((8, tokens), lambda i: (0, 0)),
        ]
        shapes += [
            shapes[0],
            jax.ShapeDtypeStruct((columns, tokens), BF),
            jax.ShapeDtypeStruct((8, tokens), F32),
        ]
        scratch = [pltpu.VMEM((len(starts), tokens, LANES), F32)]
    for piece in pieces:
        lead = piece.shape[:-1]
        ins.append(pl.BlockSpec(lead + (wide,), lambda i, n=len(lead): (0,) * n + (i,)))
    return call(
        kernel,
        grid=(columns // wide,),
        in_specs=ins,
        out_specs=outs,
        out_shape=shapes,
        scratch_shapes=scratch,
        name="gated" if gate is not None else "project",
    )(*operands, *pieces)


def tri(rows_first):
    a = lax.broadcasted_iota(jnp.int32, (SPAN, SPAN), 0)
    b = lax.broadcasted_iota(jnp.int32, (SPAN, SPAN), 1)
    return (a >= b) if rows_first else (a <= b)


def pair_of(lo, cols, p):
    return jnp.where(lo, cols[:, 2 * p : 2 * p + 1], cols[:, 2 * p + 1 : 2 * p + 2])


def decays(segc, segr, segp, dt, rate):
    cum = dot(tri(True).astype(F32), dt * rate, precision=HIGH)
    last = cum[SPAN - 1 : SPAN, :]
    keep = jnp.where(segc == segp, jnp.exp(cum), 0.0)
    to_end = jnp.where(segc == segr[:, SPAN - 1 : SPAN], jnp.exp(last - cum), 0.0)
    return cum, cum.T, keep, to_end


def spread_columns(ref, first, count):
    return [jnp.broadcast_to(ref[:, first + k : first + k + 1], (SPAN, LANES)) for k in range(count)]


def taps(ext, masks, at):
    terms = [ext[pl.ds(HALO - CONV + 1 + k, SPAN), at] for k in range(CONV)]
    return [t * m for t, m in zip(terms, masks)] + terms[CONV - 1 :]


def convolved(terms, weight_ref, at):
    total = weight_ref[CONV : CONV + 1, at] + terms[0] * weight_ref[0:1, at]
    for k in range(1, CONV):
        total = total + terms[k] * weight_ref[k : k + 1, at]
    return total


def forward_kernel(
    heads,
    segp_ref,
    segc_ref,
    segr_ref,
    mask_ref,
    in_a_ref,
    in_b_ref,
    halo_ref,
    weight_ref,
    b_ref,
    c_ref,
    dt_ref,
    rate_ref,
    skip_ref,
    y_ref,
    prior_ref,
    carry,
    to_end_u,
    ext,
):
    block = pl.program_id(0)
    width = heads * HEADDIM

    @pl.when(block == 0)
    def _():
        carry[...] = jnp.zeros_like(carry)

    prior_ref[0] = carry[...]
    ext[0:HALO] = halo_ref[0].astype(F32)
    half = in_b_ref.shape[1]
    ext[HALO:, :half] = in_a_ref[:, :half].astype(F32)
    ext[HALO:, half:] = in_b_ref[...].astype(F32)
    segc, segr = segc_ref[...], segr_ref[...]
    dt = dt_ref[...]
    cum, cumr, keep, to_end = decays(segc, segr, segp_ref[block], dt, rate_ref[...])
    bm, cm = b_ref[...], c_ref[...]
    mixing = dot(cm, bm, ((1,), (1,)))
    mixing = jnp.where(tri(True) & (segc == segr), mixing, 0.0)
    masks = spread_columns(mask_ref, 0, CONV - 1)
    lo = lax.broadcasted_iota(jnp.int32, (SPAN, LANES), 1) < HEADDIM
    for p in range(heads // 2):
        at = slice(p * LANES, (p + 1) * LANES)
        pre = convolved(taps(ext, masks, at), weight_ref, at)
        x2 = pre * jax.nn.sigmoid(pre)
        u2 = x2 * pair_of(lo, dt, p)
        ub = u2.astype(BF)
        total = dot(cm, carry[:, at].astype(BF)) * pair_of(lo, keep, p) + skip_ref[:, at] * x2
        inner = []
        for h in (2 * p, 2 * p + 1):
            decay = jnp.exp(jnp.minimum(cum[:, h : h + 1] - cumr[h : h + 1, :], 0.0))
            inner.append(dot((decay * mixing).astype(BF), ub))
        y_ref[:, at] = total + jnp.where(lo, inner[0], inner[1])
        to_end_u[:, at] = (u2 * pair_of(lo, to_end, p)).astype(BF)
    fresh = dot(bm, to_end_u[...], ((0,), (0,)))
    lo_row = lax.broadcasted_iota(jnp.int32, (1, LANES), 1) < HEADDIM
    for p in range(heads // 2):
        at = slice(p * LANES, (p + 1) * LANES)
        factor = pair_of(lo_row, keep[SPAN - 1 : SPAN, :], p)
        carry[:, at] = factor * carry[:, at] + fresh[:, at]


def split_dot(value, ones):
    high = value.astype(BF)
    low = (value - high.astype(F32)).astype(BF)
    return dot(high, ones) + dot(low, ones)


def backward_kernel(
    heads,
    segp_ref,
    segc_ref,
    segr_ref,
    mask_ref,
    in_a_ref,
    in_b_ref,
    halo_ref,
    weight_ref,
    b_ref,
    c_ref,
    dt_ref,
    rate_ref,
    skip_ref,
    y_ref,
    prior_ref,
    dy_ref,
    din_ref,
    dbc_ref,
    ddt_ref,
    drate_ref,
    dsum_ref,
    dcarry,
    after_state,
    keep_dy,
    to_end_u,
    slopes,
    along,
    ext,
    dext,
):
    step = pl.program_id(0)
    block = pl.num_programs(0) - 1 - step

    @pl.when(step == 0)
    def _():
        dcarry[...] = jnp.zeros_like(dcarry)
        after_state[...] = jnp.zeros_like(after_state)
        drate_ref[...] = jnp.zeros_like(drate_ref)
        dsum_ref[...] = jnp.zeros_like(dsum_ref)
        dext[SPAN:] = jnp.zeros((HALO, dext.shape[1]), F32)

    ext[0:HALO] = halo_ref[0].astype(F32)
    half = in_b_ref.shape[1]
    ext[HALO:, :half] = in_a_ref[:, :half].astype(F32)
    ext[HALO:, half:] = in_b_ref[...].astype(F32)
    segc, segr = segc_ref[...], segr_ref[...]
    dt = dt_ref[...]
    cum, cumr, keep, to_end = decays(segc, segr, segp_ref[block], dt, rate_ref[...])
    bm, cm = b_ref[...], c_ref[...]
    allowed = tri(False) & (segc == segr)
    mixing = jnp.where(allowed, dot(bm, cm, ((1,), (1,))), 0.0)
    masks = spread_columns(mask_ref, 0, CONV - 1)
    moved = spread_columns(mask_ref, CONV - 1, CONV - 1)
    lo = lax.broadcasted_iota(jnp.int32, (SPAN, LANES), 1) < HEADDIM
    dmixing = jnp.zeros((SPAN, SPAN), F32)
    for p in range(heads // 2):
        at = slice(p * LANES, (p + 1) * LANES)
        terms = taps(ext, masks, at)
        pre = convolved(terms, weight_ref, at)
        sig = jax.nn.sigmoid(pre)
        x2 = pre * sig
        dt2 = pair_of(lo, dt, p)
        u2 = x2 * dt2
        dyb = dy_ref[:, at]
        dy2 = dyb.astype(F32)
        skip = skip_ref[:, at]
        te2 = pair_of(lo, to_end, p)
        u_sides = (jnp.where(lo, u2, 0.0).astype(BF), jnp.where(lo, 0.0, u2).astype(BF))
        du = te2 * dot(bm, dcarry[:, at].astype(BF))
        inner = []
        for k in range(2):
            h = 2 * p + k
            decay = jnp.exp(jnp.minimum(cumr[h : h + 1, :] - cum[:, h : h + 1], 0.0))
            inner.append(dot((decay * mixing).astype(BF), dyb))
            dmixing = dmixing + decay * dot(u_sides[k], dyb, ((1,), (1,)))
        du = du + jnp.where(lo, inner[0], inner[1])
        keep_dy[:, at] = (pair_of(lo, keep, p) * dy2).astype(BF)
        to_end_u[:, at] = (te2 * u2).astype(BF)
        slopes[:, at] = dy2 * (y_ref[:, at] - skip * x2) - u2.astype(BF).astype(F32) * du
        along[:, at] = x2 * du
        dpre = (dt2 * du + skip * dy2) * (sig * (1.0 + pre * (1.0 - sig)))
        dext[0:SPAN, at] = dpre
        for k in range(CONV):
            dsum_ref[k : k + 1, at] += jnp.sum(dpre * terms[k], axis=0, keepdims=True)
        dsum_ref[CONV : CONV + 1, at] += jnp.sum(dpre, axis=0, keepdims=True)
        dsum_ref[CONV + 1 : CONV + 2, at] += jnp.sum(dy2 * x2, axis=0, keepdims=True)
        din = dpre * weight_ref[CONV - 1 : CONV, at]
        for k in range(CONV - 1):
            later = dext[pl.ds(CONV - 1 - k, SPAN), at]
            din = din + later * moved[k] * weight_ref[k : k + 1, at]
        din_ref[:, at] = din.astype(BF)
    dext[SPAN:] = dext[0:HALO]
    dmixing = jnp.where(allowed, dmixing, 0.0).astype(BF)
    dstate = dcarry[...].astype(BF)
    prior = prior_ref[0]
    dbc_ref[:, :STATE] = dot(dmixing, cm) + dot(to_end_u[...], dstate, ((1,), (1,)))
    dbc_ref[:, STATE:] = dot(dmixing, bm, ((0,), (0,))) + dot(
        keep_dy[...], prior.astype(BF), ((1,), (1,))
    )
    width = heads * HEADDIM
    ones = (
        lax.broadcasted_iota(jnp.int32, (width, LANES), 0) // HEADDIM
        == lax.broadcasted_iota(jnp.int32, (width, LANES), 1)
    ).astype(BF)
    at_end = jnp.sum(dcarry[...] * after_state[...], axis=0, keepdims=True)
    at_end = split_dot(jnp.broadcast_to(at_end, (16, width)), ones)[:1]
    dcum = split_dot(slopes[...], ones)
    da = dot(tri(False).astype(F32), dcum, precision=HIGH) + at_end
    ddt_ref[...] = rate_ref[...] * da + split_dot(along[...], ones)
    drate_ref[...] += jnp.sum(dt * da, axis=0, keepdims=True)
    fresh = dot(cm, keep_dy[...], ((0,), (0,)))
    lo_row = lax.broadcasted_iota(jnp.int32, (1, LANES), 1) < HEADDIM
    for p in range(heads // 2):
        at = slice(p * LANES, (p + 1) * LANES)
        factor = pair_of(lo_row, keep[SPAN - 1 : SPAN, :], p)
        dcarry[:, at] = factor * dcarry[:, at] + fresh[:, at]
    after_state[...] = prior


def scan_specs(heads, at, in_widths):
    width = heads * HEADDIM

    def rows(n):
        return pl.BlockSpec((SPAN, n), lambda i: (at(i), 0))

    def whole(*shape):
        return pl.BlockSpec(shape, lambda i: (0,) * len(shape))

    ins = [
        pl.BlockSpec(memory_space=pltpu.SMEM),
        rows(1),
        pl.BlockSpec((1, SPAN), lambda i: (0, at(i))),
        rows(LANES),
        rows(in_widths[0]),
        rows(in_widths[1]),
        pl.BlockSpec((1, HALO, width), lambda i: (at(i), 0, 0)),
        whole(8, width),
        rows(STATE),
        rows(STATE),
        rows(LANES),
        whole(1, LANES),
        whole(1, width),
    ]
    prior = pl.BlockSpec((1, STATE, width), lambda i: (at(i), 0, 0))
    return rows, whole, ins, prior


def scan_forward(heads, blocks, operands):
    rows, whole, ins, prior = scan_specs(heads, lambda i: i, [operands[n].shape[1] for n in (4, 5)])
    width = heads * HEADDIM
    return call(
        functools.partial(forward_kernel, heads),
        grid=(blocks,),
        in_specs=ins,
        out_specs=[rows(width), prior],
        out_shape=[
            jax.ShapeDtypeStruct((blocks * SPAN, width), F32),
            jax.ShapeDtypeStruct((blocks, STATE, width), F32),
        ],
        scratch_shapes=[
            pltpu.VMEM((STATE, width), F32),
            pltpu.VMEM((SPAN, width), BF),
            pltpu.VMEM((HALO + SPAN, width), F32),
        ],
        name="scan_forward",
    )(*operands)


def scan_backward(heads, blocks, operands, y, priors, dy):
    rows, whole, ins, prior = scan_specs(
        heads, lambda i: blocks - 1 - i, [operands[n].shape[1] for n in (4, 5)]
    )
    width = heads * HEADDIM
    return call(
        functools.partial(backward_kernel, heads),
        grid=(blocks,),
        in_specs=ins + [rows(width), prior, rows(width)],
        out_specs=[rows(width), rows(2 * STATE), rows(LANES), whole(1, LANES), whole(8, width)],
        out_shape=[
            jax.ShapeDtypeStruct((blocks * SPAN, width), BF),
            jax.ShapeDtypeStruct((blocks * SPAN, 2 * STATE), F32),
            jax.ShapeDtypeStruct((blocks * SPAN, LANES), F32),
            jax.ShapeDtypeStruct((1, LANES), F32),
            jax.ShapeDtypeStruct((8, width), F32),
        ],
        scratch_shapes=[
            pltpu.VMEM((STATE, width), F32),
            pltpu.VMEM((STATE, width), F32),
            pltpu.VMEM((SPAN, width), BF),
            pltpu.VMEM((SPAN, width), BF),
            pltpu.VMEM((SPAN, width), F32),
            pltpu.VMEM((SPAN, width), F32),
            pltpu.VMEM((HALO + SPAN, width), F32),
            pltpu.VMEM((SPAN + HALO, width), F32),
        ],
        name="scan_backward",
    )(*operands, y, priors, dy)


def as_columns(rows):
    few, tokens = rows.shape
    return jnp.concatenate([rows, jnp.zeros((LANES - few, tokens), F32)]).T


def level_block(pieces, spot):
    piece, lead = spot
    return pieces[piece][lead + (slice(None), slice(None))].astype(F32)


def upper_kernel(where, plan, nd, tok, ns, here_ref, range_ref, count_ref, ratio_ref, q_turned, *refs):
    count = 3 + 2 * LEVELS
    pieces, outs = refs[:count], refs[count:]
    upper_ref, grad_refs, coefs = outs[0], outs[1 : 2 * nd], outs[2 * nd]

    @pl.when(pl.program_id(0) == 0)
    def _():
        rows = [count_ref[j, w] * ratio_ref[w : w + 1, :] for j in range(len(plan)) for w in range(LEVELS)]
        coefs[...] = as_columns(jnp.concatenate(rows))

    for k in range(ns):
        at = here_ref[0] ^ k
        rows = pl.ds(pl.multiple_of(at * tok, tok), tok)
        levels = [level_block(pieces, where[w][k]) for w in range(LEVELS)]
        for j in range(len(plan)):
            total = None
            for w in plan[j]:
                n = j * LEVELS + w
                term = coefs[rows, n : n + 1] * levels[w]
                total = term if total is None else total + term
            upper_ref[j, rows, :] = total.astype(BF)
    count = q_turned.shape[0] // nd
    for k in range(nd):
        index = here_ref[1] ^ k
        rows = pl.ds(pl.multiple_of(index * count, count), count)
        value = dot(q_turned[rows, :], upper_ref[range_ref[index]]).astype(BF)
        if k:
            grad_refs[2 * k - 1][...] = value[: count // 2]
            grad_refs[2 * k][...] = value[count // 2 :]
        else:
            grad_refs[0][...] = value


def products_kernel(where, plan, lanes, tok, ns, nd, here_ref, count_ref, q_ref, *refs):
    count = 3 + 2 * LEVELS
    held_ref, pieces, outs = refs[0], refs[1 : 1 + count], refs[1 + count :]
    prod_refs, inner_ref, w_ref, sums = outs[:ns], outs[ns], outs[ns + 1], outs[ns + 2]
    step = pl.program_id(0)
    rows_of = w_ref.shape[0] // nd
    for k in range(nd):
        at = pl.multiple_of((here_ref[1] ^ k) * rows_of, rows_of)
        w_ref[pl.ds(at, rows_of), :] = held_ref[:, k].reshape(rows_of, w_ref.shape[1])

    @pl.when(step == 0)
    def _():
        sums[...] = jnp.zeros_like(sums)

    for k in range(ns):
        at = here_ref[0] ^ k
        rows = pl.ds(pl.multiple_of(at * tok, tok), tok)
        values = [dot(q_ref[rows, a:b], w_ref[a:b, :]) for a, b in lanes]
        for j, value in enumerate(values):
            prod_refs[k][j] = value.astype(BF)
        for w in range(LEVELS):
            total = None
            for j in range(len(lanes)):
                if w in plan[j]:
                    term = values[j] * count_ref[j, w]
                    total = term if total is None else total + term
            part = total * level_block(pieces, where[w][k])
            folded = part[:, :LANES]
            for c in range(LANES, part.shape[1], LANES):
                folded = folded + part[:, c : c + LANES]
            sums[w, rows, :] += folded

    @pl.when(step == pl.num_programs(0) - 1)
    def _():
        lane = lax.broadcasted_iota(jnp.int32, sums.shape[1:], 1)
        total = jnp.zeros(sums.shape[1:], F32)
        for w in range(LEVELS):
            total = jnp.where(lane == w, jnp.sum(sums[w], axis=1, keepdims=True), total)
        inner_ref[...] = total.T[:LEVELS]


def gate_kernel(
    starts, wide, count_ref, upper_ref, w_ref, y_ref, z_ref, gain_ref, ratio_ref, mean_ref, dy_ref, dz_ref, grad_ref, coefs
):
    step = pl.program_id(0)

    @pl.when(step == 0)
    def _():
        cubes = ratio_ref[...] * ratio_ref[...] * ratio_ref[...] * mean_ref[...]
        rows = []
        for j in range(len(starts)):
            total = cubes[0:1] * count_ref[j, 0]
            for w in range(1, LEVELS):
                total = total + cubes[w : w + 1] * count_ref[j, w]
            rows.append(total)
        columns = as_columns(jnp.concatenate(rows))
        for j in range(len(starts)):
            coefs[j] = jnp.broadcast_to(columns[:, j : j + 1], coefs.shape[1:])

    grad_all = dot(upper_ref[0], w_ref[...], ((1,), (1,)))
    coef = coefs[tile_range(starts, wide, step)]
    for c in range(0, wide, LANES):
        at = slice(c, c + LANES)
        grad_t = grad_all[:, at]
        z = z_ref[:, at].astype(F32)
        sig = jax.nn.sigmoid(z)
        act = z * sig
        y = y_ref[:, at]
        q = y * act
        dq = gain_ref[:, at] * grad_t - q * coef
        dy_ref[:, at] = (dq * act).astype(BF)
        dz_ref[:, at] = (dq * y * (sig * (1.0 + z * (1.0 - sig)))).astype(BF)
        grad_ref[0:1, at] = jnp.sum(q * grad_t, axis=0, keepdims=True)


def tile_range(starts, wide, step):
    index = 0
    for start in starts[1:]:
        index = index + jnp.where(step * wide >= start, 1, 0)
    return index


def mixed_kernel(plan, ns, tok, here_ref, count_ref, ratio_ref, x_ref, *refs):
    shares, out_ref = refs[:-1], refs[-1]
    at = pl.ds(pl.multiple_of(here_ref[0] * tok, tok), tok)
    ratios = as_columns(ratio_ref[:, at])
    x = x_ref[...].astype(F32)
    for w in range(LEVELS):
        total = None
        for k in range(ns):
            for j in plan[w]:
                term = shares[k][j].astype(F32) * count_ref[k, j * LEVELS + w]
                total = term if total is None else total + term
        out_ref[w] = (x + ratios[:, w : w + 1] * total).astype(BF)


def dp_terms(others):
    return [swapped(other, "dp", k + 1) for k, other in enumerate(others)]


def over_seq(value):
    dense = value.reshape(-1, LANES)
    total = dense
    for k in range(1, lax.axis_size("seq")):
        total = total + swapped(dense, "seq", k)
    return total.reshape(value.shape)


def fsdp_half(own, got):
    nf = lax.axis_size("fsdp")
    f = lax.axis_index("fsdp")

    def part(offset):
        total = picked(own, f ^ offset).astype(F32)
        for other in got:
            total = total + picked(other, f ^ offset).astype(F32)
        return total.astype(BF)

    kept = jnp.stack([part(e) for e in range(0, nf, 2)])
    sent = jnp.stack([part(e ^ 1) for e in range(0, nf, 2)])
    return kept, sent


def fsdp_rest(kept, got):
    k = 2
    while k < lax.axis_size("fsdp"):
        total = (kept.astype(F32) + got.astype(F32)).astype(BF)
        kept, sent = total[::2], total[1::2]
        got = swapped(sent, "fsdp", k)
        k *= 2
    return kept[0], got[0]


def shards(
    tokens,
    lengths,
    norm_gain,
    w_in,
    w_dt,
    conv_w,
    conv_b,
    dt_bias,
    a_log,
    skip,
    gate_gain,
    w_out,
    cotangent,
):
    nd, ns, nf = lax.axis_size("dp"), lax.axis_size("seq"), lax.axis_size("fsdp")
    d, s, f = lax.axis_index("dp"), lax.axis_index("seq"), lax.axis_index("fsdp")
    tok = tokens.shape[1]
    length = ns * tok
    blocks = length // SPAN
    heads = HEADS // ns
    run = heads // nd
    width = heads * HEADDIM
    own_bc = 2 * STATE // ns
    used = width + own_bc
    cols = -(-(used + heads) // LANES) * LANES
    rows_in = w_in.shape[0]
    reach = CONV - 1

    levels = np.array(
        [[level_of(dd * (HEADS // nd) + ss * run + i) for dd in range(nd) for i in range(run)] for ss in range(ns)]
    )
    cuts = [0] + [h for h in range(1, heads) if (levels[:, h] != levels[:, h - 1]).any()] + [heads]
    ranges = [(a, b) for a, b in zip(cuts, cuts[1:])]
    range_level = np.array([[levels[ss, a] for a, _ in ranges] for ss in range(ns)])
    counts = (range_level[:, :, None] <= np.arange(LEVELS)[None, None, :]).astype(np.float32)
    counted = picked(jnp.asarray(counts), s)
    theirs = picked(
        jnp.asarray(np.stack([[counts[i ^ k].reshape(-1) for k in range(ns)] for i in range(ns)])), s
    )
    lowest = [int(range_level[ss].min()) for ss in range(ns)]

    def by_head(vector):
        lead = vector.shape[:-1]
        per = vector.shape[-1] // HEADS
        cut = vector.reshape(lead + (nd, ns, run * per))
        mine = lax.dynamic_index_in_dim(cut, s, len(lead) + 1, keepdims=False)
        return mine.reshape(lead + (heads * per,))

    def for_groups(matrix):
        per = matrix.shape[1] // HEADS
        cut = matrix.reshape(matrix.shape[0], nd, ns, run * per)
        return jnp.transpose(cut, (2, 0, 1, 3)).reshape(ns, matrix.shape[0], heads * per)

    def from_groups(stack):
        per = stack.shape[2] // heads
        cut = stack.reshape(ns, stack.shape[1], nd, run * per)
        return jnp.transpose(cut, (1, 2, 0, 3)).reshape(stack.shape[1], HEADS * per)

    pad_cols = cols - used - heads
    half = width // 2
    first = half + cols - width
    group_x = for_groups(w_in[:, INNER : 2 * INNER])
    stack = jnp.concatenate(
        [
            group_x[:, :, :half],
            w_in[:, 2 * INNER :].reshape(rows_in, ns, own_bc).transpose(1, 0, 2),
            for_groups(w_dt),
            jnp.zeros((ns, rows_in, pad_cols), BF),
            group_x[:, :, half:],
            for_groups(w_in[:, :INNER]),
        ],
        axis=2,
    )
    own_x = tokens[0].astype(F32)
    scale = lax.rsqrt(jnp.mean(own_x * own_x, axis=-1, keepdims=True) + EPS)
    xn_own = (own_x * scale * norm_gain).astype(BF)
    xn_across = swapped(xn_own, "seq", 2)
    xn_pieces = [xn_own, swapped(xn_own, "seq", 1), xn_across, swapped(xn_across, "seq", 1)]
    arrived = [picked(stack, s)] + [swapped(picked(stack, s ^ k), "seq", k) for k in range(1, ns)]
    mine = filled((ns, rows_in, stack.shape[2]), [(p, None, (s ^ k, None, None)) for k, p in enumerate(arrived)])
    mine_z = mine[:, :, cols:]

    def needed(at, level):
        return min(lowest[at], lowest[at ^ 1]) <= level

    halves = [cotangent[w : w + 2, 0] for w in range(0, LEVELS, 2)]
    singles = [cotangent[w, 0] for w in range(LEVELS)]

    def beside(level, *others):
        block = after(halves[level // 2], *others)
        return swapped(block, "seq", 1, lambda i, j: needed(j, level + 1))

    def across(level, *others):
        block = after(singles[level], *others)
        return swapped(block, "seq", 2, lambda i, j: needed(j, level))

    def far(level, block):
        return swapped(block, "seq", 1, lambda i, j: needed(j, level))

    positions = jnp.arange(length, dtype=jnp.int32)
    ends = jnp.cumsum(lengths[0])[:-1]
    seg = jnp.sum((positions[:, None] >= ends[None, :]).astype(jnp.int32), axis=1)
    seg_before = jnp.concatenate([jnp.full((1,), -1, jnp.int32), seg[SPAN - 1 : length - 1 : SPAN]])
    seg_pad = jnp.concatenate([jnp.full((reach,), -1, jnp.int32), seg])
    masks = [(seg_pad[k : k + length] == seg) for k in range(reach)]
    mask_cols = [m.astype(F32) for m in masks]
    mask_cols += [jnp.pad(m, (0, reach - k))[reach - k :] for k, m in enumerate(mask_cols)]
    mask_cols = jnp.pad(jnp.stack(mask_cols, axis=1), ((0, 0), (0, LANES - 2 * reach)))

    def conv_params(s_part, bc_part):
        return by_head(s_part), bc_part

    weight_s = jnp.concatenate(
        [by_head(conv_w[:, :INNER]), by_head(conv_b[None, :INNER]), jnp.zeros((3, width), F32)]
    )
    weight_r = jnp.pad(
        lax.dynamic_slice_in_dim(conv_w, INNER + s * own_bc, own_bc, 1), ((0, 0), (0, cols - used))
    )
    bias_r = jnp.pad(
        lax.dynamic_slice_in_dim(conv_b, INNER + s * own_bc, own_bc, 0), (0, cols - used)
    )
    bias = by_head(dt_bias)
    rate = -jnp.exp(by_head(a_log))
    skip_own = by_head(skip)
    gain = by_head(gate_gain)

    def over_fsdp(chunk):
        return lax.all_gather(chunk, "fsdp", axis=0, tiled=False)

    def over_dp(held):
        return [held] + [swapped(held, "dp", j) for j in range(1, nd)]

    row_halves = 2 if rows_in % 32 == 0 else 1

    def ready(parts, columns):
        if rows_in % 16 == 0:
            return [piece for pieces in parts for piece in pieces]
        moves = [
            (piece, i, (d ^ j, None, i, h, None, None))
            for h, pieces in enumerate(parts)
            for j, piece in enumerate(pieces)
            for i in range(nf)
        ]
        return [filled((nd, ns, nf, len(parts), rows_in // len(parts), columns), moves).reshape(D, columns)]

    held_a = over_fsdp(mine[:, :, :first])
    held_b = over_fsdp(mine[:, :, first:cols])
    other_out = [swapped(w_out, "dp", j) for j in range(1, nd)]
    held_a, other_out = together(held_a, other_out)
    small_ones = (seg, seg_before, mask_cols, weight_s, weight_r, bias_r, bias, rate, skip_own, gain, theirs)
    held_a, small_ones, halves, singles = together(held_a, small_ones, halves, singles)
    seg, seg_before, mask_cols, weight_s, weight_r, bias_r, bias, rate, skip_own, gain, theirs = small_ones
    near_high, near_low = beside(2, held_a), beside(0, held_a)
    chip3 = across(3, held_a)
    pieces_a = over_dp(held_a)
    held_b, pieces_a, chip3, near_high, xn_pieces = together(
        held_b, pieces_a, chip3, near_high, xn_pieces
    )
    xn = filled((ns, tok, D), [(p, None, (s ^ k, None, None)) for k, p in enumerate(xn_pieces)])
    xn = xn.reshape(length, D)

    far3 = far(3, chip3)
    pieces_b = over_dp(held_b)
    parts_z = mine_z.reshape(ns, row_halves, rows_in // row_halves, width)
    held_z = over_fsdp(after(parts_z[:, 0], held_a))
    late_z = [over_fsdp(after(parts_z[:, h], held_b)) for h in range(1, row_halves)]
    held_out = over_fsdp(after(jnp.stack([w_out] + other_out), held_z))

    xn_turned = xn.T
    here = jnp.stack([s, d]).astype(jnp.int32)
    proj_a, full_a = projections(here, xn, ready([pieces_a], first), nd, rows_in, first)

    proj_r = proj_a[:, half:]
    mixer = jnp.concatenate([jnp.zeros((reach, cols - width), BF), proj_r], axis=0)

    def taken(k):
        rows = mixer[k : k + length].astype(F32)
        return rows * mask_cols[:, k : k + 1] if k < reach else rows

    pre_r = bias_r
    for k in range(CONV):
        pre_r = pre_r + taken(k) * weight_r[k]
    bc_own = jax.nn.silu(pre_r).astype(BF)[:, :own_bc]
    bc_across = swapped(bc_own, "seq", 2)
    bc = [bc_own, swapped(bc_own, "seq", 1), bc_across, swapped(bc_across, "seq", 1)]
    bc, held_z = together(bc, held_z)
    chip2, chip1 = across(2, bc[2]), across(1, bc[2])
    pieces_z = over_dp(held_z)
    pieces_b, xn_turned = together(pieces_b, xn_turned)
    proj_b, full_b = projections(here, xn, ready([pieces_b], half), nd, rows_in, half)
    proj_b, far3, near_low = together(proj_b, far3, near_low)
    bc = reordered_by_xor(bc, s)
    b_in = jnp.concatenate(bc[: ns // 2], axis=1)
    c_out = jnp.concatenate(bc[ns // 2 :], axis=1)

    def padded(rows):
        return jnp.pad(rows, ((0, 0), (0, LANES - rows.shape[1])))

    pre_dt = proj_r[:, own_bc : own_bc + heads].astype(F32) + bias
    steps = jax.nn.softplus(pre_dt)
    tails = [
        p.reshape(blocks, SPAN, p.shape[1])[: blocks - 1, SPAN - HALO :, :half] for p in (proj_a, proj_b)
    ]
    operands = (
        seg_before,
        seg[:, None],
        seg[None, :],
        mask_cols,
        proj_a,
        proj_b,
        jnp.concatenate([jnp.zeros((1, HALO, width), BF), jnp.concatenate(tails, axis=2)]),
        weight_s,
        b_in,
        c_out,
        padded(steps),
        padded(rate[None, :]),
        jnp.repeat(skip_own, HEADDIM)[None, :],
    )
    y, priors = scan_forward(heads, blocks, operands)
    y, chip2, late_z = together(y, chip2, late_z)
    far2, chip0 = far(2, chip2), across(0, y)
    parts = [pieces_z] + [over_dp(piece) for piece in late_z]
    lanes = [(a * HEADDIM, b * HEADDIM) for a, b in ranges]
    starts = [a for a, _ in lanes]
    wide = min(min(b - a for a, b in lanes), TILE)
    proj_z, full_z, q_gain, q_turned, squares = projections(
        here, xn, ready(parts, width), nd, rows_in, width, (y, gain[None], starts, wide)
    )
    squares, chip1 = together(squares[: len(lanes)], chip1)
    far1 = far(1, chip1)
    widths = np.array([[(HEADS >> 3 - w) * HEADDIM] for w in range(LEVELS)], np.float32)
    per_level = jnp.sum(counted[:, :, None] * squares[:, None, :], axis=0)
    ratio, chip0 = together(lax.rsqrt(over_seq(per_level) / widths + EPS), chip0)
    far0 = far(0, chip0)

    plan = [[w for w in range(LEVELS) if range_level[:, j].min() <= w] for j in range(len(lanes))]
    out_rows = width // nd
    range_of = [next(j for j, (a, b) in enumerate(lanes) if a <= i * out_rows < b) for i in range(nd)]
    smem = pl.BlockSpec(memory_space=pltpu.SMEM)
    cot_pieces = [cotangent, near_low, near_high, chip0, chip1, chip2, chip3, far0, far1, far2, far3]
    cot_specs = [pl.BlockSpec((LEVELS, 1, tok, TILE), lambda i: (0, 0, 0, i))]
    cot_specs += [pl.BlockSpec((2, tok, TILE), lambda i: (0, 0, i))] * 2
    cot_specs += [pl.BlockSpec((tok, TILE), lambda i: (0, i))] * (2 * LEVELS)
    where = [[(0, (w, 0)), (1 + w // 2, (w % 2,)), (3 + w, ()), (3 + LEVELS + w, ())] for w in range(LEVELS)]
    upper, *grad_out = call(
        functools.partial(upper_kernel, where, plan, nd, tok, ns),
        grid=(D // TILE,),
        in_specs=[
            smem,
            smem,
            smem,
            pl.BlockSpec((LEVELS, length), lambda i: (0, 0)),
            pl.BlockSpec((width, length), lambda i: (0, 0)),
        ]
        + cot_specs,
        out_specs=[pl.BlockSpec((len(lanes), length, TILE), lambda i: (0, 0, i))]
        + [pl.BlockSpec((out_rows, TILE), lambda i: (0, i))]
        + [pl.BlockSpec((out_rows // 2, TILE), lambda i: (0, i))] * (2 * nd - 2),
        out_shape=[jax.ShapeDtypeStruct((len(lanes), length, D), BF)]
        + [jax.ShapeDtypeStruct((out_rows, D), BF)]
        + [jax.ShapeDtypeStruct((out_rows // 2, D), BF)] * (2 * nd - 2),
        scratch_shapes=[pltpu.VMEM((length, LANES), F32)],
        name="upper",
    )(here, jnp.asarray(range_of, jnp.int32), counted, ratio, q_turned, *cot_pieces)
    out_first, out_second = dp_terms(grad_out[1::2]), dp_terms(grad_out[2::2])

    held_out, upper = together(held_out, upper)
    *shares, inner, full_out = call(
        functools.partial(products_kernel, where, plan, lanes, tok, ns, nd),
        grid=(D // TILE,),
        in_specs=[
            smem,
            smem,
            pl.BlockSpec((length, width), lambda i: (0, 0)),
        ]
        + [pl.BlockSpec((nf, nd, w_out.shape[0], TILE), lambda i: (0, 0, 0, i))]
        + cot_specs,
        out_specs=[pl.BlockSpec((len(lanes), tok, TILE), lambda i: (0, 0, i))] * ns
        + [pl.BlockSpec((LEVELS, length), lambda i: (0, 0))]
        + [pl.BlockSpec((width, TILE), lambda i: (0, i))],
        out_shape=[jax.ShapeDtypeStruct((len(lanes), tok, D), BF)] * ns
        + [jax.ShapeDtypeStruct((LEVELS, length), F32)]
        + [jax.ShapeDtypeStruct((width, D), BF)],
        scratch_shapes=[pltpu.VMEM((LEVELS, length, LANES), F32)],
        name="products",
    )(here, counted, q_gain, held_out, *cot_pieces)
    means, out_first = together(over_seq(inner) / widths, out_first)
    shares[1:3] = [swapped(after(shares[k], means), "seq", k) for k in (1, 2)]
    split = (len(lanes) + 1) // 2
    third = [swapped(after(shares[3][:split], shares[1]), "seq", 3), shares[3][split:]]

    cols_of = pl.BlockSpec((length, wide), lambda i: (0, i))
    scalars = pl.BlockSpec((LEVELS, length), lambda i: (0, 0))
    dy, dz, grad_gate = call(
        functools.partial(gate_kernel, starts, wide),
        grid=(width // wide,),
        in_specs=[
            smem,
            pl.BlockSpec((1, length, D), lambda i: (tile_range(starts, wide, i), 0, 0)),
            pl.BlockSpec((wide, D), lambda i: (i, 0)),
            cols_of,
            cols_of,
            pl.BlockSpec((1, wide), lambda i: (0, i)),
            scalars,
            scalars,
        ],
        out_specs=[cols_of, cols_of, pl.BlockSpec((8, wide), lambda i: (0, i))],
        out_shape=[
            jax.ShapeDtypeStruct((length, width), BF),
            jax.ShapeDtypeStruct((length, width), BF),
            jax.ShapeDtypeStruct((8, width), F32),
        ],
        scratch_shapes=[pltpu.VMEM((len(lanes), length, LANES), F32)],
        name="gate_backward",
    )(counted, upper, full_out, y, proj_z, gain[None], ratio, means)
    grad_gate = grad_gate[0]

    def in_terms(dproj, at, first=0, columns=None):
        columns = columns or dproj.shape[1]
        out = row_terms(xn_turned, dproj, at, nd, ns, nf, first, columns)
        return out.reshape(nf, ns * rows_in, columns)

    z_other = [in_terms(dz, d ^ k) for k in range(1, nd)]
    z_got = dp_terms(z_other)
    dy, out_second, shares[1] = together(after(dy, *z_other), out_second, shares[1])
    chunk = (nf, out_rows // nf, D)
    out_got = [jnp.concatenate([u, v]).reshape(chunk) for u, v in zip(out_first, out_second)]
    out_kept, out_sent = fsdp_half(grad_out[0].reshape(chunk), out_got)
    dy = after(dy, out_sent)
    out_half = swapped(out_sent, "fsdp", 1)

    dproj_s, dbc, ddt, drate, dsum = scan_backward(heads, blocks, operands, y, priors, dy)
    dproj_s, dbc, out_half, shares[2], third = together(dproj_s, dbc, out_half, shares[2], third)
    out_pair = fsdp_rest(out_kept, out_half)

    dbc = dbc.astype(BF)
    slices = reordered_by_xor([dbc[:, j * own_bc : (j + 1) * own_bc] for j in range(ns)], s)
    beside_bc = swapped(jnp.concatenate([slices[1], slices[3]], axis=1), "seq", 1)
    sum_bc = jnp.concatenate([slices[0], slices[2]], axis=1).astype(F32) + beside_bc.astype(F32)
    across_bc = swapped(sum_bc[:, own_bc:].astype(BF), "seq", 2)

    z_own = in_terms(after(dz, dproj_s), d)
    z_own, z_got = together(z_own, z_got)
    z_kept, z_sent = fsdp_half(z_own, z_got)
    z_half = swapped(z_sent, "fsdp", 1)
    late_s = after(dproj_s, z_sent)
    left_other = [in_terms(late_s, d ^ k, 0, half) for k in range(1, nd)]
    left_got = dp_terms(left_other)
    third[1] = swapped(after(third[1], across_bc), "seq", 3)
    dbc_own = sum_bc[:, :own_bc] + across_bc.astype(F32)
    dproj_r, small_sums = small_back(
        own_bc,
        pre_r,
        padded(after(dbc_own, *left_other)),
        proj_r,
        mask_cols,
        weight_r,
        ddt,
        padded(pre_dt),
    )

    dxn = input_grad(dz, dproj_s, dproj_r, full_z, full_a, full_b, ns, tok)
    pair = swapped(jnp.stack([picked(dxn, s ^ 1), picked(dxn, s ^ 3)]), "seq", 1)

    late_s, late_r = together(dproj_s, after(dproj_r, dxn))
    right_other = [
        jnp.concatenate([in_terms(late_s, d ^ k, half, half), in_terms(late_r, d ^ k)], axis=2)
        for k in range(1, nd)
    ]
    right_other, z_half, left_got, out_pair = together(right_other, z_half, left_got, out_pair)
    right_got = dp_terms(right_other)
    z_pair = fsdp_rest(z_kept, z_half)
    own_s = in_terms(after(dproj_s, *right_other), d)
    left_kept, left_sent = fsdp_half(own_s[:, :, :half], left_got)
    left_half = swapped(left_sent, "fsdp", 1)
    own_r = in_terms(after(dproj_r, left_sent), d)
    flat = flattened(
        [
            jnp.concatenate([dsum[:CONV], small_sums[:CONV, :own_bc]], axis=1).reshape(-1),
            dsum[CONV],
            small_sums[CONV, :own_bc],
            grad_gate,
            small_sums[CONV + 1, :heads],
            drate[0, :heads] * rate,
            jnp.sum(dsum[CONV + 1].reshape(heads, HEADDIM), axis=1),
        ]
    )
    near = picked(dxn, s).astype(F32) + pair[0].astype(F32)
    far_sum = (picked(dxn, s ^ 2).astype(F32) + pair[1].astype(F32)).astype(BF)
    dxn_across = swapped(far_sum, "seq", 2)
    right_got, far_sum, left_half = together(right_got, far_sum, left_half)
    left_pair = fsdp_rest(left_kept, left_half)
    own_right = jnp.concatenate([own_s[:, :, half:], own_r], axis=2)
    right_kept, right_sent = fsdp_half(own_right, right_got)
    right_half = swapped(right_sent, "fsdp", 1)

    mixed = call(
        functools.partial(
            mixed_kernel,
            [[j for j in range(len(lanes)) if range_level[:, j].min() <= w] for w in range(LEVELS)],
            ns,
            tok,
        ),
        grid=(D // TILE,),
        in_specs=[
            smem,
            smem,
            pl.BlockSpec((LEVELS, length), lambda i: (0, 0)),
            pl.BlockSpec((tok, TILE), lambda i: (0, i)),
        ]
        + [pl.BlockSpec((len(lanes), tok, TILE), lambda i: (0, 0, i))] * ns,
        out_specs=pl.BlockSpec((LEVELS, tok, TILE), lambda i: (0, 0, i)),
        out_shape=jax.ShapeDtypeStruct((LEVELS, tok, D), BF),
        name="mixed",
    )(here, theirs, ratio, tokens[0], *after(shares[:3] + [jnp.concatenate(third)], right_sent))[:, None]
    right_half, mixed, dxn_across = together(right_half, mixed, dxn_across)
    right_kept = after(right_kept, mixed)
    right_pair = fsdp_rest(right_kept, right_half)
    dxn_own = near + dxn_across.astype(F32)
    grad_norm = jnp.sum(dxn_own * own_x * scale, axis=0)
    scaled = norm_gain * dxn_own
    dx = scale * scaled - own_x * scale**3 * jnp.mean(own_x * scaled, axis=-1, keepdims=True)
    dx = (dx + jnp.sum(after(cotangent, mixed)[:, 0].astype(F32), axis=0)).astype(BF)
    flat = jnp.concatenate([flat, grad_norm.reshape(-1, LANES)])
    flat = butterfly(flat, "dp")

    def whole_sum(pair):
        total = (pair[0].astype(F32) + pair[1].astype(F32)).astype(BF)
        return total.reshape(ns, rows_in, total.shape[1])

    z_pair, left_pair = together(z_pair, left_pair)
    early = jnp.concatenate([whole_sum(z_pair), whole_sum(left_pair)], axis=2)
    early_got = [picked(early, s)] + [swapped(picked(early, s ^ k), "seq", k) for k in range(1, ns)]
    early_got, right_pair, flat = together(early_got, right_pair, flat)
    flat = butterfly(flat, "fsdp")
    late = whole_sum(right_pair)
    late_got = [picked(late, s)] + [swapped(picked(late, s ^ k), "seq", k) for k in range(1, ns)]
    early = jnp.stack(reordered_by_xor(early_got, s))
    late = jnp.stack(reordered_by_xor(late_got, s))
    got_z = early[:, :, :width]
    got_x = jnp.concatenate([early[:, :, width:], late], axis=2)
    sum_out = out_pair[0].astype(F32) + out_pair[1].astype(F32)


    sum_in = jnp.concatenate(
        [
            from_groups(got_z),
            from_groups(got_x[:, :, :width]),
            jnp.transpose(got_x[:, :, width:used], (1, 0, 2)).reshape(rows_in, 2 * STATE),
        ],
        axis=1,
    ).astype(F32)
    sum_dt = from_groups(got_x[:, :, used : used + heads]).astype(F32)

    sizes = [CONV * used, used, width, heads, heads, heads]
    filling = -sum(sizes) % 1024
    sizes += [filling, D]
    every = seq_gather(flat, s).reshape(ns, -1)
    starts = np.cumsum([0] + sizes)
    pieces = [every[:, a : a + n] for a, n in zip(starts, sizes)]

    def heads_back(rows):
        lead = rows.shape[1:-1]
        cut = rows.reshape((ns,) + lead + (nd, rows.shape[-1] // nd))
        order = tuple(range(1, 1 + len(lead))) + (1 + len(lead), 0, 2 + len(lead))
        return jnp.transpose(cut, order).reshape(lead + (-1,))

    conv_rows = pieces[0].reshape(ns, CONV, used)
    conv_all = jnp.concatenate(
        [
            heads_back(conv_rows[:, :, :width]),
            jnp.transpose(conv_rows[:, :, width:], (1, 0, 2)).reshape(CONV, 2 * STATE),
        ],
        axis=1,
    )
    bias_all = jnp.concatenate([heads_back(pieces[1][:, :width]), pieces[1][:, width:].reshape(-1)])
    return (
        mixed,
        dx[None],
        jnp.sum(pieces[7], axis=0),
        sum_in,
        sum_dt,
        conv_all,
        bias_all,
        heads_back(pieces[3]),
        heads_back(pieces[4]),
        heads_back(pieces[5]),
        heads_back(pieces[2]),
        sum_out,
    )


def solution(mesh):
    rows = P(("dp", "seq", "fsdp"), None)
    held = P(("dp", "fsdp"), "seq", None)
    levels = P(None, ("dp", "fsdp"), "seq", None)
    placed = (held, P(("dp", "fsdp"), None), P(), rows, rows, P(), P(), P(), P(), P(), P(), rows, levels)
    return jax.shard_map(
        shards,
        mesh=mesh,
        in_specs=placed,
        out_specs=(levels, held, P(), rows, rows, P(), P(), P(), P(), P(), P(), rows),
        check_vma=False,
    )
```

profile of v0, /device:TPU:0, one launch (start us, length us, event | category | flops | bytes accessed | tf_op | source)
XLA Modules:
  0.0 534.3 jit_solution(14663420246910214700)
XLA Ops:
  18.0 5.3 collective-permute-done.1.refs_2_
  23.3 5.4 %collective-permute-done.2.refs_3_ = bf16[64,2176]{1,0:T(8,128)(2,1)S(1)} collective-permute-done((bf16[64,2176]{1,0:T(8,128)(2,1)S(1)}, bf16[64,2176]{1,0:T(8,128)(2,1)S(1)}, u32[]{:S(2)}, u32[]{:S(2)}) %collective-permute-start.2) | collective-permute-done | bytes 278560 | tf_op jit(solution)/shard_map/ppermute | solution.py:46
  37.0 5.1 slice_bitcast_fusion
  44.3 20.6 %all-gather.13.cloned.1.call-done = bf16[16,64,640]{2,1,0:T(8,128)(2,1)} async-done(((bf16[4,64,640]{2,1,0:T(8,128)(2,1)}), bf16[16,64,640]{2,1,0:T(8,128)(2,1)}) %all-gather.13.cloned.1.call-update) | async-done | bytes 1310736 | tf_op jit(solution)/shard_map/all_gather | solution.py:931
  73.3 20.2 %all-gather.11.cloned.1.call-done = bf16[16,64,512]{2,1,0:T(8,128)(2,1)} async-done(((bf16[4,64,512]{2,1,0:T(8,128)(2,1)}), bf16[16,64,512]{2,1,0:T(8,128)(2,1)}) %all-gather.11.cloned.1.call-update) | async-done | bytes 1048592 | tf_op jit(solution)/shard_map/all_gather | solution.py:931
  93.6 3.8 collective-permute-done.4.refs_1_
  100.2 22.3 %all-gather.15.cloned.1.call-done = bf16[16,32,1024]{2,1,0:T(8,128)(2,1)} async-done(((bf16[4,32,1024]{2,1,0:T(8,128)(2,1)}), bf16[16,32,1024]{2,1,0:T(8,128)(2,1)}) %all-gather.15.cloned.1.call-update) | async-done | bytes 1048592 | tf_op jit(solution)/shard_map/all_gather | solution.py:931
  125.9 5.1 filled.3
  131.0 10.2 %project.2 = (bf16[1024,640]{1,0:T(8,128)(2,1)S(1)}, bf16[2048,640]{1,0:T(8,128)(2,1)}) custom-call(s32[2]{0:T(128)S(1)} %pad_add_fusion.2.here_ref, bf16[1024,2048]{1,0:T(8,128)(2,1)} %bitcast.250, bf16[4,4,64,640]{3,2,1,0:T(8,128)(2,1)S(1)} %bitcast.239, bf16[4,4,64,640]{3,2,1,0:T(8,128)(2,1)S(1)} %copy-done.31), custom_call_target="tpu_custom_call" | custom-call | flops 1 | bytes 1 | tf_op jit(solution)/shard_map/project/pallas_call | solution.py:313
  144.6 7.1 %collective-permute-done.14 = bf16[1024,64]{1,0:T(8,128)(2,1)S(1)} collective-permute-done((bf16[1024,64]{1,0:T(8,128)(2,1)S(1)}, bf16[1024,64]{1,0:T(8,128)(2,1)S(1)}, u32[]{:S(2)}, u32[]{:S(2)}) %collective-permute-start.14) | collective-permute-done | bytes 131104 | tf_op jit(solution)/shard_map/ppermute | solution.py:46
  156.3 6.5 %copy.227 = bf16[1024,2048]{0,1:T(8,128)(2,1)} copy(bf16[1024,2048]{1,0:T(8,128)(2,1)} %bitcast.251) | data formatting | bytes 8388608 | tf_op jit(solution)/shard_map/reshape | solution.py:963
  165.8 12.2 %collective-permute-done.10.refs_1_ = bf16[4,4,64,512]{3,2,1,0:T(8,128)(2,1)} collective-permute-done((bf16[4,4,64,512]{3,2,1,0:T(8,128)(2,1)}, bf16[4,4,64,512]{3,2,1,0:T(8,128)(2,1)}, u32[]{:S(2)}, u32[]{:S(2)}) %collective-permute-start.10) | collective-permute-done | bytes 1048608 | tf_op jit(solution)/shard_map/ppermute | solution.py:46
  178.0 5.5 %project.3 = (bf16[1024,512]{1,0:T(8,128)(2,1)S(1)}, bf16[2048,512]{1,0:T(8,128)(2,1)S(1)}) custom-call(s32[2]{0:T(128)S(1)} %pad_add_fusion.2.here_ref, bf16[1024,2048]{1,0:T(8,128)(2,1)} %bitcast.252, bf16[4,4,64,512]{3,2,1,0:T(8,128)(2,1)} %bitcast.19.refs_0_, bf16[4,4,64,512]{3,2,1,0:T(8,128)(2,1)} %collective-permute-done.10.refs_1_), custom_call_target="tpu_custom_call" | custom-call | flops 1 | bytes 1 | tf_op jit(solution)/shard_map/project/pallas_call | solution.py:313
  185.0 16.7 %scan_forward.1 = (f32[1024,1024]{1,0:T(8,128)}, f32[8,128,1024]{2,1,0:T(8,128)}) custom-call(s32[8]{0:T(128)S(1)} %pad_add_fusion.1.segp_ref, s32[1024,1]{1,0:T(8,128)S(1)} %copy-done.12, s32[1,1024]{1,0:T(1,128)S(1)} %bitcast.245, f32[1024,128]{1,0:T(8,128)S(1)} %pad.53.mask_ref, bf16[1024,640]{1,0:T(8,128)(2,1)S(1)} %get-tuple-element.172.in_a_ref, ...), custom_call_target="tpu_custom_call" | custom-call | flops 1 | bytes 1 | tf_op jit(solution)/shard_map/scan_forward/pallas_call | solution.py:578
  206.6 19.8 %collective-permute-done.18.refs_3_ = bf16[4,4,32,1024]{3,2,1,0:T(8,128)(2,1)S(1)} collective-permute-done((bf16[4,4,32,1024]{3,2,1,0:T(8,128)(2,1)}, bf16[4,4,32,1024]{3,2,1,0:T(8,128)(2,1)S(1)}, u32[]{:S(2)}, u32[]{:S(2)}) %collective-permute-start.18) | collective-permute-done | bytes 1048608 | tf_op jit(solution)/shard_map/ppermute | solution.py:46
  227.6 12.2 %gated.1 = (bf16[1024,1024]{1,0:T(8,128)(2,1)}, bf16[2048,1024]{1,0:T(8,128)(2,1)}, bf16[1024,1024]{1,0:T(8,128)(2,1)}, bf16[1024,1024]{1,0:T(8,128)(2,1)}, f32[8,1024]{1,0:T(8,128)S(1)}) custom-call(s32[2]{0:T(128)S(1)} %pad_add_fusion.2.here_ref, bf16[1024,2048]{1,0:T(8,128)(2,1)} %bitcast.253, f32[1024,1024]{1,0:T(8,128)} %get-tuple-element.195.y_ref, ...), custom_call_target="tpu_custom_call" | custom-call | flops 1 | bytes 1 | tf_op jit(solution)/shard_map/gated/pallas_call | solution.py:313
  244.3 8.2 %collective-permute-done.21 = f32[32,128]{1,0:T(8,128)S(1)} collective-permute-done((f32[32,128]{1,0:T(8,128)S(1)}, f32[32,128]{1,0:T(8,128)S(1)}, u32[]{:S(2)}, u32[]{:S(2)}) %collective-permute-start.21) | collective-permute-done | bytes 16416 | tf_op jit(solution)/shard_map/ppermute | solution.py:46
  258.4 17.2 %upper.1 = (bf16[2,1024,2048]{2,1,0:T(8,128)(2,1)}, bf16[512,2048]{1,0:T(8,128)(2,1)}, bf16[256,2048]{1,0:T(8,128)(2,1)}, bf16[256,2048]{1,0:T(8,128)(2,1)S(1)}) custom-call(s32[2]{0:T(128)S(1)} %pad_add_fusion.2.here_ref, s32[2]{0:T(128)S(1)} %call_exported.0.range_ref, f32[2,4]{1,0:T(2,128)S(1)} %fusion.42.count_ref, f32[4,1024]{1,0:T(4,128)S(1)} %fusion.30.ratio_ref, ...), custom_call_target="tpu_custom_call" | custom-call | flops 1 | bytes 1 | tf_op jit(solution)/shard_map/upper/pallas_call | solution.py:1048
  278.4 17.4 %products.1 = (bf16[2,256,2048]{2,1,0:T(8,128)(2,1)}, bf16[2,256,2048]{2,1,0:T(8,128)(2,1)}, bf16[2,256,2048]{2,1,0:T(8,128)(2,1)}, bf16[2,256,2048]{2,1,0:T(8,1...) custom-call(s32[2]{0:T(128)S(1)} %pad_add_fusion.2.here_ref, f32[2,4]{1,0:T(2,128)S(1)} %fusion.42.count_ref, ...), custom_call_target="tpu_custom_call" | custom-call | flops 1 | bytes 1 | tf_op jit(solution)/shard_map/products/pallas_call | solution.py:1071
  303.0 12.3 %gate_backward.1 = (bf16[1024,1024]{1,0:T(8,128)(2,1)S(1)}, bf16[1024,1024]{1,0:T(8,128)(2,1)S(1)}, f32[8,1024]{1,0:T(8,128)S(1)}) custom-call(f32[2,4]{1,0:T(2,128)S(1)} %fusion.42.count_ref, bf16[2,1024,2048]{2,1,0:T(8,128)(2,1)} %get-tuple-element.217.upper_ref, bf16[1024,2048]{1,0:T(8,128)(2,1)} %get-tuple-element.220.w_ref, ...), custom_call_target="tpu_custom_call" | custom-call | flops 1 | bytes 1 | tf_op jit(solution)/shard_map/gate_backward/pallas_call | solution.py:1097
  316.6 6.4 %row_terms.7 = bf16[4,4,64,1024]{3,2,1,0:T(8,128)(2,1)} custom-call(s32[1]{0:T(128)} %bitcast.61.at_ref, bf16[2048,1024]{1,0:T(8,128)(2,1)} %bitcast.225, bf16[1024,1024]{1,0:T(8,128)(2,1)S(1)} %get-tuple-element.244.right_ref.dz_ref), custom_call_target="tpu_custom_call" | custom-call | flops 1 | bytes 1 | tf_op jit(solution)/shard_map/row_terms/pallas_call | solution.py:144
  335.5 34.8 %scan_backward.1 = (bf16[1024,1024]{1,0:T(8,128)(2,1)}, f32[1024,256]{1,0:T(8,128)S(1)}, f32[1024,128]{1,0:T(8,128)S(1)}, f32[1,128]{1,0:T(1,128)S(1)}, f32[8,1024]{1,0:T(8,128)S(1)}) custom-call(s32[8]{0:T(128)S(1)} %pad_add_fusion.1.segp_ref, s32[1024,1]{1,0:T(8,128)S(1)} %copy-done.13, s32[1,1024]{1,0:T(1,128)S(1)} %bitcast.246, ...), custom_call_target="tpu_custom_call" | custom-call | flops 1 | bytes 1 | tf_op jit(solution)/shard_map/scan_backward/pallas_call | solution.py:601
  374.1 4.9 row_terms.8
  390.4 3.9 row_terms.9
  398.0 13.6 %input_grad.1 = bf16[4,256,2048]{2,1,0:T(8,128)(2,1)} custom-call(bf16[1024,1024]{1,0:T(8,128)(2,1)S(1)} %copy-done.8, bf16[1024,1024]{1,0:T(8,128)(2,1)S(1)} %copy-done.2, bf16[1024,128]{1,0:T(8,128)(2,1)S(1)} %get-tuple-element.261.dr_ref.right_ref, bf16[2048,1024]{1,0:T(8,128)(2,1)} %get-tuple-element.251.wz_ref, ...), custom_call_target="tpu_custom_call" | custom-call | flops 1 | bytes 1 | tf_op jit(solution)/shard_map/input_grad/pallas_call | solution.py:218
  411.7 3.6 row_terms.10
  424.9 4.9 row_terms.12
  458.5 9.7 %mixed.1 = bf16[4,256,2048]{2,1,0:T(8,128)(2,1)} custom-call(s32[2]{0:T(128)S(1)} %pad_add_fusion.2.here_ref, f32[4,8]{1,0:T(4,128)S(1)} %fusion.37.count_ref, f32[4,1024]{1,0:T(4,128)S(1)} %fusion.30.ratio_ref, bf16[256,2048]{1,0:T(8,128)(2,1)S(1)} %bitcast.232, bf16[2,256,2048]{2,1,0:T(8,128)(2,1)S(1)} %copy-done.28, ...), custom_call_target="tpu_custom_call" | custom-call | flops 1 | bytes 1 | tf_op jit(solution)/shard_map/mixed/pallas_call | solution.py:1200
  469.4 4.1 collective-permute-done.49
  489.9 3.8 fusion.11
  493.7 4.3 collective-permute-done.52
  498.0 5.7 %collective-permute-done.53 = bf16[1,256,640]{2,1,0:T(8,128)(2,1)S(1)} collective-permute-done((bf16[1,256,640]{2,1,0:T(8,128)(2,1)S(1)}, bf16[1,256,640]{2,1,0:T(8,128)(2,1)S(1)}, u32[]{:S(2)}, u32[]{:S(2)}) %collective-permute-start.53) | collective-permute-done | bytes 327712 | tf_op jit(solution)/shard_map/ppermute | solution.py:46
  (495 shorter events, 185.6 us)
Async XLA Ops:
  7.2 57.7 %all-gather.13.cloned.1.call-start = ((), (), s32[]{:S(2)}) async-start(), calls=%async_computation.1 | async-start | bytes 1638400 | tf_op jit(solution)/shard_map/all_gather | solution.py:931
  15.9 28.5 %collective-permute-start.3 = (bf16[128,2048]{1,0:T(8,128)(2,1)}, bf16[128,2048]{1,0:T(8,128)(2,1)}, u32[]{:S(2)}, u32[]{:S(2)}) collective-permute-start(bf16[128,2048]{1,0:T(8,128)(2,1)} %param.28), channel_id=1, source_target_pairs={{0,16},{16,0},{1,17},{17,1},{2,18},{18,2},{3,19},{19,3},{4,20},{20... | collective-permute-start | bytes 1572872 | tf_op jit(solution)/shard_map/ppermute | solution.py:46
  30.4 63.0 %all-gather.11.cloned.1.call-start = ((), (), s32[]{:S(2)}) async-start(), calls=%async_computation | async-start | bytes 1310720 | tf_op jit(solution)/shard_map/all_gather | solution.py:931
  31.8 35.9 %collective-permute-start.8 = (bf16[256,2048]{1,0:T(8,128)(2,1)}, bf16[256,2048]{1,0:T(8,128)(2,1)}, u32[]{:S(2)}, u32[]{:S(2)}) collective-permute-start(bf16[256,2048]{1,0:T(8,128)(2,1)} %fusion.2.refs_0_), channel_id=1, source_target_pairs={{0,8},{4,12},{8,0},{12,4},{1,9},{5,13},{9,1},{13,5},{2,10},{6,14},... | collective-permute-start | bytes 3145736 | tf_op jit(solution)/shard_map/ppermute | solution.py:46
  36.9 85.5 %all-gather.15.cloned.1.call-start = ((), (), s32[]{:S(2)}) async-start(), calls=%async_computation.2 | async-start | bytes 1310720 | tf_op jit(solution)/shard_map/all_gather | solution.py:931
  64.9 32.5 %collective-permute-start.6 = (bf16[2,256,2048]{2,1,0:T(8,128)(2,1)}, bf16[2,256,2048]{2,1,0:T(8,128)(2,1)}, u32[]{:S(2)}, u32[]{:S(2)}) collective-permute-start(bf16[2,256,2048]{2,1,0:T(8,128)(2,1)} %get-tuple-element.160), channel_id=1, source_target_pairs={{0,4},{4,0},{8,12},{12,8},{1,5},{5,1},{9,13},{13,9},{2,6},{6,2},{1... | collective-permute-start | bytes 6291464 | tf_op jit(solution)/shard_map/ppermute | solution.py:46
  65.9 135.9 %all-gather.17.cloned.1.call-start = ((), (), s32[]{:S(2)}) async-start(), calls=%async_computation.3 | async-start | bytes 1310720 | tf_op jit(solution)/shard_map/all_gather | solution.py:931
  65.9 31.5 %collective-permute-start.4 = (bf16[4,4,64,640]{3,2,1,0:T(8,128)(2,1)}, bf16[4,4,64,640]{3,2,1,0:T(8,128)(2,1)S(1)}, u32[]{:S(2)}, u32[]{:S(2)}) collective-permute-start(bf16[4,4,64,640]{3,2,1,0:T(8,128)(2,1)} %bitcast.238), channel_id=1, source_target_pairs={{0,16},{16,0},{1,17},{17,1},{2,18},{18,2},{3,19},{19,3},{4,20},{20... | collective-permute-start | bytes 3932168 | tf_op jit(solution)/shard_map/ppermute | solution.py:46
  67.7 25.8 %collective-permute-start.9 = (bf16[256,2048]{1,0:T(8,128)(2,1)}, bf16[256,2048]{1,0:T(8,128)(2,1)}, u32[]{:S(2)}, u32[]{:S(2)}) collective-permute-start(bf16[256,2048]{1,0:T(8,128)(2,1)} %collective-permute-done.8.refs_2_), channel_id=1, source_target_pairs={{0,4},{4,0},{8,12},{12,8},{1,5},{5,1},{9,13},{13,9},{2,6},{6,2},{1... | collective-permute-start | bytes 3145736 | tf_op jit(solution)/shard_map/ppermute | solution.py:46
  68.0 25.6 %collective-permute-start.5 = (bf16[256,2048]{1,0:T(8,128)(2,1)}, bf16[256,2048]{1,0:T(8,128)(2,1)}, u32[]{:S(2)}, u32[]{:S(2)}) collective-permute-start(bf16[256,2048]{1,0:T(8,128)(2,1)} %get-tuple-element.158), channel_id=1, source_target_pairs={{0,8},{4,12},{8,0},{12,4},{1,9},{5,13},{9,1},{13,5},{2,10},{6,14},... | collective-permute-start | bytes 3145736 | tf_op jit(solution)/shard_map/ppermute | solution.py:46
  97.4 179.8 %all-gather.19.cloned.1.call-start = ((), (), s32[]{:S(2)}) async-start(), calls=%async_computation.4 | async-start | bytes 5242880 | tf_op jit(solution)/shard_map/all_gather | solution.py:931
  122.5 62.4 %collective-permute-start.12 = (bf16[2,256,2048]{2,1,0:T(8,128)(2,1)}, bf16[2,256,2048]{2,1,0:T(8,128)(2,1)}, u32[]{:S(2)}, u32[]{:S(2)}) collective-permute-start(bf16[2,256,2048]{2,1,0:T(8,128)(2,1)} %get-tuple-element.178), channel_id=1, source_target_pairs={{0,4},{4,0},{1,5},{5,1},{2,6},{6,2},{3,7},{7,3},{16,20},{20,16},{1... | collective-permute-start | bytes 6291464 | tf_op jit(solution)/shard_map/ppermute | solution.py:46
  151.7 26.3 %collective-permute-start.10 = (bf16[4,4,64,512]{3,2,1,0:T(8,128)(2,1)}, bf16[4,4,64,512]{3,2,1,0:T(8,128)(2,1)}, u32[]{:S(2)}, u32[]{:S(2)}) collective-permute-start(bf16[4,4,64,512]{3,2,1,0:T(8,128)(2,1)} %bitcast.19.refs_0_), channel_id=1, source_target_pairs={{0,16},{16,0},{1,17},{17,1},{2,18},{18,2},{3,19},{19,3},{4,20},{20... | collective-permute-start | bytes 3145736 | tf_op jit(solution)/shard_map/ppermute | solution.py:46
  153.2 31.6 %collective-permute-start.11 = (bf16[256,2048]{1,0:T(8,128)(2,1)}, bf16[256,2048]{1,0:T(8,128)(2,1)}, u32[]{:S(2)}, u32[]{:S(2)}) collective-permute-start(bf16[256,2048]{1,0:T(8,128)(2,1)} %collective-permute-done.5.refs_6_.refs_7_), channel_id=1, source_target_pairs={{0,4},{4,0},{8,12},{12,8},{1,5},{5,1},{9,13},{13,9},{2,6},{6,2},{1... | collective-permute-start | bytes 3145736 | tf_op jit(solution)/shard_map/ppermute | solution.py:46
  154.3 47.4 %collective-permute-start.16 = (bf16[256,2048]{1,0:T(8,128)(2,1)}, bf16[256,2048]{1,0:T(8,128)(2,1)}, u32[]{:S(2)}, u32[]{:S(2)}) collective-permute-start(bf16[256,2048]{1,0:T(8,128)(2,1)} %get-tuple-element.193), channel_id=1, source_target_pairs={{0,8},{4,12},{8,0},{12,4},{1,9},{5,13},{9,1},{13,5},{2,10},{6,14},... | collective-permute-start | bytes 3145736 | tf_op jit(solution)/shard_map/ppermute | solution.py:46
  164.0 42.5 %collective-permute-start.17 = (bf16[4,4,32,1024]{3,2,1,0:T(8,128)(2,1)}, bf16[4,4,32,1024]{3,2,1,0:T(8,128)(2,1)}, u32[]{:S(2)}, u32[]{:S(2)}) collective-permute-start(bf16[4,4,32,1024]{3,2,1,0:T(8,128)(2,1)} %bitcast.52.refs_0_), channel_id=1, source_target_pairs={{0,16},{16,0},{1,17},{17,1},{2,18},{18,2},{3,19},{19,3},{4,20},{20... | collective-permute-start | bytes 3145736 | tf_op jit(solution)/shard_map/ppermute | solution.py:46
  203.3 36.5 %collective-permute-start.19 = (bf16[256,2048]{1,0:T(8,128)(2,1)}, bf16[256,2048]{1,0:T(8,128)(2,1)S(1)}, u32[]{:S(2)}, u32[]{:S(2)}) collective-permute-start(bf16[256,2048]{1,0:T(8,128)(2,1)} %get-tuple-element.204), channel_id=1, source_target_pairs={{8,0},{12,4},{9,1},{13,5},{10,2},{14,6},{11,3},{15,7},{24,16},{28,... | collective-permute-start | bytes 3145736 | tf_op jit(solution)/shard_map/ppermute | solution.py:46
  204.6 48.1 %collective-permute-start.23 = (bf16[256,2048]{1,0:T(8,128)(2,1)}, bf16[256,2048]{1,0:T(8,128)(2,1)}, u32[]{:S(2)}, u32[]{:S(2)}) collective-permute-start(bf16[256,2048]{1,0:T(8,128)(2,1)} %get-tuple-element.207), channel_id=1, source_target_pairs={{8,0},{12,4},{9,1},{13,5},{10,2},{14,6},{11,3},{15,7},{24,16},{28,... | collective-permute-start | bytes 3145736 | tf_op jit(solution)/shard_map/ppermute | solution.py:46
  276.7 25.5 %collective-permute-start.30 = (bf16[256,2048]{1,0:T(8,128)(2,1)}, bf16[256,2048]{1,0:T(8,128)(2,1)}, u32[]{:S(2)}, u32[]{:S(2)}) collective-permute-start(bf16[256,2048]{1,0:T(8,128)(2,1)} %get-tuple-element.223), channel_id=1, source_target_pairs={{0,16},{16,0},{1,17},{17,1},{2,18},{18,2},{3,19},{19,3},{4,20},{20... | collective-permute-start | bytes 3145736 | tf_op jit(solution)/shard_map/ppermute | solution.py:46
  302.2 26.3 %collective-permute-start.31 = (bf16[256,2048]{1,0:T(8,128)(2,1)}, bf16[256,2048]{1,0:T(8,128)(2,1)}, u32[]{:S(2)}, u32[]{:S(2)}) collective-permute-start(bf16[256,2048]{1,0:T(8,128)(2,1)} %copy-done.38), channel_id=1, source_target_pairs={{0,16},{16,0},{1,17},{17,1},{2,18},{18,2},{3,19},{19,3},{4,20},{20... | collective-permute-start | bytes 3145736 | tf_op jit(solution)/shard_map/ppermute | solution.py:46
  302.7 68.6 %collective-permute-start.34 = (bf16[2,256,2048]{2,1,0:T(8,128)(2,1)}, bf16[2,256,2048]{2,1,0:T(8,128)(2,1)}, u32[]{:S(2)}, u32[]{:S(2)}) collective-permute-start(bf16[2,256,2048]{2,1,0:T(8,128)(2,1)} %get-tuple-element.239), channel_id=1, source_target_pairs={{0,8},{4,12},{8,0},{12,4},{1,9},{5,13},{9,1},{13,5},{2,10},{6,14},... | collective-permute-start | bytes 6291464 | tf_op jit(solution)/shard_map/ppermute | solution.py:46
  323.0 56.1 %collective-permute-start.38 = (bf16[4,256,1024]{2,1,0:T(8,128)(2,1)}, bf16[4,256,1024]{2,1,0:T(8,128)(2,1)}, u32[]{:S(2)}, u32[]{:S(2)}) collective-permute-start(bf16[4,256,1024]{2,1,0:T(8,128)(2,1)} %bitcast.62), channel_id=1, source_target_pairs={{0,16},{16,0},{1,17},{17,1},{2,18},{18,2},{3,19},{19,3},{4,20},{20... | collective-permute-start | bytes 6291464 | tf_op jit(solution)/shard_map/ppermute | solution.py:46
  325.8 46.8 %collective-permute-start.35 = (bf16[1,256,2048]{2,1,0:T(8,128)(2,1)}, bf16[1,256,2048]{2,1,0:T(8,128)(2,1)}, u32[]{:S(2)}, u32[]{:S(2)}) collective-permute-start(bf16[1,256,2048]{2,1,0:T(8,128)(2,1)} %get-tuple-element.241), channel_id=1, source_target_pairs={{0,12},{4,8},{8,4},{12,0},{1,13},{5,9},{9,5},{13,1},{2,14},{6,10},... | collective-permute-start | bytes 3145736 | tf_op jit(solution)/shard_map/ppermute | solution.py:46
  333.1 39.4 %collective-permute-start.33 = (bf16[2,128,2048]{2,1,0:T(8,128)(2,1)}, bf16[2,128,2048]{2,1,0:T(8,128)(2,1)}, u32[]{:S(2)}, u32[]{:S(2)}) collective-permute-start(bf16[2,128,2048]{2,1,0:T(8,128)(2,1)} %pad_maximum_fusion.12), channel_id=1, source_target_pairs={{0,1},{1,0},{2,3},{3,2},{4,5},{5,4},{6,7},{7,6},{8,9},{9,8},{10,11... | collective-permute-start | bytes 3145736 | tf_op jit(solution)/shard_map/ppermute | solution.py:46
  383.7 40.1 %collective-permute-start.39 = (bf16[2,256,1024]{2,1,0:T(8,128)(2,1)}, bf16[2,256,1024]{2,1,0:T(8,128)(2,1)}, u32[]{:S(2)}, u32[]{:S(2)}) collective-permute-start(bf16[2,256,1024]{2,1,0:T(8,128)(2,1)} %pad_maximum_fusion.13), channel_id=1, source_target_pairs={{0,1},{1,0},{2,3},{3,2},{4,5},{5,4},{6,7},{7,6},{8,9},{9,8},{10,11... | collective-permute-start | bytes 3145736 | tf_op jit(solution)/shard_map/ppermute | solution.py:46
  389.3 34.5 %collective-permute-start.41 = (bf16[1,128,2048]{2,1,0:T(8,128)(2,1)}, bf16[1,128,2048]{2,1,0:T(8,128)(2,1)}, u32[]{:S(2)}, u32[]{:S(2)}) collective-permute-start(bf16[1,128,2048]{2,1,0:T(8,128)(2,1)} %get-tuple-element.421), channel_id=1, source_target_pairs={{0,2},{1,3},{2,0},{3,1},{4,6},{5,7},{6,4},{7,5},{8,10},{9,11},{10,... | collective-permute-start | bytes 1572872 | tf_op jit(solution)/shard_map/ppermute | solution.py:46
  394.4 29.4 %collective-permute-start.40 = (bf16[4,256,512]{2,1,0:T(8,128)(2,1)}, bf16[4,256,512]{2,1,0:T(8,128)(2,1)}, u32[]{:S(2)}, u32[]{:S(2)}) collective-permute-start(bf16[4,256,512]{2,1,0:T(8,128)(2,1)} %bitcast.66), channel_id=1, source_target_pairs={{0,16},{16,0},{1,17},{17,1},{2,18},{18,2},{3,19},{19,3},{4,20},{20... | collective-permute-start | bytes 3145736 | tf_op jit(solution)/shard_map/ppermute | solution.py:46
  417.7 25.6 %collective-permute-start.46 = (bf16[1,256,2048]{2,1,0:T(8,128)(2,1)}, bf16[1,256,2048]{2,1,0:T(8,128)(2,1)}, u32[]{:S(2)}, u32[]{:S(2)}) collective-permute-start(bf16[1,256,2048]{2,1,0:T(8,128)(2,1)} %get-tuple-element.269), channel_id=1, source_target_pairs={{0,12},{4,8},{8,4},{12,0},{1,13},{5,9},{9,5},{13,1},{2,14},{6,10},... | collective-permute-start | bytes 3145736 | tf_op jit(solution)/shard_map/ppermute | solution.py:46
  423.8 30.8 %collective-permute-start.42 = (bf16[4,256,640]{2,1,0:T(8,128)(2,1)S(1)}, bf16[4,256,640]{2,1,0:T(8,128)(2,1)S(1)}, u32[]{:S(2)}, u32[]{:S(2)}) collective-permute-start(bf16[4,256,640]{2,1,0:T(8,128)(2,1)S(1)} %pad_maximum_fusion.4), channel_id=1, source_target_pairs={{0,16},{16,0},{1,17},{17,1},{2,18},{18,2},{3,19},{19,3},{4,20},{20... | collective-permute-start | bytes 3932168 | tf_op jit(solution)/shard_map/ppermute | solution.py:46
  436.6 32.8 %collective-permute-start.48 = (bf16[1,256,1024]{2,1,0:T(8,128)(2,1)S(1)}, bf16[1,256,1024]{2,1,0:T(8,128)(2,1)S(1)}, u32[]{:S(2)}, u32[]{:S(2)}) collective-permute-start(bf16[1,256,1024]{2,1,0:T(8,128)(2,1)S(1)} %get-tuple-element.419), channel_id=1, source_target_pairs={{0,2},{1,3},{2,0},{3,1},{4,6},{5,7},{6,4},{7,5},{8,10},{9,11},{10,... | collective-permute-start | bytes 1572872 | tf_op jit(solution)/shard_map/ppermute | solution.py:46
  449.3 33.7 %collective-permute-start.47 = (bf16[256,2048]{1,0:T(8,128)(2,1)}, bf16[256,2048]{1,0:T(8,128)(2,1)}, u32[]{:S(2)}, u32[]{:S(2)}) collective-permute-start(bf16[256,2048]{1,0:T(8,128)(2,1)} %fusion.10), channel_id=1, source_target_pairs={{0,8},{4,12},{8,0},{12,4},{1,9},{5,13},{9,1},{13,5},{2,10},{6,14},... | collective-permute-start | bytes 3145736 | tf_op jit(solution)/shard_map/ppermute | solution.py:46
  457.9 25.1 %collective-permute-start.45 = (bf16[2,256,640]{2,1,0:T(8,128)(2,1)}, bf16[2,256,640]{2,1,0:T(8,128)(2,1)}, u32[]{:S(2)}, u32[]{:S(2)}) collective-permute-start(bf16[2,256,640]{2,1,0:T(8,128)(2,1)} %pad_maximum_fusion.14), channel_id=1, source_target_pairs={{0,1},{1,0},{2,3},{3,2},{4,5},{5,4},{6,7},{7,6},{8,9},{9,8},{10,11... | collective-permute-start | bytes 1966088 | tf_op jit(solution)/shard_map/ppermute | solution.py:46
  (117 other events, 1109.8 us)
Sparse Core Ops, SparseCore 0:
  30.5 34.3 all-gather.12
  66.5 26.9 all-gather.10
  95.0 27.4 all-gather.14
  123.9 27.4 all-gather.16
  152.8 80.2 all-gather.18
where the time goes:
time: 541 us; the launch traced here: 534 us
  Pallas kernels  182 us (34%)
  waiting for transfers between devices  164 us (30%)
  starting transfers between devices  59 us (11%)
  local copies, waits for them, and re-layouts  58.8 us (11%)
  other arithmetic  55.3 us (10%)
  between operations  15.9 us (3%)
    ppermute x63, waiting for transfers between devices, swapped(): return lax.ppermute(value, axis, pairs)  100 us
    all_gather x5, waiting for transfers between devices, over_fsdp(): return lax.all_gather(chunk, 'fsdp', axis=0, tiled=False)  63.1 us
    ppermute x63, starting transfers between devices, swapped(): return lax.ppermute(value, axis, pairs)  58.7 us
    pallas_call x1, Pallas kernels, scan_backward(): call(functools.partial(backward_kernel, heads), grid=(blocks,), in_specs=...  34.8 us
    pallas_call x3, Pallas kernels, projections(): call(kernel, grid=(columns // wide,), in_specs=ins, out_specs=outs, out_s...  27.9 us
    pallas_call x7, Pallas kernels, row_terms(): call(functools.partial(terms_kernel, ns, nf), grid_spec=pltpu.PrefetchSca...  25.1 us
    unnamed x165, local copies, waits for them, and re-layouts  19.3 us
    pallas_call x1, Pallas kernels, shards(): call(functools.partial(products_kernel, where, plan, lanes, tok, ns, nd),...  17.4 us
  transfers between devices with their start and end apart: 68, of which 27 were waited for; matrix products, arithmetic and copies ran while one was open for 16% of the time, Pallas kernels for 34%

commit v1 on v0

--- a/solution.py
+++ b/solution.py
@@ -23,6 +23,7 @@
 LANES = 128
 HALO = 16
 TILE = 256
+WIDE = 512
 VMEM_LIMIT = 48 * 1024 * 1024
 
 
@@ -84,11 +85,11 @@
     return pieces
 
 
-def call(kernel, **kwargs):
+def call(kernel, flops=1, **kwargs):
     return pl.pallas_call(
         kernel,
         compiler_params=pltpu.CompilerParams(vmem_limit_bytes=VMEM_LIMIT),
-        cost_estimate=pl.CostEstimate(flops=1, bytes_accessed=1, transcendentals=0),
+        cost_estimate=pl.CostEstimate(flops=flops, bytes_accessed=1, transcendentals=0),
         **kwargs,
     )
 
@@ -114,6 +115,7 @@
 
     return call(
         kernel,
+        flops=5 * 10**9,
         grid_spec=pltpu.PrefetchScalarGridSpec(
             num_scalar_prefetch=1,
             grid=(len(plan),),
@@ -282,7 +284,7 @@
 def projections(here, xn, pieces, nd, rows, columns, gate=None):
     if pieces[0].ndim == 2:
         nd = 0
-    wide = TILE if columns % TILE == 0 else LANES
+    wide = TILE if columns % TILE == 0 else columns
     if gate is not None:
         y, gain, starts, wide = gate
     tokens, depth = xn.shape
@@ -312,6 +314,7 @@
         ins.append(pl.BlockSpec(lead + (wide,), lambda i, n=len(lead): (0,) * n + (i,)))
     return call(
         kernel,
+        flops=2 * tokens * depth * columns if gate is None else 1,
         grid=(columns // wide,),
         in_specs=ins,
         out_specs=outs,
@@ -749,7 +752,7 @@
     return index
 
 
-def mixed_kernel(plan, ns, tok, here_ref, count_ref, ratio_ref, x_ref, *refs):
+def mixed_kernel(plan, split, ns, tok, here_ref, count_ref, ratio_ref, x_ref, *refs):
     shares, out_ref = refs[:-1], refs[-1]
     at = pl.ds(pl.multiple_of(here_ref[0] * tok, tok), tok)
     ratios = as_columns(ratio_ref[:, at])
@@ -758,7 +761,8 @@
         total = None
         for k in range(ns):
             for j in plan[w]:
-                term = shares[k][j].astype(F32) * count_ref[k, j * LEVELS + w]
+                at = (k, j) if k < 3 or j < split else (k + 1, j - split)
+                term = shares[at[0]][at[1]].astype(F32) * count_ref[k, j * LEVELS + w]
                 total = term if total is None else total + term
         out_ref[w] = (x + ratios[:, w : w + 1] * total).astype(BF)
 
@@ -956,11 +960,9 @@
     near_high, near_low = beside(2, held_a), beside(0, held_a)
     chip3 = across(3, held_a)
     pieces_a = over_dp(held_a)
-    held_b, pieces_a, chip3, near_high, xn_pieces = together(
-        held_b, pieces_a, chip3, near_high, xn_pieces
-    )
     xn = filled((ns, tok, D), [(p, None, (s ^ k, None, None)) for k, p in enumerate(xn_pieces)])
     xn = xn.reshape(length, D)
+    held_b, pieces_a, chip3, near_high, xn = together(held_b, pieces_a, chip3, near_high, xn)
 
     far3 = far(3, chip3)
     pieces_b = over_dp(held_b)
@@ -986,12 +988,11 @@
     bc_own = jax.nn.silu(pre_r).astype(BF)[:, :own_bc]
     bc_across = swapped(bc_own, "seq", 2)
     bc = [bc_own, swapped(bc_own, "seq", 1), bc_across, swapped(bc_across, "seq", 1)]
-    bc, held_z = together(bc, held_z)
     chip2, chip1 = across(2, bc[2]), across(1, bc[2])
+    pieces_b, xn_turned = together(pieces_b, xn_turned)
+    proj_b, full_b = projections(here, after(xn, bc[2]), ready([pieces_b], half), nd, rows_in, half)
+    proj_b, far3, near_low, held_z = together(proj_b, far3, near_low, held_z)
     pieces_z = over_dp(held_z)
-    pieces_b, xn_turned = together(pieces_b, xn_turned)
-    proj_b, full_b = projections(here, xn, ready([pieces_b], half), nd, rows_in, half)
-    proj_b, far3, near_low = together(proj_b, far3, near_low)
     bc = reordered_by_xor(bc, s)
     b_in = jnp.concatenate(bc[: ns // 2], axis=1)
     c_out = jnp.concatenate(bc[ns // 2 :], axis=1)
@@ -1041,13 +1042,13 @@
     range_of = [next(j for j, (a, b) in enumerate(lanes) if a <= i * out_rows < b) for i in range(nd)]
     smem = pl.BlockSpec(memory_space=pltpu.SMEM)
     cot_pieces = [cotangent, near_low, near_high, chip0, chip1, chip2, chip3, far0, far1, far2, far3]
-    cot_specs = [pl.BlockSpec((LEVELS, 1, tok, TILE), lambda i: (0, 0, 0, i))]
-    cot_specs += [pl.BlockSpec((2, tok, TILE), lambda i: (0, 0, i))] * 2
-    cot_specs += [pl.BlockSpec((tok, TILE), lambda i: (0, i))] * (2 * LEVELS)
+    cot_specs = [pl.BlockSpec((LEVELS, 1, tok, WIDE), lambda i: (0, 0, 0, i))]
+    cot_specs += [pl.BlockSpec((2, tok, WIDE), lambda i: (0, 0, i))] * 2
+    cot_specs += [pl.BlockSpec((tok, WIDE), lambda i: (0, i))] * (2 * LEVELS)
     where = [[(0, (w, 0)), (1 + w // 2, (w % 2,)), (3 + w, ()), (3 + LEVELS + w, ())] for w in range(LEVELS)]
     upper, *grad_out = call(
         functools.partial(upper_kernel, where, plan, nd, tok, ns),
-        grid=(D // TILE,),
+        grid=(D // WIDE,),
         in_specs=[
             smem,
             smem,
@@ -1056,9 +1057,9 @@
             pl.BlockSpec((width, length), lambda i: (0, 0)),
         ]
         + cot_specs,
-        out_specs=[pl.BlockSpec((len(lanes), length, TILE), lambda i: (0, 0, i))]
-        + [pl.BlockSpec((out_rows, TILE), lambda i: (0, i))]
-        + [pl.BlockSpec((out_rows // 2, TILE), lambda i: (0, i))] * (2 * nd - 2),
+        out_specs=[pl.BlockSpec((len(lanes), length, WIDE), lambda i: (0, 0, i))]
+        + [pl.BlockSpec((out_rows, WIDE), lambda i: (0, i))]
+        + [pl.BlockSpec((out_rows // 2, WIDE), lambda i: (0, i))] * (2 * nd - 2),
         out_shape=[jax.ShapeDtypeStruct((len(lanes), length, D), BF)]
         + [jax.ShapeDtypeStruct((out_rows, D), BF)]
         + [jax.ShapeDtypeStruct((out_rows // 2, D), BF)] * (2 * nd - 2),
@@ -1070,17 +1071,17 @@
     held_out, upper = together(held_out, upper)
     *shares, inner, full_out = call(
         functools.partial(products_kernel, where, plan, lanes, tok, ns, nd),
-        grid=(D // TILE,),
+        grid=(D // WIDE,),
         in_specs=[
             smem,
             smem,
             pl.BlockSpec((length, width), lambda i: (0, 0)),
         ]
-        + [pl.BlockSpec((nf, nd, w_out.shape[0], TILE), lambda i: (0, 0, 0, i))]
+        + [pl.BlockSpec((nf, nd, w_out.shape[0], WIDE), lambda i: (0, 0, 0, i))]
         + cot_specs,
-        out_specs=[pl.BlockSpec((len(lanes), tok, TILE), lambda i: (0, 0, i))] * ns
+        out_specs=[pl.BlockSpec((len(lanes), tok, WIDE), lambda i: (0, 0, i))] * ns
         + [pl.BlockSpec((LEVELS, length), lambda i: (0, 0))]
-        + [pl.BlockSpec((width, TILE), lambda i: (0, i))],
+        + [pl.BlockSpec((width, WIDE), lambda i: (0, i))],
         out_shape=[jax.ShapeDtypeStruct((len(lanes), tok, D), BF)] * ns
         + [jax.ShapeDtypeStruct((LEVELS, length), F32)]
         + [jax.ShapeDtypeStruct((width, D), BF)],
@@ -1165,16 +1166,20 @@
     dxn = input_grad(dz, dproj_s, dproj_r, full_z, full_a, full_b, ns, tok)
     pair = swapped(jnp.stack([picked(dxn, s ^ 1), picked(dxn, s ^ 3)]), "seq", 1)
 
-    late_s, late_r = together(dproj_s, after(dproj_r, dxn))
+    late_s, late_r, z_half = together(dproj_s, after(dproj_r, dxn), z_half)
+    z_pair = fsdp_rest(z_kept, z_half)
     right_other = [
         jnp.concatenate([in_terms(late_s, d ^ k, half, half), in_terms(late_r, d ^ k)], axis=2)
         for k in range(1, nd)
     ]
-    right_other, z_half, left_got, out_pair = together(right_other, z_half, left_got, out_pair)
+    right_other, left_got, out_pair = together(right_other, left_got, out_pair)
     right_got = dp_terms(right_other)
-    z_pair = fsdp_rest(z_kept, z_half)
-    own_s = in_terms(after(dproj_s, *right_other), d)
+    near = picked(dxn, s).astype(F32) + pair[0].astype(F32)
+    far_sum = (picked(dxn, s ^ 2).astype(F32) + pair[1].astype(F32)).astype(BF)
+    dxn_across = swapped(far_sum, "seq", 2)
+    own_s = in_terms(after(dproj_s, far_sum, *right_other), d)
     left_kept, left_sent = fsdp_half(own_s[:, :, :half], left_got)
+    left_sent, z_pair = together(left_sent, z_pair)
     left_half = swapped(left_sent, "fsdp", 1)
     own_r = in_terms(after(dproj_r, left_sent), d)
     flat = flattened(
@@ -1188,10 +1193,7 @@
             jnp.sum(dsum[CONV + 1].reshape(heads, HEADDIM), axis=1),
         ]
     )
-    near = picked(dxn, s).astype(F32) + pair[0].astype(F32)
-    far_sum = (picked(dxn, s ^ 2).astype(F32) + pair[1].astype(F32)).astype(BF)
-    dxn_across = swapped(far_sum, "seq", 2)
-    right_got, far_sum, left_half = together(right_got, far_sum, left_half)
+    right_got, left_half = together(right_got, left_half)
     left_pair = fsdp_rest(left_kept, left_half)
     own_right = jnp.concatenate([own_s[:, :, half:], own_r], axis=2)
     right_kept, right_sent = fsdp_half(own_right, right_got)
@@ -1201,21 +1203,22 @@
         functools.partial(
             mixed_kernel,
             [[j for j in range(len(lanes)) if range_level[:, j].min() <= w] for w in range(LEVELS)],
+            split,
             ns,
             tok,
         ),
-        grid=(D // TILE,),
+        grid=(D // WIDE,),
         in_specs=[
             smem,
             smem,
             pl.BlockSpec((LEVELS, length), lambda i: (0, 0)),
-            pl.BlockSpec((tok, TILE), lambda i: (0, i)),
+            pl.BlockSpec((tok, WIDE), lambda i: (0, i)),
         ]
-        + [pl.BlockSpec((len(lanes), tok, TILE), lambda i: (0, 0, i))] * ns,
-        out_specs=pl.BlockSpec((LEVELS, tok, TILE), lambda i: (0, 0, i)),
+        + [pl.BlockSpec((p.shape[0], tok, WIDE), lambda i: (0, 0, i)) for p in shares[:3] + third],
+        out_specs=pl.BlockSpec((LEVELS, tok, WIDE), lambda i: (0, 0, i)),
         out_shape=jax.ShapeDtypeStruct((LEVELS, tok, D), BF),
         name="mixed",
-    )(here, theirs, ratio, tokens[0], *after(shares[:3] + [jnp.concatenate(third)], right_sent))[:, None]
+    )(here, theirs, ratio, tokens[0], *after(shares[:3] + third, right_sent))[:, None]
     right_half, mixed, dxn_across = together(right_half, mixed, dxn_across)
     right_kept = after(right_kept, mixed)
     right_pair = fsdp_rest(right_kept, right_half)

time: 541 us -> 562 us (1.039)
  waiting for transfers between devices: 164 us -> 181 us
  local copies, waits for them, and re-layouts: 58.8 us -> 73 us
  Pallas kernels: 182 us -> 171 us
    ppermute x63, waiting for transfers between devices: 100 us -> 129 us  [swapped(): return lax.ppermute(value, axis, pairs)]
    optimization_barrier x0 -> x2, local copies, waits for them, and re-layouts: none -> 12.9 us  [the longest x1 6.5 us: after(): return lax.optimization_barrier((value,) + others)[0]]
    all_gather x5, waiting for transfers between devices: 63.1 us -> 52.5 us  [over_fsdp(): return lax.all_gather(chunk, 'fsdp', axis=0, tiled=False)]
  transfers between devices with their start and end apart: 68 -> 68, of which waited for: 27 -> 25; matrix products, arithmetic and copies ran while one was open for 16% -> 19% of each run, Pallas kernels for 34% -> 31%
where the time goes in v1:
time: 562 us; the launch traced here: 555 us
  waiting for transfers between devices  181 us (32%)
  Pallas kernels  171 us (30%)
  local copies, waits for them, and re-layouts  73 us (13%)
  starting transfers between devices  60.3 us (11%)
  other arithmetic  53.6 us (10%)
  between operations  15.7 us (3%)
    ppermute x63, waiting for transfers between devices, swapped(): return lax.ppermute(value, axis, pairs)  129 us
    ppermute x63, starting transfers between devices, swapped(): return lax.ppermute(value, axis, pairs)  60.1 us
    all_gather x5, waiting for transfers between devices, over_fsdp(): return lax.all_gather(chunk, 'fsdp', axis=0, tiled=False)  52.5 us
    pallas_call x1, Pallas kernels, scan_backward(): call(functools.partial(backward_kernel, heads), grid=(blocks,), in_specs=...  35 us
    pallas_call x7, Pallas kernels, row_terms(): call(functools.partial(terms_kernel, ns, nf), grid_spec=pltpu.PrefetchSca...  24.9 us
    pallas_call x3, Pallas kernels, projections(): call(kernel, flops=2 * tokens * depth * columns if gate is None else 1, g...  23.4 us
    pallas_call x1, Pallas kernels, scan_forward(): call(functools.partial(forward_kernel, heads), grid=(blocks,), in_specs=i...  16.9 us
    pallas_call x1, Pallas kernels, shards(): call(functools.partial(products_kernel, where, plan, lanes, tok, ns, nd),...  16.4 us
  transfers between devices with their start and end apart: 68, of which 25 were waited for; matrix products, arithmetic and copies ran while one was open for 19% of the time, Pallas kernels for 31%

profile of v1, /device:TPU:0, one launch (start us, length us, event | category | flops | bytes accessed | tf_op | source)
XLA Modules:
  0.0 554.8 jit_solution(15298141224506248757)
XLA Ops:
  18.0 5.3 collective-permute-done.1.refs_2_
  23.3 5.4 collective-permute-done.2.refs_3_
  37.0 5.1 slice_bitcast_fusion
  44.3 20.6 %all-gather.13.cloned.1.call-done = bf16[16,64,640]{2,1,0:T(8,128)(2,1)} async-done(((bf16[4,64,640]{2,1,0:T(8,128)(2,1)}), bf16[16,64,640]{2,1,0:T(8,128)(2,1)}) %all-gather.13.cloned.1.call-update) | async-done | bytes 1310736 | tf_op jit(solution)/shard_map/all_gather | solution.py:935
  72.3 4.7 filled.3
  77.0 6.4 %copy.227 = bf16[1024,2048]{0,1:T(8,128)(2,1)} copy(bf16[1024,2048]{1,0:T(8,128)(2,1)} %bitcast.256) | data formatting | bytes 8388608 | tf_op jit(solution)/shard_map/reshape | solution.py:964
  83.4 10.1 %all-gather.11.cloned.1.call-done = bf16[16,64,512]{2,1,0:T(8,128)(2,1)} async-done(((bf16[4,64,512]{2,1,0:T(8,128)(2,1)}), bf16[16,64,512]{2,1,0:T(8,128)(2,1)}) %all-gather.11.cloned.1.call-update) | async-done | bytes 1048592 | tf_op jit(solution)/shard_map/all_gather | solution.py:935
  93.6 4.3 collective-permute-done.4.refs_1_
  100.7 21.8 %all-gather.15.cloned.1.call-done = bf16[16,32,1024]{2,1,0:T(8,128)(2,1)} async-done(((bf16[4,32,1024]{2,1,0:T(8,128)(2,1)}), bf16[16,32,1024]{2,1,0:T(8,128)(2,1)}) %all-gather.15.cloned.1.call-update) | async-done | bytes 1048592 | tf_op jit(solution)/shard_map/all_gather | solution.py:935
  127.3 6.4 %copy.198.xn_ref = bf16[1024,2048]{1,0:T(8,128)(2,1)} copy(bf16[1024,2048]{0,1:T(8,128)(2,1)} %copy.227) | data formatting | bytes 8388608 | tf_op jit(solution)/shard_map/optimization_barrier | solution.py:55
  136.4 5.8 %project.2 = (bf16[1024,640]{1,0:T(8,128)(2,1)S(1)}, bf16[2048,640]{1,0:T(8,128)(2,1)}) custom-call(s32[2]{0:T(128)S(1)} %pad_add_fusion.2.here_ref, bf16[1024,2048]{1,0:T(8,128)(2,1)} %copy.198.xn_ref, bf16[4,4,64,640]{3,2,1,0:T(8,128)(2,1)S(1)} %bitcast.248, bf16[4,4,64,640]{3,2,1,0:T(8,128)(2,1)S(1)} %copy-done.38), custom_call_target="tpu_custom_call" | custom-call | flops 2684354560 | bytes 1 | tf_op jit(solution)/shard_map/project/pallas_call | solution.py:315
  147.5 5.5 collective-permute-done.11
  156.5 6.5 %copy.199.xn_ref = bf16[1024,2048]{1,0:T(8,128)(2,1)} copy(bf16[1024,2048]{0,1:T(8,128)(2,1)} %copy.227) | data formatting | bytes 8388608 | tf_op jit(solution)/shard_map/optimization_barrier | solution.py:51
  164.8 5.4 project.3
  171.1 16.9 %scan_forward.1 = (f32[1024,1024]{1,0:T(8,128)}, f32[8,128,1024]{2,1,0:T(8,128)}) custom-call(s32[8]{0:T(128)S(1)} %pad_add_fusion.1.segp_ref, s32[1024,1]{1,0:T(8,128)S(1)} %copy-done.12, s32[1,1024]{1,0:T(1,128)S(1)} %bitcast.243, f32[1024,128]{1,0:T(8,128)S(1)} %pad.53.mask_ref, bf16[1024,640]{1,0:T(8,128)(2,1)S(1)} %get-tuple-element.167.in_a_ref, ...), custom_call_target="tpu_custom_call" | custom-call | flops 1 | bytes 1 | tf_op jit(solution)/shard_map/scan_forward/pallas_call | solution.py:581
  196.6 22.0 %collective-permute-done.18.refs_3_ = bf16[4,4,32,1024]{3,2,1,0:T(8,128)(2,1)S(1)} collective-permute-done((bf16[4,4,32,1024]{3,2,1,0:T(8,128)(2,1)}, bf16[4,4,32,1024]{3,2,1,0:T(8,128)(2,1)S(1)}, u32[]{:S(2)}, u32[]{:S(2)}) %collective-permute-start.18) | collective-permute-done | bytes 1048608 | tf_op jit(solution)/shard_map/ppermute | solution.py:47
  219.8 12.2 %gated.1 = (bf16[1024,1024]{1,0:T(8,128)(2,1)}, bf16[2048,1024]{1,0:T(8,128)(2,1)}, bf16[1024,1024]{1,0:T(8,128)(2,1)}, bf16[1024,1024]{1,0:T(8,128)(2,1)}, f32[8,1024]{1,0:T(8,128)S(1)}) custom-call(s32[2]{0:T(128)S(1)} %pad_add_fusion.2.here_ref, bf16[1024,2048]{1,0:T(8,128)(2,1)} %copy.198.xn_ref, f32[1024,1024]{1,0:T(8,128)} %get-tuple-element.187.y_ref, ...), custom_call_target="tpu_custom_call" | custom-call | flops 1 | bytes 1 | tf_op jit(solution)/shard_map/gated/pallas_call | solution.py:315
  245.5 14.1 %upper.1 = (bf16[2,1024,2048]{2,1,0:T(8,128)(2,1)}, bf16[512,2048]{1,0:T(8,128)(2,1)}, bf16[256,2048]{1,0:T(8,128)(2,1)}, bf16[256,2048]{1,0:T(8,128)(2,1)S(1)}) custom-call(s32[2]{0:T(128)S(1)} %pad_add_fusion.2.here_ref, s32[2]{0:T(128)S(1)} %call_exported.0.range_ref, f32[2,4]{1,0:T(2,128)S(1)} %fusion.42.count_ref, f32[4,1024]{1,0:T(4,128)S(1)} %fusion.30.ratio_ref, ...), custom_call_target="tpu_custom_call" | custom-call | flops 1 | bytes 1 | tf_op jit(solution)/shard_map/upper/pallas_call | solution.py:1049
  262.5 16.4 %products.1 = (bf16[2,256,2048]{2,1,0:T(8,128)(2,1)}, bf16[2,256,2048]{2,1,0:T(8,128)(2,1)}, bf16[2,256,2048]{2,1,0:T(8,128)(2,1)}, bf16[2,256,2048]{2,1,0:T(8,1...) custom-call(s32[2]{0:T(128)S(1)} %pad_add_fusion.2.here_ref, f32[2,4]{1,0:T(2,128)S(1)} %fusion.42.count_ref, ...), custom_call_target="tpu_custom_call" | custom-call | flops 1 | bytes 1 | tf_op jit(solution)/shard_map/products/pallas_call | solution.py:1072
  289.5 12.3 %gate_backward.1 = (bf16[1024,1024]{1,0:T(8,128)(2,1)S(1)}, bf16[1024,1024]{1,0:T(8,128)(2,1)S(1)}, f32[8,1024]{1,0:T(8,128)S(1)}) custom-call(f32[2,4]{1,0:T(2,128)S(1)} %fusion.42.count_ref, bf16[2,1024,2048]{2,1,0:T(8,128)(2,1)} %get-tuple-element.209.upper_ref, bf16[1024,2048]{1,0:T(8,128)(2,1)} %get-tuple-element.212.w_ref, ...), custom_call_target="tpu_custom_call" | custom-call | flops 1 | bytes 1 | tf_op jit(solution)/shard_map/gate_backward/pallas_call | solution.py:1098
  303.1 6.2 %row_terms.7 = bf16[4,4,64,1024]{3,2,1,0:T(8,128)(2,1)} custom-call(s32[1]{0:T(128)} %bitcast.61.at_ref, bf16[2048,1024]{1,0:T(8,128)(2,1)} %bitcast.225, bf16[1024,1024]{1,0:T(8,128)(2,1)S(1)} %get-tuple-element.236.right_ref.dz_ref), custom_call_target="tpu_custom_call" | custom-call | flops 1 | bytes 1 | tf_op jit(solution)/shard_map/row_terms/pallas_call | solution.py:146
  318.1 35.0 %scan_backward.1 = (bf16[1024,1024]{1,0:T(8,128)(2,1)}, f32[1024,256]{1,0:T(8,128)S(1)}, f32[1024,128]{1,0:T(8,128)S(1)}, f32[1,128]{1,0:T(1,128)S(1)}, f32[8,1024]{1,0:T(8,128)S(1)}) custom-call(s32[8]{0:T(128)S(1)} %pad_add_fusion.1.segp_ref, s32[1024,1]{1,0:T(8,128)S(1)} %copy-done.12, s32[1,1024]{1,0:T(1,128)S(1)} %bitcast.244, ...), custom_call_target="tpu_custom_call" | custom-call | flops 1 | bytes 1 | tf_op jit(solution)/shard_map/scan_backward/pallas_call | solution.py:604
  360.7 4.9 row_terms.8
  380.5 13.6 %input_grad.1 = bf16[4,256,2048]{2,1,0:T(8,128)(2,1)} custom-call(bf16[1024,1024]{1,0:T(8,128)(2,1)S(1)} %copy-done.8, bf16[1024,1024]{1,0:T(8,128)(2,1)S(1)} %copy-done.2, bf16[1024,128]{1,0:T(8,128)(2,1)S(1)} %get-tuple-element.255.dr_ref.right_ref, bf16[2048,1024]{1,0:T(8,128)(2,1)} %get-tuple-element.243.wz_ref, ...), custom_call_target="tpu_custom_call" | custom-call | flops 1 | bytes 1 | tf_op jit(solution)/shard_map/input_grad/pallas_call | solution.py:220
  406.3 19.4 %collective-permute-done.42 = bf16[1,128,2048]{2,1,0:T(8,128)(2,1)} collective-permute-done((bf16[1,128,2048]{2,1,0:T(8,128)(2,1)}, bf16[1,128,2048]{2,1,0:T(8,128)(2,1)}, u32[]{:S(2)}, u32[]{:S(2)}) %collective-permute-start.42) | collective-permute-done | bytes 524320 | tf_op jit(solution)/shard_map/ppermute | solution.py:47
  432.6 4.9 row_terms.12
  439.4 13.7 %collective-permute-done.43 = bf16[1,256,1024]{2,1,0:T(8,128)(2,1)S(1)} collective-permute-done((bf16[1,256,1024]{2,1,0:T(8,128)(2,1)S(1)}, bf16[1,256,1024]{2,1,0:T(8,128)(2,1)S(1)}, u32[]{:S(2)}, u32[]{:S(2)}) %collective-permute-start.43) | collective-permute-done | bytes 524320 | tf_op jit(solution)/shard_map/ppermute | solution.py:47
  458.4 8.5 %collective-permute-done.45 = bf16[2,256,512]{2,1,0:T(8,128)(2,1)S(1)} collective-permute-done((bf16[2,256,512]{2,1,0:T(8,128)(2,1)S(1)}, bf16[2,256,512]{2,1,0:T(8,128)(2,1)S(1)}, u32[]{:S(2)}, u32[]{:S(2)}) %collective-permute-start.45) | collective-permute-done | bytes 524320 | tf_op jit(solution)/shard_map/ppermute | solution.py:47
  470.5 8.0 %collective-permute-done.47.refs_4_ = bf16[1,256,2048]{2,1,0:T(8,128)(2,1)S(1)} collective-permute-done((bf16[1,256,2048]{2,1,0:T(8,128)(2,1)S(1)}, bf16[1,256,2048]{2,1,0:T(8,128)(2,1)S(1)}, u32[]{:S(2)}, u32[]{:S(2)}) %collective-permute-start.47) | collective-permute-done | bytes 1048608 | tf_op jit(solution)/shard_map/ppermute | solution.py:47
  478.5 7.8 %mixed.1 = bf16[4,256,2048]{2,1,0:T(8,128)(2,1)} custom-call(s32[2]{0:T(128)S(1)} %pad_add_fusion.2.here_ref, f32[4,8]{1,0:T(4,128)S(1)} %fusion.37.count_ref, f32[4,1024]{1,0:T(4,128)S(1)} %fusion.30.ratio_ref, bf16[256,2048]{1,0:T(8,128)(2,1)S(1)} %bitcast.232, bf16[2,256,2048]{2,1,0:T(8,128)(2,1)S(1)} %copy-done.30, ...), custom_call_target="tpu_custom_call" | custom-call | flops 1 | bytes 1 | tf_op jit(solution)/shard_map/mixed/pallas_call | solution.py:1202
  496.8 5.0 collective-permute-done.48
  517.7 6.3 %collective-permute-done.53 = bf16[1,256,640]{2,1,0:T(8,128)(2,1)S(1)} collective-permute-done((bf16[1,256,640]{2,1,0:T(8,128)(2,1)S(1)}, bf16[1,256,640]{2,1,0:T(8,128)(2,1)S(1)}, u32[]{:S(2)}, u32[]{:S(2)}) %collective-permute-start.53) | collective-permute-done | bytes 327712 | tf_op jit(solution)/shard_map/ppermute | solution.py:47
  (496 shorter events, 198.4 us)
Async XLA Ops:
  7.2 57.7 %all-gather.13.cloned.1.call-start = ((), (), s32[]{:S(2)}) async-start(), calls=%async_computation.1 | async-start | bytes 1638400 | tf_op jit(solution)/shard_map/all_gather | solution.py:935
  15.9 28.4 %collective-permute-start.3 = (bf16[128,2048]{1,0:T(8,128)(2,1)}, bf16[128,2048]{1,0:T(8,128)(2,1)}, u32[]{:S(2)}, u32[]{:S(2)}) collective-permute-start(bf16[128,2048]{1,0:T(8,128)(2,1)} %param.28), channel_id=1, source_target_pairs={{0,16},{16,0},{1,17},{17,1},{2,18},{18,2},{3,19},{19,3},{4,20},{20... | collective-permute-start | bytes 1572872 | tf_op jit(solution)/shard_map/ppermute | solution.py:47
  30.4 63.0 %all-gather.11.cloned.1.call-start = ((), (), s32[]{:S(2)}) async-start(), calls=%async_computation | async-start | bytes 1310720 | tf_op jit(solution)/shard_map/all_gather | solution.py:935
  31.8 34.7 %collective-permute-start.8 = (bf16[256,2048]{1,0:T(8,128)(2,1)}, bf16[256,2048]{1,0:T(8,128)(2,1)}, u32[]{:S(2)}, u32[]{:S(2)}) collective-permute-start(bf16[256,2048]{1,0:T(8,128)(2,1)} %fusion.2.refs_0_), channel_id=1, source_target_pairs={{0,8},{4,12},{8,0},{12,4},{1,9},{5,13},{9,1},{13,5},{2,10},{6,14},... | collective-permute-start | bytes 3145736 | tf_op jit(solution)/shard_map/ppermute | solution.py:47
  36.9 85.5 %all-gather.15.cloned.1.call-start = ((), (), s32[]{:S(2)}) async-start(), calls=%async_computation.2 | async-start | bytes 1310720 | tf_op jit(solution)/shard_map/all_gather | solution.py:935
  64.9 33.0 %collective-permute-start.6 = (bf16[2,256,2048]{2,1,0:T(8,128)(2,1)}, bf16[2,256,2048]{2,1,0:T(8,128)(2,1)}, u32[]{:S(2)}, u32[]{:S(2)}) collective-permute-start(bf16[2,256,2048]{2,1,0:T(8,128)(2,1)} %get-tuple-element.158), channel_id=1, source_target_pairs={{0,4},{4,0},{8,12},{12,8},{1,5},{5,1},{9,13},{13,9},{2,6},{6,2},{1... | collective-permute-start | bytes 6291464 | tf_op jit(solution)/shard_map/ppermute | solution.py:47
  65.9 122.1 %all-gather.17.cloned.1.call-start = ((), (), s32[]{:S(2)}) async-start(), calls=%async_computation.3 | async-start | bytes 1310720 | tf_op jit(solution)/shard_map/all_gather | solution.py:935
  66.6 31.3 %collective-permute-start.4 = (bf16[4,4,64,640]{3,2,1,0:T(8,128)(2,1)}, bf16[4,4,64,640]{3,2,1,0:T(8,128)(2,1)S(1)}, u32[]{:S(2)}, u32[]{:S(2)}) collective-permute-start(bf16[4,4,64,640]{3,2,1,0:T(8,128)(2,1)} %bitcast.247), channel_id=1, source_target_pairs={{0,16},{16,0},{1,17},{17,1},{2,18},{18,2},{3,19},{19,3},{4,20},{20... | collective-permute-start | bytes 3932168 | tf_op jit(solution)/shard_map/ppermute | solution.py:47
  68.1 25.5 %collective-permute-start.5 = (bf16[256,2048]{1,0:T(8,128)(2,1)}, bf16[256,2048]{1,0:T(8,128)(2,1)}, u32[]{:S(2)}, u32[]{:S(2)}) collective-permute-start(bf16[256,2048]{1,0:T(8,128)(2,1)} %get-tuple-element.156), channel_id=1, source_target_pairs={{0,8},{4,12},{8,0},{12,4},{1,9},{5,13},{9,1},{13,5},{2,10},{6,14},... | collective-permute-start | bytes 3145736 | tf_op jit(solution)/shard_map/ppermute | solution.py:47
  98.0 163.3 %all-gather.19.cloned.1.call-start = ((), (), s32[]{:S(2)}) async-start(), calls=%async_computation.4 | async-start | bytes 5242880 | tf_op jit(solution)/shard_map/all_gather | solution.py:935
  122.6 47.7 %collective-permute-start.13 = (bf16[2,256,2048]{2,1,0:T(8,128)(2,1)}, bf16[2,256,2048]{2,1,0:T(8,128)(2,1)}, u32[]{:S(2)}, u32[]{:S(2)}) collective-permute-start(bf16[2,256,2048]{2,1,0:T(8,128)(2,1)} %get-tuple-element.176), channel_id=1, source_target_pairs={{0,4},{4,0},{1,5},{5,1},{2,6},{6,2},{3,7},{7,3},{16,20},{20,16},{1... | collective-permute-start | bytes 6291464 | tf_op jit(solution)/shard_map/ppermute | solution.py:47
  125.8 39.0 %collective-permute-start.10 = (bf16[4,4,64,512]{3,2,1,0:T(8,128)(2,1)}, bf16[4,4,64,512]{3,2,1,0:T(8,128)(2,1)}, u32[]{:S(2)}, u32[]{:S(2)}) collective-permute-start(bf16[4,4,64,512]{3,2,1,0:T(8,128)(2,1)} %bitcast.249), channel_id=1, source_target_pairs={{0,16},{16,0},{1,17},{17,1},{2,18},{18,2},{3,19},{19,3},{4,20},{20... | collective-permute-start | bytes 3145736 | tf_op jit(solution)/shard_map/ppermute | solution.py:47
  153.1 35.0 %collective-permute-start.16 = (bf16[256,2048]{1,0:T(8,128)(2,1)}, bf16[256,2048]{1,0:T(8,128)(2,1)}, u32[]{:S(2)}, u32[]{:S(2)}) collective-permute-start(bf16[256,2048]{1,0:T(8,128)(2,1)} %get-tuple-element.185), channel_id=1, source_target_pairs={{0,8},{4,12},{8,0},{12,4},{1,9},{5,13},{9,1},{13,5},{2,10},{6,14},... | collective-permute-start | bytes 3145736 | tf_op jit(solution)/shard_map/ppermute | solution.py:47
  170.3 26.3 %collective-permute-start.17 = (bf16[4,4,32,1024]{3,2,1,0:T(8,128)(2,1)}, bf16[4,4,32,1024]{3,2,1,0:T(8,128)(2,1)}, u32[]{:S(2)}, u32[]{:S(2)}) collective-permute-start(bf16[4,4,32,1024]{3,2,1,0:T(8,128)(2,1)} %bitcast.50.refs_0_), channel_id=1, source_target_pairs={{0,16},{16,0},{1,17},{17,1},{2,18},{18,2},{3,19},{19,3},{4,20},{20... | collective-permute-start | bytes 3145736 | tf_op jit(solution)/shard_map/ppermute | solution.py:47
  188.1 30.6 %collective-permute-start.18 = (bf16[4,4,32,1024]{3,2,1,0:T(8,128)(2,1)}, bf16[4,4,32,1024]{3,2,1,0:T(8,128)(2,1)S(1)}, u32[]{:S(2)}, u32[]{:S(2)}) collective-permute-start(bf16[4,4,32,1024]{3,2,1,0:T(8,128)(2,1)} %bitcast.238), channel_id=1, source_target_pairs={{0,16},{16,0},{1,17},{17,1},{2,18},{18,2},{3,19},{19,3},{4,20},{20... | collective-permute-start | bytes 3145736 | tf_op jit(solution)/shard_map/ppermute | solution.py:47
  189.5 42.5 %collective-permute-start.19 = (bf16[256,2048]{1,0:T(8,128)(2,1)}, bf16[256,2048]{1,0:T(8,128)(2,1)S(1)}, u32[]{:S(2)}, u32[]{:S(2)}) collective-permute-start(bf16[256,2048]{1,0:T(8,128)(2,1)} %get-tuple-element.196), channel_id=1, source_target_pairs={{8,0},{12,4},{9,1},{13,5},{10,2},{14,6},{11,3},{15,7},{24,16},{28,... | collective-permute-start | bytes 3145736 | tf_op jit(solution)/shard_map/ppermute | solution.py:47
  190.8 48.9 %collective-permute-start.23 = (bf16[256,2048]{1,0:T(8,128)(2,1)}, bf16[256,2048]{1,0:T(8,128)(2,1)}, u32[]{:S(2)}, u32[]{:S(2)}) collective-permute-start(bf16[256,2048]{1,0:T(8,128)(2,1)} %get-tuple-element.199), channel_id=1, source_target_pairs={{8,0},{12,4},{9,1},{13,5},{10,2},{14,6},{11,3},{15,7},{24,16},{28,... | collective-permute-start | bytes 3145736 | tf_op jit(solution)/shard_map/ppermute | solution.py:47
  260.7 25.5 %collective-permute-start.30 = (bf16[256,2048]{1,0:T(8,128)(2,1)}, bf16[256,2048]{1,0:T(8,128)(2,1)}, u32[]{:S(2)}, u32[]{:S(2)}) collective-permute-start(bf16[256,2048]{1,0:T(8,128)(2,1)} %get-tuple-element.215), channel_id=1, source_target_pairs={{0,16},{16,0},{1,17},{17,1},{2,18},{18,2},{3,19},{19,3},{4,20},{20... | collective-permute-start | bytes 3145736 | tf_op jit(solution)/shard_map/ppermute | solution.py:47
  286.2 25.9 %collective-permute-start.31 = (bf16[256,2048]{1,0:T(8,128)(2,1)}, bf16[256,2048]{1,0:T(8,128)(2,1)}, u32[]{:S(2)}, u32[]{:S(2)}) collective-permute-start(bf16[256,2048]{1,0:T(8,128)(2,1)} %copy-done.40), channel_id=1, source_target_pairs={{0,16},{16,0},{1,17},{17,1},{2,18},{18,2},{3,19},{19,3},{4,20},{20... | collective-permute-start | bytes 3145736 | tf_op jit(solution)/shard_map/ppermute | solution.py:47
  286.8 66.3 %collective-permute-start.34 = (bf16[2,256,2048]{2,1,0:T(8,128)(2,1)}, bf16[2,256,2048]{2,1,0:T(8,128)(2,1)S(1)}, u32[]{:S(2)}, u32[]{:S(2)}) collective-permute-start(bf16[2,256,2048]{2,1,0:T(8,128)(2,1)} %get-tuple-element.231), channel_id=1, source_target_pairs={{0,8},{4,12},{8,0},{12,4},{1,9},{5,13},{9,1},{13,5},{2,10},{6,14},... | collective-permute-start | bytes 6291464 | tf_op jit(solution)/shard_map/ppermute | solution.py:47
  309.4 56.2 %collective-permute-start.38 = (bf16[4,256,1024]{2,1,0:T(8,128)(2,1)}, bf16[4,256,1024]{2,1,0:T(8,128)(2,1)}, u32[]{:S(2)}, u32[]{:S(2)}) collective-permute-start(bf16[4,256,1024]{2,1,0:T(8,128)(2,1)} %bitcast.62), channel_id=1, source_target_pairs={{0,16},{16,0},{1,17},{17,1},{2,18},{18,2},{3,19},{19,3},{4,20},{20... | collective-permute-start | bytes 6291464 | tf_op jit(solution)/shard_map/ppermute | solution.py:47
  310.8 45.8 %collective-permute-start.35 = (bf16[1,256,2048]{2,1,0:T(8,128)(2,1)S(1)}, bf16[1,256,2048]{2,1,0:T(8,128)(2,1)S(1)}, u32[]{:S(2)}, u32[]{:S(2)}) collective-permute-start(bf16[1,256,2048]{2,1,0:T(8,128)(2,1)S(1)} %get-tuple-element.233), channel_id=1, source_target_pairs={{0,12},{4,8},{8,4},{12,0},{1,13},{5,9},{9,5},{13,1},{2,14},{6,10},... | collective-permute-start | bytes 3145736 | tf_op jit(solution)/shard_map/ppermute | solution.py:47
  315.7 40.9 %collective-permute-start.33 = (bf16[2,128,2048]{2,1,0:T(8,128)(2,1)S(1)}, bf16[2,128,2048]{2,1,0:T(8,128)(2,1)S(1)}, u32[]{:S(2)}, u32[]{:S(2)}) collective-permute-start(bf16[2,128,2048]{2,1,0:T(8,128)(2,1)S(1)} %pad_maximum_fusion.11), channel_id=1, source_target_pairs={{0,1},{1,0},{2,3},{3,2},{4,5},{5,4},{6,7},{7,6},{8,9},{9,8},{10,11... | collective-permute-start | bytes 3145736 | tf_op jit(solution)/shard_map/ppermute | solution.py:47
  372.0 29.9 %collective-permute-start.40 = (bf16[2,256,1024]{2,1,0:T(8,128)(2,1)}, bf16[2,256,1024]{2,1,0:T(8,128)(2,1)}, u32[]{:S(2)}, u32[]{:S(2)}) collective-permute-start(bf16[2,256,1024]{2,1,0:T(8,128)(2,1)} %pad_maximum_fusion.12), channel_id=1, source_target_pairs={{0,1},{1,0},{2,3},{3,2},{4,5},{5,4},{6,7},{7,6},{8,9},{9,8},{10,11... | collective-permute-start | bytes 3145736 | tf_op jit(solution)/shard_map/ppermute | solution.py:47
  377.3 48.4 %collective-permute-start.41 = (bf16[4,256,512]{2,1,0:T(8,128)(2,1)}, bf16[4,256,512]{2,1,0:T(8,128)(2,1)}, u32[]{:S(2)}, u32[]{:S(2)}) collective-permute-start(bf16[4,256,512]{2,1,0:T(8,128)(2,1)} %bitcast.66), channel_id=1, source_target_pairs={{0,16},{16,0},{1,17},{17,1},{2,18},{18,2},{3,19},{19,3},{4,20},{20... | collective-permute-start | bytes 3145736 | tf_op jit(solution)/shard_map/ppermute | solution.py:47
  397.3 32.2 %collective-permute-start.39 = (bf16[2,256,2048]{2,1,0:T(8,128)(2,1)}, bf16[2,256,2048]{2,1,0:T(8,128)(2,1)}, u32[]{:S(2)}, u32[]{:S(2)}) collective-permute-start(bf16[2,256,2048]{2,1,0:T(8,128)(2,1)} %pad_maximum_fusion.1), channel_id=1, source_target_pairs={{0,4},{4,0},{8,12},{12,8},{1,5},{5,1},{9,13},{13,9},{2,6},{6,2},{1... | collective-permute-start | bytes 6291464 | tf_op jit(solution)/shard_map/ppermute | solution.py:47
  399.7 26.0 %collective-permute-start.42 = (bf16[1,128,2048]{2,1,0:T(8,128)(2,1)}, bf16[1,128,2048]{2,1,0:T(8,128)(2,1)}, u32[]{:S(2)}, u32[]{:S(2)}) collective-permute-start(bf16[1,128,2048]{2,1,0:T(8,128)(2,1)} %get-tuple-element.417), channel_id=1, source_target_pairs={{0,2},{1,3},{2,0},{3,1},{4,6},{5,7},{6,4},{7,5},{8,10},{9,11},{10,... | collective-permute-start | bytes 1572872 | tf_op jit(solution)/shard_map/ppermute | solution.py:47
  428.2 24.8 %collective-permute-start.43 = (bf16[1,256,1024]{2,1,0:T(8,128)(2,1)S(1)}, bf16[1,256,1024]{2,1,0:T(8,128)(2,1)S(1)}, u32[]{:S(2)}, u32[]{:S(2)}) collective-permute-start(bf16[1,256,1024]{2,1,0:T(8,128)(2,1)S(1)} %get-tuple-element.415), channel_id=1, source_target_pairs={{0,2},{1,3},{2,0},{3,1},{4,6},{5,7},{6,4},{7,5},{8,10},{9,11},{10,... | collective-permute-start | bytes 1572872 | tf_op jit(solution)/shard_map/ppermute | solution.py:47
  428.2 30.2 %collective-permute-start.44 = (bf16[4,256,640]{2,1,0:T(8,128)(2,1)S(1)}, bf16[4,256,640]{2,1,0:T(8,128)(2,1)S(1)}, u32[]{:S(2)}, u32[]{:S(2)}) collective-permute-start(bf16[4,256,640]{2,1,0:T(8,128)(2,1)S(1)} %pad_maximum_fusion.3), channel_id=1, source_target_pairs={{0,16},{16,0},{1,17},{17,1},{2,18},{18,2},{3,19},{19,3},{4,20},{20... | collective-permute-start | bytes 3932168 | tf_op jit(solution)/shard_map/ppermute | solution.py:47
  453.0 25.5 %collective-permute-start.47 = (bf16[1,256,2048]{2,1,0:T(8,128)(2,1)S(1)}, bf16[1,256,2048]{2,1,0:T(8,128)(2,1)S(1)}, u32[]{:S(2)}, u32[]{:S(2)}) collective-permute-start(bf16[1,256,2048]{2,1,0:T(8,128)(2,1)S(1)} %copy-done.61), channel_id=1, source_target_pairs={{0,12},{4,8},{8,4},{12,0},{1,13},{5,9},{9,5},{13,1},{2,14},{6,10},... | collective-permute-start | bytes 3145736 | tf_op jit(solution)/shard_map/ppermute | solution.py:47
  457.1 44.7 %collective-permute-start.48 = (bf16[256,2048]{1,0:T(8,128)(2,1)}, bf16[256,2048]{1,0:T(8,128)(2,1)S(1)}, u32[]{:S(2)}, u32[]{:S(2)}) collective-permute-start(bf16[256,2048]{1,0:T(8,128)(2,1)} %fusion.10), channel_id=1, source_target_pairs={{0,8},{4,12},{8,0},{12,4},{1,9},{5,13},{9,1},{13,5},{2,10},{6,14},... | collective-permute-start | bytes 3145736 | tf_op jit(solution)/shard_map/ppermute | solution.py:47
  468.8 33.0 %collective-permute-start.46 = (bf16[2,256,640]{2,1,0:T(8,128)(2,1)}, bf16[2,256,640]{2,1,0:T(8,128)(2,1)}, u32[]{:S(2)}, u32[]{:S(2)}) collective-permute-start(bf16[2,256,640]{2,1,0:T(8,128)(2,1)} %pad_maximum_fusion.13), channel_id=1, source_target_pairs={{0,1},{1,0},{2,3},{3,2},{4,5},{5,4},{6,7},{7,6},{8,9},{9,8},{10,11... | collective-permute-start | bytes 1966088 | tf_op jit(solution)/shard_map/ppermute | solution.py:47
  (117 other events, 1161.8 us)
Sparse Core Ops, SparseCore 0:
  30.5 34.3 all-gather.12
  66.5 26.9 all-gather.10
  95.0 27.4 all-gather.14
  123.9 27.4 all-gather.16
  153.4 80.2 all-gather.18

commit v2 on v1

--- a/solution.py
+++ b/solution.py
@@ -85,11 +85,11 @@
     return pieces
 
 
-def call(kernel, flops=1, **kwargs):
+def call(kernel, **kwargs):
     return pl.pallas_call(
         kernel,
         compiler_params=pltpu.CompilerParams(vmem_limit_bytes=VMEM_LIMIT),
-        cost_estimate=pl.CostEstimate(flops=flops, bytes_accessed=1, transcendentals=0),
+        cost_estimate=pl.CostEstimate(flops=1, bytes_accessed=1, transcendentals=0),
         **kwargs,
     )
 
@@ -115,7 +115,6 @@
 
     return call(
         kernel,
-        flops=5 * 10**9,
         grid_spec=pltpu.PrefetchScalarGridSpec(
             num_scalar_prefetch=1,
             grid=(len(plan),),
@@ -239,15 +238,6 @@
                 full_ref[pl.ds(at, rows), :] = piece[k, i]
 
 
-def project_kernel(nd, count, here_ref, xn_ref, *refs):
-    pieces, (out_ref, full_ref) = refs[:count], refs[count:]
-    if nd:
-        assembled(here_ref, pieces, nd, full_ref)
-    else:
-        full_ref[...] = pieces[0][...]
-    out_ref[...] = dot(xn_ref[...], full_ref[...]).astype(BF)
-
-
 def gated_kernel(nd, count, starts, wide, here_ref, xn_ref, y_ref, gain_ref, *refs):
     pieces, (out_ref, full_ref, gated_ref, turned_ref, squares_ref, sums) = refs[:count], refs[count:]
     step = pl.program_id(0)
@@ -281,47 +271,41 @@
         squares_ref[...] = total.T[: squares_ref.shape[0]]
 
 
-def projections(here, xn, pieces, nd, rows, columns, gate=None):
+def gated_projection(here, xn, pieces, nd, columns, y, gain, starts, wide):
     if pieces[0].ndim == 2:
         nd = 0
-    wide = TILE if columns % TILE == 0 else columns
-    if gate is not None:
-        y, gain, starts, wide = gate
     tokens, depth = xn.shape
-    outs = [pl.BlockSpec((tokens, wide), lambda i: (0, i)), pl.BlockSpec((depth, wide), lambda i: (0, i))]
-    shapes = [jax.ShapeDtypeStruct((tokens, columns), BF), jax.ShapeDtypeStruct((depth, columns), BF)]
-    ins = [pl.BlockSpec(memory_space=pltpu.SMEM), pl.BlockSpec((tokens, depth), lambda i: (0, 0))]
-    operands = [here, xn]
-    scratch = []
-    kernel = functools.partial(project_kernel, nd, len(pieces))
-    if gate is not None:
-        kernel = functools.partial(gated_kernel, nd, len(pieces), starts, wide)
-        operands += [y, gain]
-        ins += [outs[0], pl.BlockSpec((1, wide), lambda i: (0, i))]
-        outs += [
-            outs[0],
-            pl.BlockSpec((wide, tokens), lambda i: (i, 0)),
-            pl.BlockSpec((8, tokens), lambda i: (0, 0)),
-        ]
-        shapes += [
-            shapes[0],
-            jax.ShapeDtypeStruct((columns, tokens), BF),
-            jax.ShapeDtypeStruct((8, tokens), F32),
-        ]
-        scratch = [pltpu.VMEM((len(starts), tokens, LANES), F32)]
+    tile = pl.BlockSpec((tokens, wide), lambda i: (0, i))
+    ins = [
+        pl.BlockSpec(memory_space=pltpu.SMEM),
+        pl.BlockSpec((tokens, depth), lambda i: (0, 0)),
+        tile,
+        pl.BlockSpec((1, wide), lambda i: (0, i)),
+    ]
     for piece in pieces:
         lead = piece.shape[:-1]
         ins.append(pl.BlockSpec(lead + (wide,), lambda i, n=len(lead): (0,) * n + (i,)))
     return call(
-        kernel,
-        flops=2 * tokens * depth * columns if gate is None else 1,
+        functools.partial(gated_kernel, nd, len(pieces), starts, wide),
         grid=(columns // wide,),
         in_specs=ins,
-        out_specs=outs,
-        out_shape=shapes,
-        scratch_shapes=scratch,
-        name="gated" if gate is not None else "project",
-    )(*operands, *pieces)
+        out_specs=[
+            tile,
+            pl.BlockSpec((depth, wide), lambda i: (0, i)),
+            tile,
+            pl.BlockSpec((wide, tokens), lambda i: (i, 0)),
+            pl.BlockSpec((8, tokens), lambda i: (0, 0)),
+        ],
+        out_shape=[
+            jax.ShapeDtypeStruct((tokens, columns), BF),
+            jax.ShapeDtypeStruct((depth, columns), BF),
+            jax.ShapeDtypeStruct((tokens, columns), BF),
+            jax.ShapeDtypeStruct((columns, tokens), BF),
+            jax.ShapeDtypeStruct((8, tokens), F32),
+        ],
+        scratch_shapes=[pltpu.VMEM((len(starts), tokens, LANES), F32)],
+        name="gated",
+    )(here, xn, y, gain, *pieces)
 
 
 def tri(rows_first):
@@ -937,18 +921,11 @@
     def over_dp(held):
         return [held] + [swapped(held, "dp", j) for j in range(1, nd)]
 
-    row_halves = 2 if rows_in % 32 == 0 else 1
-
-    def ready(parts, columns):
-        if rows_in % 16 == 0:
-            return [piece for pieces in parts for piece in pieces]
+    def whole(pieces, columns):
         moves = [
-            (piece, i, (d ^ j, None, i, h, None, None))
-            for h, pieces in enumerate(parts)
-            for j, piece in enumerate(pieces)
-            for i in range(nf)
+            (piece, i, (d ^ j, None, i, None, None)) for j, piece in enumerate(pieces) for i in range(nf)
         ]
-        return [filled((nd, ns, nf, len(parts), rows_in // len(parts), columns), moves).reshape(D, columns)]
+        return filled((nd, ns, nf, rows_in, columns), moves).reshape(D, columns)
 
     held_a = over_fsdp(mine[:, :, :first])
     held_b = over_fsdp(mine[:, :, first:cols])
@@ -960,20 +937,21 @@
     near_high, near_low = beside(2, held_a), beside(0, held_a)
     chip3 = across(3, held_a)
     pieces_a = over_dp(held_a)
+    held_b, pieces_a, chip3, near_high, xn_pieces = together(
+        held_b, pieces_a, chip3, near_high, xn_pieces
+    )
     xn = filled((ns, tok, D), [(p, None, (s ^ k, None, None)) for k, p in enumerate(xn_pieces)])
     xn = xn.reshape(length, D)
-    held_b, pieces_a, chip3, near_high, xn = together(held_b, pieces_a, chip3, near_high, xn)
 
     far3 = far(3, chip3)
     pieces_b = over_dp(held_b)
-    parts_z = mine_z.reshape(ns, row_halves, rows_in // row_halves, width)
-    held_z = over_fsdp(after(parts_z[:, 0], held_a))
-    late_z = [over_fsdp(after(parts_z[:, h], held_b)) for h in range(1, row_halves)]
+    held_z = over_fsdp(after(mine_z, held_a))
     held_out = over_fsdp(after(jnp.stack([w_out] + other_out), held_z))
 
     xn_turned = xn.T
     here = jnp.stack([s, d]).astype(jnp.int32)
-    proj_a, full_a = projections(here, xn, ready([pieces_a], first), nd, rows_in, first)
+    full_a = whole(pieces_a, first)
+    proj_a = dot(xn, full_a).astype(BF)
 
     proj_r = proj_a[:, half:]
     mixer = jnp.concatenate([jnp.zeros((reach, cols - width), BF), proj_r], axis=0)
@@ -989,8 +967,8 @@
     bc_across = swapped(bc_own, "seq", 2)
     bc = [bc_own, swapped(bc_own, "seq", 1), bc_across, swapped(bc_across, "seq", 1)]
     chip2, chip1 = across(2, bc[2]), across(1, bc[2])
-    pieces_b, xn_turned = together(pieces_b, xn_turned)
-    proj_b, full_b = projections(here, after(xn, bc[2]), ready([pieces_b], half), nd, rows_in, half)
+    full_b = whole(pieces_b, half)
+    proj_b = dot(xn, after(full_b, proj_a, xn_turned, bc[2])).astype(BF)
     proj_b, far3, near_low, held_z = together(proj_b, far3, near_low, held_z)
     pieces_z = over_dp(held_z)
     bc = reordered_by_xor(bc, s)
@@ -1021,14 +999,14 @@
         jnp.repeat(skip_own, HEADDIM)[None, :],
     )
     y, priors = scan_forward(heads, blocks, operands)
-    y, chip2, late_z = together(y, chip2, late_z)
+    y, chip2 = together(y, chip2)
     far2, chip0 = far(2, chip2), across(0, y)
-    parts = [pieces_z] + [over_dp(piece) for piece in late_z]
+    parts = pieces_z if rows_in % 16 == 0 else [whole(pieces_z, width)]
     lanes = [(a * HEADDIM, b * HEADDIM) for a, b in ranges]
     starts = [a for a, _ in lanes]
     wide = min(min(b - a for a, b in lanes), TILE)
-    proj_z, full_z, q_gain, q_turned, squares = projections(
-        here, xn, ready(parts, width), nd, rows_in, width, (y, gain[None], starts, wide)
+    proj_z, full_z, q_gain, q_turned, squares = gated_projection(
+        here, xn, parts, nd, width, y, gain[None], starts, wide
     )
     squares, chip1 = together(squares[: len(lanes)], chip1)
     far1 = far(1, chip1)
@@ -1166,20 +1144,16 @@
     dxn = input_grad(dz, dproj_s, dproj_r, full_z, full_a, full_b, ns, tok)
     pair = swapped(jnp.stack([picked(dxn, s ^ 1), picked(dxn, s ^ 3)]), "seq", 1)
 
-    late_s, late_r, z_half = together(dproj_s, after(dproj_r, dxn), z_half)
-    z_pair = fsdp_rest(z_kept, z_half)
+    late_s, late_r = together(dproj_s, after(dproj_r, dxn))
     right_other = [
         jnp.concatenate([in_terms(late_s, d ^ k, half, half), in_terms(late_r, d ^ k)], axis=2)
         for k in range(1, nd)
     ]
-    right_other, left_got, out_pair = together(right_other, left_got, out_pair)
+    right_other, z_half, left_got, out_pair = together(right_other, z_half, left_got, out_pair)
     right_got = dp_terms(right_other)
-    near = picked(dxn, s).astype(F32) + pair[0].astype(F32)
-    far_sum = (picked(dxn, s ^ 2).astype(F32) + pair[1].astype(F32)).astype(BF)
-    dxn_across = swapped(far_sum, "seq", 2)
-    own_s = in_terms(after(dproj_s, far_sum, *right_other), d)
+    z_pair = fsdp_rest(z_kept, z_half)
+    own_s = in_terms(after(dproj_s, *right_other), d)
     left_kept, left_sent = fsdp_half(own_s[:, :, :half], left_got)
-    left_sent, z_pair = together(left_sent, z_pair)
     left_half = swapped(left_sent, "fsdp", 1)
     own_r = in_terms(after(dproj_r, left_sent), d)
     flat = flattened(
@@ -1193,7 +1167,10 @@
             jnp.sum(dsum[CONV + 1].reshape(heads, HEADDIM), axis=1),
         ]
     )
-    right_got, left_half = together(right_got, left_half)
+    near = picked(dxn, s).astype(F32) + pair[0].astype(F32)
+    far_sum = (picked(dxn, s ^ 2).astype(F32) + pair[1].astype(F32)).astype(BF)
+    dxn_across = swapped(far_sum, "seq", 2)
+    right_got, far_sum, left_half = together(right_got, far_sum, left_half)
     left_pair = fsdp_rest(left_kept, left_half)
     own_right = jnp.concatenate([own_s[:, :, half:], own_r], axis=2)
     right_kept, right_sent = fsdp_half(own_right, right_got)

time: 562 us -> 521 us (0.927)
  waiting for transfers between devices: 181 us -> 152 us
  local copies, waits for them, and re-layouts: 73 us -> 61.6 us
  matrix products: 0 us -> 9.72 us
    all_gather x5 -> x4, waiting for transfers between devices: 52.5 us -> 33.8 us  [over_fsdp(): return lax.all_gather(chunk, 'fsdp', axis=0, tiled=False)]
    optimization_barrier x2 -> x0, local copies, waits for them, and re-layouts: 12.9 us -> none  [the longest x1 6.5 us: after(): return lax.optimization_barrier((value,) + others)[0]]
    ppermute x63 -> x62, waiting for transfers between devices: 129 us -> 118 us  [swapped(): return lax.ppermute(value, axis, pairs)]
    dot_general x0 -> x2, matrix products: none -> 9.72 us  [dot(): lax.dot_general(a, b, (dims, ((), ())), preferred_element_type=F32, preci...]
    unnamed x165 -> x157, local copies, waits for them, and re-layouts: 16.3 us -> 21.3 us
    ppermute x63 -> x62, starting transfers between devices: 60.1 us -> 55.4 us  [swapped(): return lax.ppermute(value, axis, pairs)]
  transfers between devices with their start and end apart: 68 -> 66, of which waited for: 25 -> 22; matrix products, arithmetic and copies ran while one was open for 19% -> 18% of each run, Pallas kernels for 31% -> 32%
where the time goes in v2:
time: 521 us; the launch traced here: 514 us
  Pallas kernels  166 us (32%)
  waiting for transfers between devices  152 us (29%)
  local copies, waits for them, and re-layouts  61.6 us (12%)
  starting transfers between devices  55.6 us (11%)
  other arithmetic  53.1 us (10%)
  between operations  15.7 us (3%)
  matrix products  9.72 us (2%)
    ppermute x62, waiting for transfers between devices, swapped(): return lax.ppermute(value, axis, pairs)  118 us
    ppermute x62, starting transfers between devices, swapped(): return lax.ppermute(value, axis, pairs)  55.4 us
    pallas_call x1, Pallas kernels, scan_backward(): call(functools.partial(backward_kernel, heads), grid=(blocks,), in_specs=...  35 us
    all_gather x4, waiting for transfers between devices, over_fsdp(): return lax.all_gather(chunk, 'fsdp', axis=0, tiled=False)  33.8 us
    pallas_call x7, Pallas kernels, row_terms(): call(functools.partial(terms_kernel, ns, nf), grid_spec=pltpu.PrefetchSca...  25 us
    unnamed x157, local copies, waits for them, and re-layouts  21.3 us
    pallas_call x1, Pallas kernels, scan_forward(): call(functools.partial(forward_kernel, heads), grid=(blocks,), in_specs=i...  16.7 us
    pallas_call x1, Pallas kernels, shards(): call(functools.partial(products_kernel, where, plan, lanes, tok, ns, nd),...  16.4 us
  transfers between devices with their start and end apart: 66, of which 22 were waited for; matrix products, arithmetic and copies ran while one was open for 18% of the time, Pallas kernels for 32%

profile of v2, /device:TPU:0, one launch (start us, length us, event | category | flops | bytes accessed | tf_op | source)
XLA Modules:
  0.0 514.1 jit_solution(2808174360712506843)
XLA Ops:
  15.9 7.4 %collective-permute-done.1.refs_2_ = bf16[64,2176]{1,0:T(8,128)(2,1)S(1)} collective-permute-done((bf16[64,2176]{1,0:T(8,128)(2,1)S(1)}, bf16[64,2176]{1,0:T(8,128)(2,1)S(1)}, u32[]{:S(2)}, u32[]{:S(2)}) %collective-permute-start.1) | collective-permute-done | bytes 278560 | tf_op jit(solution)/shard_map/ppermute | solution.py:47
  23.3 5.4 %collective-permute-done.2.refs_3_ = bf16[64,2176]{1,0:T(8,128)(2,1)S(1)} collective-permute-done((bf16[64,2176]{1,0:T(8,128)(2,1)S(1)}, bf16[64,2176]{1,0:T(8,128)(2,1)S(1)}, u32[]{:S(2)}, u32[]{:S(2)}) %collective-permute-start.2) | collective-permute-done | bytes 278560 | tf_op jit(solution)/shard_map/ppermute | solution.py:47
  35.7 5.0 slice_bitcast_fusion
  44.8 19.8 %all-gather.11.cloned.1.call-done = bf16[16,64,640]{2,1,0:T(8,128)(2,1)} async-done(((bf16[4,64,640]{2,1,0:T(8,128)(2,1)}), bf16[16,64,640]{2,1,0:T(8,128)(2,1)}) %all-gather.11.cloned.1.call-update) | async-done | bytes 1310736 | tf_op jit(solution)/shard_map/all_gather | solution.py:919
  68.5 21.2 %collective-permute-done.8.refs_2_ = bf16[256,2048]{1,0:T(8,128)(2,1)} collective-permute-done((bf16[256,2048]{1,0:T(8,128)(2,1)S(1)}, bf16[256,2048]{1,0:T(8,128)(2,1)}, u32[]{:S(2)}, u32[]{:S(2)}) %collective-permute-start.8) | collective-permute-done | bytes 1048608 | tf_op jit(solution)/shard_map/ppermute | solution.py:47
  97.1 18.5 %collective-permute-done.5.refs_6_.refs_7_ = bf16[256,2048]{1,0:T(8,128)(2,1)} collective-permute-done((bf16[256,2048]{1,0:T(8,128)(2,1)}, bf16[256,2048]{1,0:T(8,128)(2,1)}, u32[]{:S(2)}, u32[]{:S(2)}) %collective-permute-start.5) | collective-permute-done | bytes 1048608 | tf_op jit(solution)/shard_map/ppermute | solution.py:47
  121.8 4.9 filled.5
  126.7 14.0 %all-gather.13.cloned.1.call-done = bf16[16,64,1024]{2,1,0:T(8,128)(2,1)} async-done(((bf16[4,64,1024]{2,1,0:T(8,128)(2,1)}), bf16[16,64,1024]{2,1,0:T(8,128)(2,1)}) %all-gather.13.cloned.1.call-update) | async-done | bytes 2097168 | tf_op jit(solution)/shard_map/all_gather | solution.py:919
  140.7 6.4 %convolution_convert_fusion.in_a_ref = bf16[1024,640]{1,0:T(8,128)(2,1)S(1)} fusion(bf16[1024,2048]{1,0:T(8,128)(2,1)} %bitcast.265, bf16[2048,640]{1,0:T(8,128)(2,1)} %bitcast.246), kind=kOutput, calls=%fused_computation.36 | convolution fusion | flops 2685009920 | bytes 8126464 | tf_op jit(solution)/shard_map/dot_general | solution.py:31
  150.8 6.5 %copy.203 = bf16[1024,2048]{0,1:T(8,128)(2,1)} copy(bf16[1024,2048]{1,0:T(8,128)(2,1)} %bitcast.266) | data formatting | bytes 8388608 | tf_op jit(solution)/shard_map/reshape | solution.py:944
  161.5 3.3 convolution_convert_fusion.1.in_b_ref
  173.0 16.7 %scan_forward.1 = (f32[1024,1024]{1,0:T(8,128)}, f32[8,128,1024]{2,1,0:T(8,128)}) custom-call(s32[8]{0:T(128)S(1)} %pad_add_fusion.15.segp_ref, s32[1024,1]{1,0:T(8,128)S(1)} %copy-done.14, s32[1,1024]{1,0:T(1,128)S(1)} %bitcast.260, f32[1024,128]{1,0:T(8,128)S(1)} %pad.55.mask_ref, bf16[1024,640]{1,0:T(8,128)(2,1)S(1)} %convolution_convert_fusion.in_a_ref, ...), custom_call_target="tpu_custom_call" | custom-call | flops 1 | bytes 1 | tf_op jit(solution)/shard_map/scan_forward/pallas_call | solution.py:565
  195.0 18.0 %collective-permute-done.17.refs_1_ = bf16[4,4,64,1024]{3,2,1,0:T(8,128)(2,1)} collective-permute-done((bf16[4,4,64,1024]{3,2,1,0:T(8,128)(2,1)}, bf16[4,4,64,1024]{3,2,1,0:T(8,128)(2,1)}, u32[]{:S(2)}, u32[]{:S(2)}) %collective-permute-start.17) | collective-permute-done | bytes 2097184 | tf_op jit(solution)/shard_map/ppermute | solution.py:47
  213.0 12.1 %gated.1 = (bf16[1024,1024]{1,0:T(8,128)(2,1)S(1)}, bf16[2048,1024]{1,0:T(8,128)(2,1)}, bf16[1024,1024]{1,0:T(8,128)(2,1)S(1)}, bf16[1024,1024]{1,0:T(8,128)(2,1)}, f32[8,1024]{1,0:T(8,128)S(1)}) custom-call(s32[2]{0:T(128)S(1)} %pad_add_fusion.16.here_ref, bf16[1024,2048]{1,0:T(8,128)(2,1)} %bitcast.267, f32[1024,1024]{1,0:T(8,128)} %get-tuple-element.175.y_ref, ...), custom_call_target="tpu_custom_call" | custom-call | flops 1 | bytes 1 | tf_op jit(solution)/shard_map/gated/pallas_call | solution.py:288
  232.3 4.8 collective-permute-done.20
  242.7 14.1 %upper.1 = (bf16[2,1024,2048]{2,1,0:T(8,128)(2,1)}, bf16[512,2048]{1,0:T(8,128)(2,1)}, bf16[256,2048]{1,0:T(8,128)(2,1)}, bf16[256,2048]{1,0:T(8,128)(2,1)S(1)}) custom-call(s32[2]{0:T(128)S(1)} %pad_add_fusion.16.here_ref, s32[2]{0:T(128)S(1)} %call_exported.0.range_ref, f32[2,4]{1,0:T(2,128)S(1)} %fusion.42.count_ref, f32[4,1024]{1,0:T(4,128)S(1)} %fusion.30.ratio_ref, ...), custom_call_target="tpu_custom_call" | custom-call | flops 1 | bytes 1 | tf_op jit(solution)/shard_map/upper/pallas_call | solution.py:1027
  259.6 16.4 %products.1 = (bf16[2,256,2048]{2,1,0:T(8,128)(2,1)}, bf16[2,256,2048]{2,1,0:T(8,128)(2,1)}, bf16[2,256,2048]{2,1,0:T(8,128)(2,1)}, bf16[2,256,2048]{2,1,0:T(8,1...) custom-call(s32[2]{0:T(128)S(1)} %pad_add_fusion.16.here_ref, f32[2,4]{1,0:T(2,128)S(1)} %fusion.42.count_ref, ...), custom_call_target="tpu_custom_call" | custom-call | flops 1 | bytes 1 | tf_op jit(solution)/shard_map/products/pallas_call | solution.py:1050
  283.9 12.3 %gate_backward.1 = (bf16[1024,1024]{1,0:T(8,128)(2,1)S(1)}, bf16[1024,1024]{1,0:T(8,128)(2,1)S(1)}, f32[8,1024]{1,0:T(8,128)S(1)}) custom-call(f32[2,4]{1,0:T(2,128)S(1)} %fusion.42.count_ref, bf16[2,1024,2048]{2,1,0:T(8,128)(2,1)} %get-tuple-element.196.upper_ref, bf16[1024,2048]{1,0:T(8,128)(2,1)} %get-tuple-element.199.w_ref, ...), custom_call_target="tpu_custom_call" | custom-call | flops 1 | bytes 1 | tf_op jit(solution)/shard_map/gate_backward/pallas_call | solution.py:1076
  297.6 6.3 %row_terms.7 = bf16[4,4,64,1024]{3,2,1,0:T(8,128)(2,1)} custom-call(s32[1]{0:T(128)} %bitcast.49.at_ref, bf16[2048,1024]{1,0:T(8,128)(2,1)} %bitcast.238, bf16[1024,1024]{1,0:T(8,128)(2,1)S(1)} %get-tuple-element.223.right_ref.dz_ref), custom_call_target="tpu_custom_call" | custom-call | flops 1 | bytes 1 | tf_op jit(solution)/shard_map/row_terms/pallas_call | solution.py:145
  315.2 35.0 %scan_backward.1 = (bf16[1024,1024]{1,0:T(8,128)(2,1)}, f32[1024,256]{1,0:T(8,128)S(1)}, f32[1024,128]{1,0:T(8,128)S(1)}, f32[1,128]{1,0:T(1,128)S(1)}, f32[8,1024]{1,0:T(8,128)S(1)}) custom-call(s32[8]{0:T(128)S(1)} %pad_add_fusion.15.segp_ref, s32[1024,1]{1,0:T(8,128)S(1)} %copy-done.15, s32[1,1024]{1,0:T(1,128)S(1)} %bitcast.261, ...), custom_call_target="tpu_custom_call" | custom-call | flops 1 | bytes 1 | tf_op jit(solution)/shard_map/scan_backward/pallas_call | solution.py:588
  355.6 4.9 row_terms.8
  360.6 3.5 add_convert_fusion.7
  371.2 4.0 row_terms.9
  378.9 13.6 %input_grad.1 = bf16[4,256,2048]{2,1,0:T(8,128)(2,1)} custom-call(bf16[1024,1024]{1,0:T(8,128)(2,1)S(1)} %copy-done.8, bf16[1024,1024]{1,0:T(8,128)(2,1)S(1)} %copy-done.2, bf16[1024,128]{1,0:T(8,128)(2,1)S(1)} %get-tuple-element.238.dr_ref.right_ref, bf16[2048,1024]{1,0:T(8,128)(2,1)} %get-tuple-element.230.wz_ref, bf16[2048,640]{1,0:T(8,128)(2,1)} %bitcast.247, ...), custom_call_target="tpu_custom_call" | custom-call | flops 1 | bytes 1 | tf_op jit(solution)/shard_map/input_grad/pallas_call | solution.py:219
  395.7 3.5 row_terms.10
  405.5 4.9 row_terms.12
  423.7 11.0 %collective-permute-done.43 = bf16[2,256,512]{2,1,0:T(8,128)(2,1)S(1)} collective-permute-done((bf16[2,256,512]{2,1,0:T(8,128)(2,1)S(1)}, bf16[2,256,512]{2,1,0:T(8,128)(2,1)S(1)}, u32[]{:S(2)}, u32[]{:S(2)}) %collective-permute-start.43) | collective-permute-done | bytes 524320 | tf_op jit(solution)/shard_map/ppermute | solution.py:47
  439.8 7.9 %mixed.1 = bf16[4,256,2048]{2,1,0:T(8,128)(2,1)} custom-call(s32[2]{0:T(128)S(1)} %pad_add_fusion.16.here_ref, f32[4,8]{1,0:T(4,128)S(1)} %fusion.37.count_ref, f32[4,1024]{1,0:T(4,128)S(1)} %fusion.30.ratio_ref, bf16[256,2048]{1,0:T(8,128)(2,1)S(1)} %bitcast.245, bf16[2,256,2048]{2,1,0:T(8,128)(2,1)S(1)} %copy-done.30, ...), custom_call_target="tpu_custom_call" | custom-call | flops 1 | bytes 1 | tf_op jit(solution)/shard_map/mixed/pallas_call | solution.py:1179
  448.7 3.6 collective-permute-done.48
  468.6 3.4 fusion.11
  472.1 6.7 %collective-permute-done.51 = bf16[64,1536]{0,1:T(8,128)(2,1)S(1)} collective-permute-done((bf16[64,1536]{0,1:T(8,128)(2,1)S(1)}, bf16[64,1536]{0,1:T(8,128)(2,1)S(1)}, u32[]{:S(2)}, u32[]{:S(2)}) %collective-permute-start.51) | collective-permute-done | bytes 196640 | tf_op jit(solution)/shard_map/ppermute | solution.py:47
  478.8 4.9 collective-permute-done.52
  (488 shorter events, 178.2 us)
Async XLA Ops:
  7.2 57.4 %all-gather.11.cloned.1.call-start = ((), (), s32[]{:S(2)}) async-start(), calls=%async_computation.1 | async-start | bytes 1638400 | tf_op jit(solution)/shard_map/all_gather | solution.py:919
  30.4 66.7 %all-gather.9.cloned.1.call-start = ((), (), s32[]{:S(2)}) async-start(), calls=%async_computation | async-start | bytes 1310720 | tf_op jit(solution)/shard_map/all_gather | solution.py:919
  34.2 106.5 %all-gather.13.cloned.1.call-start = ((), (), s32[]{:S(2)}) async-start(), calls=%async_computation.2 | async-start | bytes 2621440 | tf_op jit(solution)/shard_map/all_gather | solution.py:919
  64.6 193.8 %all-gather.15.cloned.1.call-start = ((), (), s32[]{:S(2)}) async-start(), calls=%async_computation.3 | async-start | bytes 5242880 | tf_op jit(solution)/shard_map/all_gather | solution.py:919
  65.3 24.4 %collective-permute-start.8 = (bf16[256,2048]{1,0:T(8,128)(2,1)S(1)}, bf16[256,2048]{1,0:T(8,128)(2,1)}, u32[]{:S(2)}, u32[]{:S(2)}) collective-permute-start(bf16[256,2048]{1,0:T(8,128)(2,1)S(1)} %fusion.2.refs_0_), channel_id=1, source_target_pairs={{0,8},{4,12},{8,0},{12,4},{1,9},{5,13},{9,1},{13,5},{2,10},{6,14},... | collective-permute-start | bytes 3145736 | tf_op jit(solution)/shard_map/ppermute | solution.py:47
  66.8 48.8 %collective-permute-start.6 = (bf16[2,256,2048]{2,1,0:T(8,128)(2,1)}, bf16[2,256,2048]{2,1,0:T(8,128)(2,1)}, u32[]{:S(2)}, u32[]{:S(2)}) collective-permute-start(bf16[2,256,2048]{2,1,0:T(8,128)(2,1)} %get-tuple-element.149), channel_id=1, source_target_pairs={{0,4},{4,0},{8,12},{12,8},{1,5},{5,1},{9,13},{13,9},{2,6},{6,2},{1... | collective-permute-start | bytes 6291464 | tf_op jit(solution)/shard_map/ppermute | solution.py:47
  66.8 48.8 %collective-permute-start.4 = (bf16[4,4,64,640]{3,2,1,0:T(8,128)(2,1)}, bf16[4,4,64,640]{3,2,1,0:T(8,128)(2,1)}, u32[]{:S(2)}, u32[]{:S(2)}) collective-permute-start(bf16[4,4,64,640]{3,2,1,0:T(8,128)(2,1)} %bitcast.20.refs_0_), channel_id=1, source_target_pairs={{0,16},{16,0},{1,17},{17,1},{2,18},{18,2},{3,19},{19,3},{4,20},{20... | collective-permute-start | bytes 3932168 | tf_op jit(solution)/shard_map/ppermute | solution.py:47
  68.3 25.4 %collective-permute-start.7 = (bf16[256,2048]{1,0:T(8,128)(2,1)S(1)}, bf16[256,2048]{1,0:T(8,128)(2,1)}, u32[]{:S(2)}, u32[]{:S(2)}) collective-permute-start(bf16[256,2048]{1,0:T(8,128)(2,1)S(1)} %fusion.2.refs_0_), channel_id=1, source_target_pairs={{0,4},{4,0},{8,12},{12,8},{1,5},{5,1},{9,13},{13,9},{2,6},{6,2},{1... | collective-permute-start | bytes 3145736 | tf_op jit(solution)/shard_map/ppermute | solution.py:47
  89.7 25.9 %collective-permute-start.5 = (bf16[256,2048]{1,0:T(8,128)(2,1)}, bf16[256,2048]{1,0:T(8,128)(2,1)}, u32[]{:S(2)}, u32[]{:S(2)}) collective-permute-start(bf16[256,2048]{1,0:T(8,128)(2,1)} %get-tuple-element.147), channel_id=1, source_target_pairs={{0,8},{4,12},{8,0},{12,4},{1,9},{5,13},{9,1},{13,5},{2,10},{6,14},... | collective-permute-start | bytes 3145736 | tf_op jit(solution)/shard_map/ppermute | solution.py:47
  93.7 71.1 %collective-permute-start.13 = (bf16[2,256,2048]{2,1,0:T(8,128)(2,1)}, bf16[2,256,2048]{2,1,0:T(8,128)(2,1)}, u32[]{:S(2)}, u32[]{:S(2)}) collective-permute-start(bf16[2,256,2048]{2,1,0:T(8,128)(2,1)} %get-tuple-element.165), channel_id=1, source_target_pairs={{0,4},{4,0},{1,5},{5,1},{2,6},{6,2},{3,7},{7,3},{16,20},{20,16},{1... | collective-permute-start | bytes 6291464 | tf_op jit(solution)/shard_map/ppermute | solution.py:47
  115.6 41.7 %collective-permute-start.10 = (bf16[4,4,64,512]{3,2,1,0:T(8,128)(2,1)}, bf16[4,4,64,512]{3,2,1,0:T(8,128)(2,1)}, u32[]{:S(2)}, u32[]{:S(2)}) collective-permute-start(bf16[4,4,64,512]{3,2,1,0:T(8,128)(2,1)} %bitcast.255), channel_id=1, source_target_pairs={{0,16},{16,0},{1,17},{17,1},{2,18},{18,2},{3,19},{19,3},{4,20},{20... | collective-permute-start | bytes 3145736 | tf_op jit(solution)/shard_map/ppermute | solution.py:47
  164.9 48.1 %collective-permute-start.17 = (bf16[4,4,64,1024]{3,2,1,0:T(8,128)(2,1)}, bf16[4,4,64,1024]{3,2,1,0:T(8,128)(2,1)}, u32[]{:S(2)}, u32[]{:S(2)}) collective-permute-start(bf16[4,4,64,1024]{3,2,1,0:T(8,128)(2,1)} %bitcast.60.refs_0_), channel_id=1, source_target_pairs={{0,16},{16,0},{1,17},{17,1},{2,18},{18,2},{3,19},{19,3},{4,20},{20... | collective-permute-start | bytes 6291464 | tf_op jit(solution)/shard_map/ppermute | solution.py:47
  166.4 26.4 %collective-permute-start.16 = (bf16[256,2048]{1,0:T(8,128)(2,1)}, bf16[256,2048]{1,0:T(8,128)(2,1)}, u32[]{:S(2)}, u32[]{:S(2)}) collective-permute-start(bf16[256,2048]{1,0:T(8,128)(2,1)} %get-tuple-element.174), channel_id=1, source_target_pairs={{0,8},{4,12},{8,0},{12,4},{1,9},{5,13},{9,1},{13,5},{2,10},{6,14},... | collective-permute-start | bytes 3145736 | tf_op jit(solution)/shard_map/ppermute | solution.py:47
  170.0 57.8 %collective-permute-start.18 = (bf16[256,2048]{1,0:T(8,128)(2,1)S(1)}, bf16[256,2048]{1,0:T(8,128)(2,1)}, u32[]{:S(2)}, u32[]{:S(2)}) collective-permute-start(bf16[256,2048]{1,0:T(8,128)(2,1)S(1)} %copy-done.59), channel_id=1, source_target_pairs={{8,0},{12,4},{9,1},{13,5},{10,2},{14,6},{11,3},{15,7},{24,16},{28,... | collective-permute-start | bytes 3145736 | tf_op jit(solution)/shard_map/ppermute | solution.py:47
  192.7 44.4 %collective-permute-start.22 = (bf16[256,2048]{1,0:T(8,128)(2,1)}, bf16[256,2048]{1,0:T(8,128)(2,1)S(1)}, u32[]{:S(2)}, u32[]{:S(2)}) collective-permute-start(bf16[256,2048]{1,0:T(8,128)(2,1)} %get-tuple-element.186), channel_id=1, source_target_pairs={{8,0},{12,4},{9,1},{13,5},{10,2},{14,6},{11,3},{15,7},{24,16},{28,... | collective-permute-start | bytes 3145736 | tf_op jit(solution)/shard_map/ppermute | solution.py:47
  257.8 25.5 %collective-permute-start.29 = (bf16[256,2048]{1,0:T(8,128)(2,1)}, bf16[256,2048]{1,0:T(8,128)(2,1)}, u32[]{:S(2)}, u32[]{:S(2)}) collective-permute-start(bf16[256,2048]{1,0:T(8,128)(2,1)} %get-tuple-element.202), channel_id=1, source_target_pairs={{0,16},{16,0},{1,17},{17,1},{2,18},{18,2},{3,19},{19,3},{4,20},{20... | collective-permute-start | bytes 3145736 | tf_op jit(solution)/shard_map/ppermute | solution.py:47
  283.3 23.7 %collective-permute-start.31 = (bf16[2,256,2048]{2,1,0:T(8,128)(2,1)}, bf16[2,256,2048]{2,1,0:T(8,128)(2,1)}, u32[]{:S(2)}, u32[]{:S(2)}) collective-permute-start(bf16[2,256,2048]{2,1,0:T(8,128)(2,1)} %get-tuple-element.209), channel_id=1, source_target_pairs={{0,4},{4,0},{8,12},{12,8},{1,5},{5,1},{9,13},{13,9},{2,6},{6,2},{1... | collective-permute-start | bytes 6291464 | tf_op jit(solution)/shard_map/ppermute | solution.py:47
  283.3 26.3 %collective-permute-start.30 = (bf16[256,2048]{1,0:T(8,128)(2,1)}, bf16[256,2048]{1,0:T(8,128)(2,1)}, u32[]{:S(2)}, u32[]{:S(2)}) collective-permute-start(bf16[256,2048]{1,0:T(8,128)(2,1)} %copy-done.40), channel_id=1, source_target_pairs={{0,16},{16,0},{1,17},{17,1},{2,18},{18,2},{3,19},{19,3},{4,20},{20... | collective-permute-start | bytes 3145736 | tf_op jit(solution)/shard_map/ppermute | solution.py:47
  283.9 68.2 %collective-permute-start.33 = (bf16[2,256,2048]{2,1,0:T(8,128)(2,1)}, bf16[2,256,2048]{2,1,0:T(8,128)(2,1)}, u32[]{:S(2)}, u32[]{:S(2)}) collective-permute-start(bf16[2,256,2048]{2,1,0:T(8,128)(2,1)} %get-tuple-element.218), channel_id=1, source_target_pairs={{0,8},{4,12},{8,0},{12,4},{1,9},{5,13},{9,1},{13,5},{2,10},{6,14},... | collective-permute-start | bytes 6291464 | tf_op jit(solution)/shard_map/ppermute | solution.py:47
  304.0 56.6 %collective-permute-start.37 = (bf16[4,256,1024]{2,1,0:T(8,128)(2,1)}, bf16[4,256,1024]{2,1,0:T(8,128)(2,1)}, u32[]{:S(2)}, u32[]{:S(2)}) collective-permute-start(bf16[4,256,1024]{2,1,0:T(8,128)(2,1)} %bitcast.69), channel_id=1, source_target_pairs={{0,16},{16,0},{1,17},{17,1},{2,18},{18,2},{3,19},{19,3},{4,20},{20... | collective-permute-start | bytes 6291464 | tf_op jit(solution)/shard_map/ppermute | solution.py:47
  307.0 46.6 %collective-permute-start.34 = (bf16[1,256,2048]{2,1,0:T(8,128)(2,1)}, bf16[1,256,2048]{2,1,0:T(8,128)(2,1)S(1)}, u32[]{:S(2)}, u32[]{:S(2)}) collective-permute-start(bf16[1,256,2048]{2,1,0:T(8,128)(2,1)} %get-tuple-element.220), channel_id=1, source_target_pairs={{0,12},{4,8},{8,4},{12,0},{1,13},{5,9},{9,5},{13,1},{2,14},{6,10},... | collective-permute-start | bytes 3145736 | tf_op jit(solution)/shard_map/ppermute | solution.py:47
  314.3 39.4 %collective-permute-start.32 = (bf16[2,128,2048]{2,1,0:T(8,128)(2,1)}, bf16[2,128,2048]{2,1,0:T(8,128)(2,1)}, u32[]{:S(2)}, u32[]{:S(2)}) collective-permute-start(bf16[2,128,2048]{2,1,0:T(8,128)(2,1)} %pad_maximum_fusion.11), channel_id=1, source_target_pairs={{0,1},{1,0},{2,3},{3,2},{4,5},{5,4},{6,7},{7,6},{8,9},{9,8},{10,11... | collective-permute-start | bytes 3145736 | tf_op jit(solution)/shard_map/ppermute | solution.py:47
  365.2 39.4 %collective-permute-start.38 = (bf16[2,256,1024]{2,1,0:T(8,128)(2,1)}, bf16[2,256,1024]{2,1,0:T(8,128)(2,1)}, u32[]{:S(2)}, u32[]{:S(2)}) collective-permute-start(bf16[2,256,1024]{2,1,0:T(8,128)(2,1)} %pad_maximum_fusion.12), channel_id=1, source_target_pairs={{0,1},{1,0},{2,3},{3,2},{4,5},{5,4},{6,7},{7,6},{8,9},{9,8},{10,11... | collective-permute-start | bytes 3145736 | tf_op jit(solution)/shard_map/ppermute | solution.py:47
  370.1 34.4 %collective-permute-start.40 = (bf16[1,128,2048]{2,1,0:T(8,128)(2,1)}, bf16[1,128,2048]{2,1,0:T(8,128)(2,1)}, u32[]{:S(2)}, u32[]{:S(2)}) collective-permute-start(bf16[1,128,2048]{2,1,0:T(8,128)(2,1)} %get-tuple-element.399), channel_id=1, source_target_pairs={{0,2},{1,3},{2,0},{3,1},{4,6},{5,7},{6,4},{7,5},{8,10},{9,11},{10,... | collective-permute-start | bytes 1572872 | tf_op jit(solution)/shard_map/ppermute | solution.py:47
  375.1 29.4 %collective-permute-start.39 = (bf16[4,256,512]{2,1,0:T(8,128)(2,1)}, bf16[4,256,512]{2,1,0:T(8,128)(2,1)}, u32[]{:S(2)}, u32[]{:S(2)}) collective-permute-start(bf16[4,256,512]{2,1,0:T(8,128)(2,1)} %bitcast.73), channel_id=1, source_target_pairs={{0,16},{16,0},{1,17},{17,1},{2,18},{18,2},{3,19},{19,3},{4,20},{20... | collective-permute-start | bytes 3145736 | tf_op jit(solution)/shard_map/ppermute | solution.py:47
  395.7 24.4 %collective-permute-start.42 = (bf16[2,256,2048]{2,1,0:T(8,128)(2,1)}, bf16[2,256,2048]{2,1,0:T(8,128)(2,1)}, u32[]{:S(2)}, u32[]{:S(2)}) collective-permute-start(bf16[2,256,2048]{2,1,0:T(8,128)(2,1)} %pad_maximum_fusion.1), channel_id=1, source_target_pairs={{0,4},{4,0},{8,12},{12,8},{1,5},{5,1},{9,13},{13,9},{2,6},{6,2},{1... | collective-permute-start | bytes 6291464 | tf_op jit(solution)/shard_map/ppermute | solution.py:47
  401.7 38.1 %collective-permute-start.45 = (bf16[1,256,2048]{2,1,0:T(8,128)(2,1)}, bf16[1,256,2048]{2,1,0:T(8,128)(2,1)}, u32[]{:S(2)}, u32[]{:S(2)}) collective-permute-start(bf16[1,256,2048]{2,1,0:T(8,128)(2,1)} %get-tuple-element.246), channel_id=1, source_target_pairs={{0,12},{4,8},{8,4},{12,0},{1,13},{5,9},{9,5},{13,1},{2,14},{6,10},... | collective-permute-start | bytes 3145736 | tf_op jit(solution)/shard_map/ppermute | solution.py:47
  404.5 30.8 %collective-permute-start.41 = (bf16[4,256,640]{2,1,0:T(8,128)(2,1)S(1)}, bf16[4,256,640]{2,1,0:T(8,128)(2,1)S(1)}, u32[]{:S(2)}, u32[]{:S(2)}) collective-permute-start(bf16[4,256,640]{2,1,0:T(8,128)(2,1)S(1)} %pad_maximum_fusion.3), channel_id=1, source_target_pairs={{0,16},{16,0},{1,17},{17,1},{2,18},{18,2},{3,19},{19,3},{4,20},{20... | collective-permute-start | bytes 3932168 | tf_op jit(solution)/shard_map/ppermute | solution.py:47
  412.3 22.4 %collective-permute-start.43 = (bf16[2,256,512]{2,1,0:T(8,128)(2,1)S(1)}, bf16[2,256,512]{2,1,0:T(8,128)(2,1)S(1)}, u32[]{:S(2)}, u32[]{:S(2)}) collective-permute-start(bf16[2,256,512]{2,1,0:T(8,128)(2,1)S(1)} %pad_maximum_fusion.15), channel_id=1, source_target_pairs={{0,1},{1,0},{2,3},{3,2},{4,5},{5,4},{6,7},{7,6},{8,9},{9,8},{10,11... | collective-permute-start | bytes 1572872 | tf_op jit(solution)/shard_map/ppermute | solution.py:47
  415.4 33.2 %collective-permute-start.47 = (bf16[1,256,1024]{2,1,0:T(8,128)(2,1)S(1)}, bf16[1,256,1024]{2,1,0:T(8,128)(2,1)S(1)}, u32[]{:S(2)}, u32[]{:S(2)}) collective-permute-start(bf16[1,256,1024]{2,1,0:T(8,128)(2,1)S(1)} %get-tuple-element.397), channel_id=1, source_target_pairs={{0,2},{1,3},{2,0},{3,1},{4,6},{5,7},{6,4},{7,5},{8,10},{9,11},{10,... | collective-permute-start | bytes 1572872 | tf_op jit(solution)/shard_map/ppermute | solution.py:47
  423.1 39.0 %collective-permute-start.46 = (bf16[256,2048]{1,0:T(8,128)(2,1)}, bf16[256,2048]{1,0:T(8,128)(2,1)S(1)}, u32[]{:S(2)}, u32[]{:S(2)}) collective-permute-start(bf16[256,2048]{1,0:T(8,128)(2,1)} %fusion.10), channel_id=1, source_target_pairs={{0,8},{4,12},{8,0},{12,4},{1,9},{5,13},{9,1},{13,5},{2,10},{6,14},... | collective-permute-start | bytes 3145736 | tf_op jit(solution)/shard_map/ppermute | solution.py:47
  438.6 23.5 %collective-permute-start.44 = (bf16[2,256,640]{2,1,0:T(8,128)(2,1)}, bf16[2,256,640]{2,1,0:T(8,128)(2,1)}, u32[]{:S(2)}, u32[]{:S(2)}) collective-permute-start(bf16[2,256,640]{2,1,0:T(8,128)(2,1)} %pad_maximum_fusion.13), channel_id=1, source_target_pairs={{0,1},{1,0},{2,3},{3,2},{4,5},{5,4},{6,7},{7,6},{8,9},{9,8},{10,11... | collective-permute-start | bytes 1966088 | tf_op jit(solution)/shard_map/ppermute | solution.py:47
  (111 other events, 1002.3 us)
Sparse Core Ops, SparseCore 0:
  30.5 34.0 all-gather.10
  66.7 26.9 all-gather.8
  95.2 45.4 all-gather.12
  142.7 79.4 all-gather.14

commit v3 on v2

--- a/solution.py
+++ b/solution.py
@@ -314,16 +314,25 @@
     return (a >= b) if rows_first else (a <= b)
 
 
-def pair_of(lo, cols, p):
-    return jnp.where(lo, cols[:, 2 * p : 2 * p + 1], cols[:, 2 * p + 1 : 2 * p + 2])
-
-
 def decays(segc, segr, segp, dt, rate):
     cum = dot(tri(True).astype(F32), dt * rate, precision=HIGH)
     last = cum[SPAN - 1 : SPAN, :]
     keep = jnp.where(segc == segp, jnp.exp(cum), 0.0)
     to_end = jnp.where(segc == segr[:, SPAN - 1 : SPAN], jnp.exp(last - cum), 0.0)
     return cum, cum.T, keep, to_end
+
+
+def expanded(columns, ones):
+    high = columns.astype(BF)
+    low = (columns - high.astype(F32)).astype(BF)
+    return dot(high, ones) + dot(low, ones)
+
+
+def head_of_channel(width):
+    return (
+        lax.broadcasted_iota(jnp.int32, (LANES, width), 1) // HEADDIM
+        == lax.broadcasted_iota(jnp.int32, (LANES, width), 0)
+    ).astype(BF)
 
 
 def spread_columns(ref, first, count):
@@ -362,6 +371,9 @@
     carry,
     to_end_u,
     ext,
+    wide_dt,
+    wide_keep,
+    wide_end,
 ):
     block = pl.program_id(0)
     width = heads * HEADDIM
@@ -381,27 +393,27 @@
     bm, cm = b_ref[...], c_ref[...]
     mixing = dot(cm, bm, ((1,), (1,)))
     mixing = jnp.where(tri(True) & (segc == segr), mixing, 0.0)
+    heads_ones = head_of_channel(width)
+    wide_dt[...] = expanded(dt, heads_ones)
+    wide_keep[...] = expanded(keep, heads_ones)
+    wide_end[...] = expanded(to_end, heads_ones)
     masks = spread_columns(mask_ref, 0, CONV - 1)
     lo = lax.broadcasted_iota(jnp.int32, (SPAN, LANES), 1) < HEADDIM
     for p in range(heads // 2):
         at = slice(p * LANES, (p + 1) * LANES)
         pre = convolved(taps(ext, masks, at), weight_ref, at)
         x2 = pre * jax.nn.sigmoid(pre)
-        u2 = x2 * pair_of(lo, dt, p)
+        u2 = x2 * wide_dt[:, at]
         ub = u2.astype(BF)
-        total = dot(cm, carry[:, at].astype(BF)) * pair_of(lo, keep, p) + skip_ref[:, at] * x2
+        total = dot(cm, carry[:, at].astype(BF)) * wide_keep[:, at] + skip_ref[:, at] * x2
         inner = []
         for h in (2 * p, 2 * p + 1):
             decay = jnp.exp(jnp.minimum(cum[:, h : h + 1] - cumr[h : h + 1, :], 0.0))
             inner.append(dot((decay * mixing).astype(BF), ub))
         y_ref[:, at] = total + jnp.where(lo, inner[0], inner[1])
-        to_end_u[:, at] = (u2 * pair_of(lo, to_end, p)).astype(BF)
+        to_end_u[:, at] = (u2 * wide_end[:, at]).astype(BF)
     fresh = dot(bm, to_end_u[...], ((0,), (0,)))
-    lo_row = lax.broadcasted_iota(jnp.int32, (1, LANES), 1) < HEADDIM
-    for p in range(heads // 2):
-        at = slice(p * LANES, (p + 1) * LANES)
-        factor = pair_of(lo_row, keep[SPAN - 1 : SPAN, :], p)
-        carry[:, at] = factor * carry[:, at] + fresh[:, at]
+    carry[...] = wide_keep[SPAN - 1 : SPAN, :] * carry[...] + fresh
 
 
 def split_dot(value, ones):
@@ -441,6 +453,9 @@
     along,
     ext,
     dext,
+    wide_dt,
+    wide_keep,
+    wide_end,
 ):
     step = pl.program_id(0)
     block = pl.num_programs(0) - 1 - step
@@ -463,6 +478,10 @@
     bm, cm = b_ref[...], c_ref[...]
     allowed = tri(False) & (segc == segr)
     mixing = jnp.where(allowed, dot(bm, cm, ((1,), (1,))), 0.0)
+    heads_ones = head_of_channel(heads * HEADDIM)
+    wide_dt[...] = expanded(dt, heads_ones)
+    wide_keep[...] = expanded(keep, heads_ones)
+    wide_end[...] = expanded(to_end, heads_ones)
     masks = spread_columns(mask_ref, 0, CONV - 1)
     moved = spread_columns(mask_ref, CONV - 1, CONV - 1)
     lo = lax.broadcasted_iota(jnp.int32, (SPAN, LANES), 1) < HEADDIM
@@ -473,12 +492,12 @@
         pre = convolved(terms, weight_ref, at)
         sig = jax.nn.sigmoid(pre)
         x2 = pre * sig
-        dt2 = pair_of(lo, dt, p)
+        dt2 = wide_dt[:, at]
         u2 = x2 * dt2
         dyb = dy_ref[:, at]
         dy2 = dyb.astype(F32)
         skip = skip_ref[:, at]
-        te2 = pair_of(lo, to_end, p)
+        te2 = wide_end[:, at]
         u_sides = (jnp.where(lo, u2, 0.0).astype(BF), jnp.where(lo, 0.0, u2).astype(BF))
         du = te2 * dot(bm, dcarry[:, at].astype(BF))
         inner = []
@@ -488,7 +507,7 @@
             inner.append(dot((decay * mixing).astype(BF), dyb))
             dmixing = dmixing + decay * dot(u_sides[k], dyb, ((1,), (1,)))
         du = du + jnp.where(lo, inner[0], inner[1])
-        keep_dy[:, at] = (pair_of(lo, keep, p) * dy2).astype(BF)
+        keep_dy[:, at] = (wide_keep[:, at] * dy2).astype(BF)
         to_end_u[:, at] = (te2 * u2).astype(BF)
         slopes[:, at] = dy2 * (y_ref[:, at] - skip * x2) - u2.astype(BF).astype(F32) * du
         along[:, at] = x2 * du
@@ -523,11 +542,7 @@
     ddt_ref[...] = rate_ref[...] * da + split_dot(along[...], ones)
     drate_ref[...] += jnp.sum(dt * da, axis=0, keepdims=True)
     fresh = dot(cm, keep_dy[...], ((0,), (0,)))
-    lo_row = lax.broadcasted_iota(jnp.int32, (1, LANES), 1) < HEADDIM
-    for p in range(heads // 2):
-        at = slice(p * LANES, (p + 1) * LANES)
-        factor = pair_of(lo_row, keep[SPAN - 1 : SPAN, :], p)
-        dcarry[:, at] = factor * dcarry[:, at] + fresh[:, at]
+    dcarry[...] = wide_keep[SPAN - 1 : SPAN, :] * dcarry[...] + fresh
     after_state[...] = prior
 
 
@@ -575,6 +590,9 @@
             pltpu.VMEM((STATE, width), F32),
             pltpu.VMEM((SPAN, width), BF),
             pltpu.VMEM((HALO + SPAN, width), F32),
+            pltpu.VMEM((SPAN, width), F32),
+            pltpu.VMEM((SPAN, width), F32),
+            pltpu.VMEM((SPAN, width), F32),
         ],
         name="scan_forward",
     )(*operands)
@@ -606,6 +624,9 @@
             pltpu.VMEM((SPAN, width), F32),
             pltpu.VMEM((HALO + SPAN, width), F32),
             pltpu.VMEM((SPAN + HALO, width), F32),
+            pltpu.VMEM((SPAN, width), F32),
+            pltpu.VMEM((SPAN, width), F32),
+            pltpu.VMEM((SPAN, width), F32),
         ],
         name="scan_backward",
     )(*operands, y, priors, dy)
@@ -930,7 +951,7 @@
     held_a = over_fsdp(mine[:, :, :first])
     held_b = over_fsdp(mine[:, :, first:cols])
     other_out = [swapped(w_out, "dp", j) for j in range(1, nd)]
-    held_a, other_out = together(held_a, other_out)
+    held_a, other_out, xn_pieces[2] = together(held_a, other_out, xn_pieces[2])
     small_ones = (seg, seg_before, mask_cols, weight_s, weight_r, bias_r, bias, rate, skip_own, gain, theirs)
     held_a, small_ones, halves, singles = together(held_a, small_ones, halves, singles)
     seg, seg_before, mask_cols, weight_s, weight_r, bias_r, bias, rate, skip_own, gain, theirs = small_ones
@@ -946,7 +967,7 @@
     far3 = far(3, chip3)
     pieces_b = over_dp(held_b)
     held_z = over_fsdp(after(mine_z, held_a))
-    held_out = over_fsdp(after(jnp.stack([w_out] + other_out), held_z))
+    pair_out = jnp.stack([w_out] + other_out)
 
     xn_turned = xn.T
     here = jnp.stack([s, d]).astype(jnp.int32)
@@ -971,6 +992,7 @@
     proj_b = dot(xn, after(full_b, proj_a, xn_turned, bc[2])).astype(BF)
     proj_b, far3, near_low, held_z = together(proj_b, far3, near_low, held_z)
     pieces_z = over_dp(held_z)
+    held_out = over_fsdp(after(pair_out, proj_b))
     bc = reordered_by_xor(bc, s)
     b_in = jnp.concatenate(bc[: ns // 2], axis=1)
     c_out = jnp.concatenate(bc[ns // 2 :], axis=1)
@@ -1141,18 +1163,19 @@
         padded(pre_dt),
     )
 
-    dxn = input_grad(dz, dproj_s, dproj_r, full_z, full_a, full_b, ns, tok)
-    pair = swapped(jnp.stack([picked(dxn, s ^ 1), picked(dxn, s ^ 3)]), "seq", 1)
-
-    late_s, late_r = together(dproj_s, after(dproj_r, dxn))
+    late_s, late_r = after(dproj_s, *left_other), dproj_r
     right_other = [
         jnp.concatenate([in_terms(late_s, d ^ k, half, half), in_terms(late_r, d ^ k)], axis=2)
         for k in range(1, nd)
     ]
-    right_other, z_half, left_got, out_pair = together(right_other, z_half, left_got, out_pair)
     right_got = dp_terms(right_other)
+
+    dxn = input_grad(dz, dproj_s, after(dproj_r, *right_other), full_z, full_a, full_b, ns, tok)
+    pair = swapped(jnp.stack([picked(dxn, s ^ 1), picked(dxn, s ^ 3)]), "seq", 1)
+
+    dxn, z_half, left_got, out_pair = together(dxn, z_half, left_got, out_pair)
     z_pair = fsdp_rest(z_kept, z_half)
-    own_s = in_terms(after(dproj_s, *right_other), d)
+    own_s = in_terms(after(dproj_s, dxn), d)
     left_kept, left_sent = fsdp_half(own_s[:, :, :half], left_got)
     left_half = swapped(left_sent, "fsdp", 1)
     own_r = in_terms(after(dproj_r, left_sent), d)

time: 521 us -> 501 us (0.962)
  waiting for transfers between devices: 152 us -> 129 us
    ppermute x62, waiting for transfers between devices: 118 us -> 86.5 us  [swapped(): return lax.ppermute(value, axis, pairs)]
    all_gather x4, waiting for transfers between devices: 33.8 us -> 42 us  [over_fsdp(): return lax.all_gather(chunk, 'fsdp', axis=0, tiled=False)]
    unnamed x157 -> x161, local copies, waits for them, and re-layouts: 21.3 us -> 21.4 us
  transfers between devices with their start and end apart: 66 -> 66, of which waited for: 22 -> 23; matrix products, arithmetic and copies ran while one was open for 18% -> 19% of each run, Pallas kernels for 32% -> 32%
where the time goes in v3:
time: 501 us; the launch traced here: 494 us
  Pallas kernels  164 us (33%)
  waiting for transfers between devices  129 us (26%)
  local copies, waits for them, and re-layouts  64.7 us (13%)
  starting transfers between devices  56.4 us (11%)
  other arithmetic  55.6 us (11%)
  between operations  15.6 us (3%)
  matrix products  8.91 us (2%)
    ppermute x62, waiting for transfers between devices, swapped(): return lax.ppermute(value, axis, pairs)  86.5 us
    ppermute x62, starting transfers between devices, swapped(): return lax.ppermute(value, axis, pairs)  56.2 us
    all_gather x4, waiting for transfers between devices, over_fsdp(): return lax.all_gather(chunk, 'fsdp', axis=0, tiled=False)  42 us
    pallas_call x1, Pallas kernels, scan_backward(): call(functools.partial(backward_kernel, heads), grid=(blocks,), in_specs=...  34.2 us
    pallas_call x7, Pallas kernels, row_terms(): call(functools.partial(terms_kernel, ns, nf), grid_spec=pltpu.PrefetchSca...  24.9 us
    unnamed x161, local copies, waits for them, and re-layouts  21.4 us
    pallas_call x1, Pallas kernels, shards(): call(functools.partial(products_kernel, where, plan, lanes, tok, ns, nd),...  16.4 us
    pallas_call x1, Pallas kernels, scan_forward(): call(functools.partial(forward_kernel, heads), grid=(blocks,), in_specs=i...  14.9 us
  transfers between devices with their start and end apart: 66, of which 23 were waited for; matrix products, arithmetic and copies ran while one was open for 19% of the time, Pallas kernels for 32%

profile of v3, /device:TPU:0, one launch (start us, length us, event | category | flops | bytes accessed | tf_op | source)
XLA Modules:
  0.0 493.8 jit_solution(378042718522289394)
XLA Ops:
  24.2 5.6 %collective-permute-done.2.refs_3_ = bf16[64,2176]{1,0:T(8,128)(2,1)S(1)} collective-permute-done((bf16[64,2176]{1,0:T(8,128)(2,1)}, bf16[64,2176]{1,0:T(8,128)(2,1)S(1)}, u32[]{:S(2)}, u32[]{:S(2)}) %collective-permute-start.2) | collective-permute-done | bytes 278560 | tf_op jit(solution)/shard_map/ppermute | solution.py:47
  34.1 4.8 slice_bitcast_fusion
  39.8 4.5 slice_bitcast_fusion.2
  44.3 8.3 %collective-permute-done.4.refs_2_ = bf16[256,2048]{1,0:T(8,128)(2,1)} collective-permute-done((bf16[256,2048]{1,0:T(8,128)(2,1)}, bf16[256,2048]{1,0:T(8,128)(2,1)}, u32[]{:S(2)}, u32[]{:S(2)}) %collective-permute-start.4) | collective-permute-done | bytes 1048608 | tf_op jit(solution)/shard_map/ppermute | solution.py:47
  52.6 13.6 %all-gather.11.cloned.1.call-done = bf16[16,64,640]{2,1,0:T(8,128)(2,1)} async-done(((bf16[4,64,640]{2,1,0:T(8,128)(2,1)}), bf16[16,64,640]{2,1,0:T(8,128)(2,1)}) %all-gather.11.cloned.1.call-update) | async-done | bytes 1310736 | tf_op jit(solution)/shard_map/all_gather | solution.py:940
  74.7 20.0 %all-gather.9.cloned.1.call-done = bf16[16,64,512]{2,1,0:T(8,128)(2,1)} async-done(((bf16[4,64,512]{2,1,0:T(8,128)(2,1)}), bf16[16,64,512]{2,1,0:T(8,128)(2,1)}) %all-gather.9.cloned.1.call-update) | async-done | bytes 1048592 | tf_op jit(solution)/shard_map/all_gather | solution.py:940
  102.1 5.8 %filled.5 = bf16[4,256,2048]{2,1,0:T(8,128)(2,1)} custom-call(s32[4,3]{1,0:T(4,128)S(1)} %pad_add_fusion.index_ref, bf16[256,2048]{1,0:T(8,128)(2,1)} %fusion.2.refs_0_, bf16[256,2048]{1,0:T(8,128)(2,1)} %collective-permute-done.8.refs_1_, bf16[256,2048]{1,0:T(8,128)(2,1)} %collective-permute-done.4.refs_2_, bf16[256,2048]{1,0:T(8,128)(2,1)} %collective-permute-done.9.refs_3_), custom_call_target="tpu_custom_call" | custom-call | flops 1 | bytes 1 | tf_op jit(solution)/shard_map/filled/pallas_call | solution.py:116
  107.9 5.6 %convolution_convert_fusion.in_a_ref = bf16[1024,640]{1,0:T(8,128)(2,1)S(1)} fusion(bf16[1024,2048]{1,0:T(8,128)(2,1)} %bitcast.267, bf16[2048,640]{1,0:T(8,128)(2,1)S(1)} %bitcast.246), kind=kOutput, calls=%fused_computation.36 | convolution fusion | flops 2685009920 | bytes 8126464 | tf_op jit(solution)/shard_map/dot_general | solution.py:31
  119.5 6.4 %copy.203 = bf16[1024,2048]{0,1:T(8,128)(2,1)} copy(bf16[1024,2048]{1,0:T(8,128)(2,1)} %bitcast.268) | data formatting | bytes 8388608 | tf_op jit(solution)/shard_map/reshape | solution.py:965
  133.4 8.3 %all-gather.13.cloned.1.call-done = bf16[16,64,1024]{2,1,0:T(8,128)(2,1)} async-done(((bf16[4,64,1024]{2,1,0:T(8,128)(2,1)}), bf16[16,64,1024]{2,1,0:T(8,128)(2,1)}) %all-gather.13.cloned.1.call-update) | async-done | bytes 2097168 | tf_op jit(solution)/shard_map/all_gather | solution.py:940
  150.9 14.9 %scan_forward.1 = (f32[1024,1024]{1,0:T(8,128)}, f32[8,128,1024]{2,1,0:T(8,128)}) custom-call(s32[8]{0:T(128)S(1)} %pad_add_fusion.15.segp_ref, s32[1024,1]{1,0:T(8,128)S(1)} %copy-done.14, s32[1,1024]{1,0:T(1,128)S(1)} %bitcast.262, f32[1024,128]{1,0:T(8,128)S(1)} %pad.55.mask_ref, bf16[1024,640]{1,0:T(8,128)(2,1)S(1)} %convolution_convert_fusion.in_a_ref, ...), custom_call_target="tpu_custom_call" | custom-call | flops 1 | bytes 1 | tf_op jit(solution)/shard_map/scan_forward/pallas_call | solution.py:580
  165.9 3.9 collective-permute-done.16.refs_5_.refs_6_
  171.9 17.6 %collective-permute-done.17.refs_1_ = bf16[4,4,64,1024]{3,2,1,0:T(8,128)(2,1)} collective-permute-done((bf16[4,4,64,1024]{3,2,1,0:T(8,128)(2,1)}, bf16[4,4,64,1024]{3,2,1,0:T(8,128)(2,1)}, u32[]{:S(2)}, u32[]{:S(2)}) %collective-permute-start.17) | collective-permute-done | bytes 2097184 | tf_op jit(solution)/shard_map/ppermute | solution.py:47
  189.6 12.2 %gated.1 = (bf16[1024,1024]{1,0:T(8,128)(2,1)S(1)}, bf16[2048,1024]{1,0:T(8,128)(2,1)}, bf16[1024,1024]{1,0:T(8,128)(2,1)S(1)}, bf16[1024,1024]{1,0:T(8,128)(2,1)}, f32[8,1024]{1,0:T(8,128)S(1)}) custom-call(s32[2]{0:T(128)S(1)} %pad_add_fusion.16.here_ref, bf16[1024,2048]{1,0:T(8,128)(2,1)} %bitcast.269, f32[1024,1024]{1,0:T(8,128)} %get-tuple-element.176.y_ref, ...), custom_call_target="tpu_custom_call" | custom-call | flops 1 | bytes 1 | tf_op jit(solution)/shard_map/gated/pallas_call | solution.py:288
  208.9 4.7 collective-permute-done.20
  219.3 14.1 %upper.1 = (bf16[2,1024,2048]{2,1,0:T(8,128)(2,1)}, bf16[512,2048]{1,0:T(8,128)(2,1)}, bf16[256,2048]{1,0:T(8,128)(2,1)}, bf16[256,2048]{1,0:T(8,128)(2,1)S(1)}) custom-call(s32[2]{0:T(128)S(1)} %pad_add_fusion.16.here_ref, s32[2]{0:T(128)S(1)} %call_exported.0.range_ref, f32[2,4]{1,0:T(2,128)S(1)} %fusion.42.count_ref, f32[4,1024]{1,0:T(4,128)S(1)} %fusion.30.ratio_ref, ...), custom_call_target="tpu_custom_call" | custom-call | flops 1 | bytes 1 | tf_op jit(solution)/shard_map/upper/pallas_call | solution.py:1049
  236.2 16.4 %products.1 = (bf16[2,256,2048]{2,1,0:T(8,128)(2,1)}, bf16[2,256,2048]{2,1,0:T(8,128)(2,1)}, bf16[2,256,2048]{2,1,0:T(8,128)(2,1)}, bf16[2,256,2048]{2,1,0:T(8,1...) custom-call(s32[2]{0:T(128)S(1)} %pad_add_fusion.16.here_ref, f32[2,4]{1,0:T(2,128)S(1)} %fusion.42.count_ref, ...), custom_call_target="tpu_custom_call" | custom-call | flops 1 | bytes 1 | tf_op jit(solution)/shard_map/products/pallas_call | solution.py:1072
  256.6 3.5 collective-permute-done.29
  260.7 12.3 %gate_backward.1 = (bf16[1024,1024]{1,0:T(8,128)(2,1)S(1)}, bf16[1024,1024]{1,0:T(8,128)(2,1)S(1)}, f32[8,1024]{1,0:T(8,128)S(1)}) custom-call(f32[2,4]{1,0:T(2,128)S(1)} %fusion.42.count_ref, bf16[2,1024,2048]{2,1,0:T(8,128)(2,1)} %get-tuple-element.197.upper_ref, bf16[1024,2048]{1,0:T(8,128)(2,1)} %get-tuple-element.200.w_ref, ...), custom_call_target="tpu_custom_call" | custom-call | flops 1 | bytes 1 | tf_op jit(solution)/shard_map/gate_backward/pallas_call | solution.py:1098
  274.4 6.3 %row_terms.7 = bf16[4,4,64,1024]{3,2,1,0:T(8,128)(2,1)} custom-call(s32[1]{0:T(128)} %bitcast.49.at_ref, bf16[2048,1024]{1,0:T(8,128)(2,1)} %bitcast.238, bf16[1024,1024]{1,0:T(8,128)(2,1)S(1)} %get-tuple-element.224.right_ref.dz_ref), custom_call_target="tpu_custom_call" | custom-call | flops 1 | bytes 1 | tf_op jit(solution)/shard_map/row_terms/pallas_call | solution.py:145
  292.3 34.2 %scan_backward.1 = (bf16[1024,1024]{1,0:T(8,128)(2,1)}, f32[1024,256]{1,0:T(8,128)S(1)}, f32[1024,128]{1,0:T(8,128)S(1)}, f32[1,128]{1,0:T(1,128)S(1)}, f32[8,1024]{1,0:T(8,128)S(1)}) custom-call(s32[8]{0:T(128)S(1)} %pad_add_fusion.15.segp_ref, s32[1024,1]{1,0:T(8,128)S(1)} %copy-done.15, s32[1,1024]{1,0:T(1,128)S(1)} %bitcast.263, ...), custom_call_target="tpu_custom_call" | custom-call | flops 1 | bytes 1 | tf_op jit(solution)/shard_map/scan_backward/pallas_call | solution.py:606
  332.4 4.9 row_terms.8
  337.4 3.5 add_convert_fusion.7
  342.9 4.1 row_terms.9
  366.1 13.7 %input_grad.1 = bf16[4,256,2048]{2,1,0:T(8,128)(2,1)} custom-call(bf16[1024,1024]{1,0:T(8,128)(2,1)S(1)} %copy-done.8, bf16[1024,1024]{1,0:T(8,128)(2,1)S(1)} %copy-done.2, bf16[1024,128]{1,0:T(8,128)(2,1)S(1)} %get-tuple-element.238.right_ref.dr_ref, bf16[2048,1024]{1,0:T(8,128)(2,1)} %get-tuple-element.233.wz_ref, bf16[2048,640]{1,0:T(8,128)(2,1)} %bitcast.247, ...), custom_call_target="tpu_custom_call" | custom-call | flops 1 | bytes 1 | tf_op jit(solution)/shard_map/input_grad/pallas_call | solution.py:219
  385.2 4.9 row_terms.12
  402.9 11.1 %collective-permute-done.43 = bf16[2,256,512]{2,1,0:T(8,128)(2,1)S(1)} collective-permute-done((bf16[2,256,512]{2,1,0:T(8,128)(2,1)S(1)}, bf16[2,256,512]{2,1,0:T(8,128)(2,1)S(1)}, u32[]{:S(2)}, u32[]{:S(2)}) %collective-permute-start.43) | collective-permute-done | bytes 524320 | tf_op jit(solution)/shard_map/ppermute | solution.py:47
  419.6 7.8 %mixed.1 = bf16[4,256,2048]{2,1,0:T(8,128)(2,1)} custom-call(s32[2]{0:T(128)S(1)} %pad_add_fusion.16.here_ref, f32[4,8]{1,0:T(4,128)S(1)} %fusion.37.count_ref, f32[4,1024]{1,0:T(4,128)S(1)} %fusion.30.ratio_ref, bf16[256,2048]{1,0:T(8,128)(2,1)S(1)} %bitcast.245, bf16[2,256,2048]{2,1,0:T(8,128)(2,1)S(1)} %copy-done.33, ...), custom_call_target="tpu_custom_call" | custom-call | flops 1 | bytes 1 | tf_op jit(solution)/shard_map/mixed/pallas_call | solution.py:1202
  428.3 3.9 collective-permute-done.48
  449.0 3.4 fusion.11
  452.5 6.2 %collective-permute-done.51 = bf16[64,1536]{0,1:T(8,128)(2,1)S(1)} collective-permute-done((bf16[64,1536]{0,1:T(8,128)(2,1)S(1)}, bf16[64,1536]{0,1:T(8,128)(2,1)S(1)}, u32[]{:S(2)}, u32[]{:S(2)}) %collective-permute-start.51) | collective-permute-done | bytes 196640 | tf_op jit(solution)/shard_map/ppermute | solution.py:47
  458.7 4.2 collective-permute-done.52
  (492 shorter events, 187.2 us)
Async XLA Ops:
  7.2 59.0 %all-gather.11.cloned.1.call-start = ((), (), s32[]{:S(2)}) async-start(), calls=%async_computation.1 | async-start | bytes 1638400 | tf_op jit(solution)/shard_map/all_gather | solution.py:940
  18.3 34.3 %collective-permute-start.4 = (bf16[256,2048]{1,0:T(8,128)(2,1)}, bf16[256,2048]{1,0:T(8,128)(2,1)}, u32[]{:S(2)}, u32[]{:S(2)}) collective-permute-start(bf16[256,2048]{1,0:T(8,128)(2,1)} %fusion.2.refs_0_), channel_id=1, source_target_pairs={{0,8},{4,12},{8,0},{12,4},{1,9},{5,13},{9,1},{13,5},{2,10},{6,14},... | collective-permute-start | bytes 3145736 | tf_op jit(solution)/shard_map/ppermute | solution.py:47
  20.1 24.2 %collective-permute-start.3 = (bf16[128,2048]{1,0:T(8,128)(2,1)}, bf16[128,2048]{1,0:T(8,128)(2,1)}, u32[]{:S(2)}, u32[]{:S(2)}) collective-permute-start(bf16[128,2048]{1,0:T(8,128)(2,1)} %param.28), channel_id=1, source_target_pairs={{0,16},{16,0},{1,17},{17,1},{2,18},{18,2},{3,19},{19,3},{4,20},{20... | collective-permute-start | bytes 1572872 | tf_op jit(solution)/shard_map/ppermute | solution.py:47
  31.4 63.3 %all-gather.9.cloned.1.call-start = ((), (), s32[]{:S(2)}) async-start(), calls=%async_computation | async-start | bytes 1310720 | tf_op jit(solution)/shard_map/all_gather | solution.py:940
  39.7 102.1 %all-gather.13.cloned.1.call-start = ((), (), s32[]{:S(2)}) async-start(), calls=%async_computation.2 | async-start | bytes 2621440 | tf_op jit(solution)/shard_map/all_gather | solution.py:940
  66.2 31.5 %collective-permute-start.7 = (bf16[2,256,2048]{2,1,0:T(8,128)(2,1)}, bf16[2,256,2048]{2,1,0:T(8,128)(2,1)}, u32[]{:S(2)}, u32[]{:S(2)}) collective-permute-start(bf16[2,256,2048]{2,1,0:T(8,128)(2,1)} %get-tuple-element.149), channel_id=1, source_target_pairs={{0,4},{4,0},{8,12},{12,8},{1,5},{5,1},{9,13},{13,9},{2,6},{6,2},{1... | collective-permute-start | bytes 6291464 | tf_op jit(solution)/shard_map/ppermute | solution.py:47
  66.2 31.5 %collective-permute-start.5 = (bf16[4,4,64,640]{3,2,1,0:T(8,128)(2,1)}, bf16[4,4,64,640]{3,2,1,0:T(8,128)(2,1)}, u32[]{:S(2)}, u32[]{:S(2)}) collective-permute-start(bf16[4,4,64,640]{3,2,1,0:T(8,128)(2,1)} %bitcast.255), channel_id=1, source_target_pairs={{0,16},{16,0},{1,17},{17,1},{2,18},{18,2},{3,19},{19,3},{4,20},{20... | collective-permute-start | bytes 3932168 | tf_op jit(solution)/shard_map/ppermute | solution.py:47
  67.9 26.8 %collective-permute-start.9 = (bf16[256,2048]{1,0:T(8,128)(2,1)}, bf16[256,2048]{1,0:T(8,128)(2,1)}, u32[]{:S(2)}, u32[]{:S(2)}) collective-permute-start(bf16[256,2048]{1,0:T(8,128)(2,1)} %collective-permute-done.4.refs_2_), channel_id=1, source_target_pairs={{0,4},{4,0},{8,12},{12,8},{1,5},{5,1},{9,13},{13,9},{2,6},{6,2},{1... | collective-permute-start | bytes 3145736 | tf_op jit(solution)/shard_map/ppermute | solution.py:47
  68.2 26.6 %collective-permute-start.6 = (bf16[256,2048]{1,0:T(8,128)(2,1)}, bf16[256,2048]{1,0:T(8,128)(2,1)}, u32[]{:S(2)}, u32[]{:S(2)}) collective-permute-start(bf16[256,2048]{1,0:T(8,128)(2,1)} %get-tuple-element.147), channel_id=1, source_target_pairs={{0,8},{4,12},{8,0},{12,4},{1,9},{5,13},{9,1},{13,5},{2,10},{6,14},... | collective-permute-start | bytes 3145736 | tf_op jit(solution)/shard_map/ppermute | solution.py:47
  70.6 164.4 %all-gather.15.cloned.1.call-start = ((), (), s32[]{:S(2)}) async-start(), calls=%async_computation.3 | async-start | bytes 5242880 | tf_op jit(solution)/shard_map/all_gather | solution.py:940
  72.2 61.2 %collective-permute-start.13 = (bf16[2,256,2048]{2,1,0:T(8,128)(2,1)}, bf16[2,256,2048]{2,1,0:T(8,128)(2,1)}, u32[]{:S(2)}, u32[]{:S(2)}) collective-permute-start(bf16[2,256,2048]{2,1,0:T(8,128)(2,1)} %get-tuple-element.166), channel_id=1, source_target_pairs={{0,4},{4,0},{1,5},{5,1},{2,6},{6,2},{3,7},{7,3},{16,20},{20,16},{1... | collective-permute-start | bytes 6291464 | tf_op jit(solution)/shard_map/ppermute | solution.py:47
  97.7 28.2 %collective-permute-start.10 = (bf16[4,4,64,512]{3,2,1,0:T(8,128)(2,1)}, bf16[4,4,64,512]{3,2,1,0:T(8,128)(2,1)}, u32[]{:S(2)}, u32[]{:S(2)}) collective-permute-start(bf16[4,4,64,512]{3,2,1,0:T(8,128)(2,1)} %bitcast.257), channel_id=1, source_target_pairs={{0,16},{16,0},{1,17},{17,1},{2,18},{18,2},{3,19},{19,3},{4,20},{20... | collective-permute-start | bytes 3145736 | tf_op jit(solution)/shard_map/ppermute | solution.py:47
  113.6 28.2 %collective-permute-start.12 = (bf16[256,2048]{1,0:T(8,128)(2,1)}, bf16[256,2048]{1,0:T(8,128)(2,1)}, u32[]{:S(2)}, u32[]{:S(2)}) collective-permute-start(bf16[256,2048]{1,0:T(8,128)(2,1)} %collective-permute-done.6.refs_6_.refs_7_), channel_id=1, source_target_pairs={{0,4},{4,0},{8,12},{12,8},{1,5},{5,1},{9,13},{13,9},{2,6},{6,2},{1... | collective-permute-start | bytes 3145736 | tf_op jit(solution)/shard_map/ppermute | solution.py:47
  141.8 47.8 %collective-permute-start.17 = (bf16[4,4,64,1024]{3,2,1,0:T(8,128)(2,1)}, bf16[4,4,64,1024]{3,2,1,0:T(8,128)(2,1)}, u32[]{:S(2)}, u32[]{:S(2)}) collective-permute-start(bf16[4,4,64,1024]{3,2,1,0:T(8,128)(2,1)} %bitcast.280), channel_id=1, source_target_pairs={{0,16},{16,0},{1,17},{17,1},{2,18},{18,2},{3,19},{19,3},{4,20},{20... | collective-permute-start | bytes 6291464 | tf_op jit(solution)/shard_map/ppermute | solution.py:47
  143.3 26.4 %collective-permute-start.16 = (bf16[256,2048]{1,0:T(8,128)(2,1)}, bf16[256,2048]{1,0:T(8,128)(2,1)}, u32[]{:S(2)}, u32[]{:S(2)}) collective-permute-start(bf16[256,2048]{1,0:T(8,128)(2,1)} %get-tuple-element.175), channel_id=1, source_target_pairs={{0,8},{4,12},{8,0},{12,4},{1,9},{5,13},{9,1},{13,5},{2,10},{6,14},... | collective-permute-start | bytes 3145736 | tf_op jit(solution)/shard_map/ppermute | solution.py:47
  147.8 56.6 %collective-permute-start.18 = (bf16[256,2048]{1,0:T(8,128)(2,1)S(1)}, bf16[256,2048]{1,0:T(8,128)(2,1)}, u32[]{:S(2)}, u32[]{:S(2)}) collective-permute-start(bf16[256,2048]{1,0:T(8,128)(2,1)S(1)} %copy-done.61), channel_id=1, source_target_pairs={{8,0},{12,4},{9,1},{13,5},{10,2},{14,6},{11,3},{15,7},{24,16},{28,... | collective-permute-start | bytes 3145736 | tf_op jit(solution)/shard_map/ppermute | solution.py:47
  169.7 44.0 %collective-permute-start.22 = (bf16[256,2048]{1,0:T(8,128)(2,1)}, bf16[256,2048]{1,0:T(8,128)(2,1)S(1)}, u32[]{:S(2)}, u32[]{:S(2)}) collective-permute-start(bf16[256,2048]{1,0:T(8,128)(2,1)} %get-tuple-element.187), channel_id=1, source_target_pairs={{8,0},{12,4},{9,1},{13,5},{10,2},{14,6},{11,3},{15,7},{24,16},{28,... | collective-permute-start | bytes 3145736 | tf_op jit(solution)/shard_map/ppermute | solution.py:47
  234.4 25.8 %collective-permute-start.29 = (bf16[256,2048]{1,0:T(8,128)(2,1)}, bf16[256,2048]{1,0:T(8,128)(2,1)}, u32[]{:S(2)}, u32[]{:S(2)}) collective-permute-start(bf16[256,2048]{1,0:T(8,128)(2,1)} %get-tuple-element.203), channel_id=1, source_target_pairs={{0,16},{16,0},{1,17},{17,1},{2,18},{18,2},{3,19},{19,3},{4,20},{20... | collective-permute-start | bytes 3145736 | tf_op jit(solution)/shard_map/ppermute | solution.py:47
  260.1 23.6 %collective-permute-start.31 = (bf16[2,256,2048]{2,1,0:T(8,128)(2,1)}, bf16[2,256,2048]{2,1,0:T(8,128)(2,1)}, u32[]{:S(2)}, u32[]{:S(2)}) collective-permute-start(bf16[2,256,2048]{2,1,0:T(8,128)(2,1)} %get-tuple-element.210), channel_id=1, source_target_pairs={{0,4},{4,0},{8,12},{12,8},{1,5},{5,1},{9,13},{13,9},{2,6},{6,2},{1... | collective-permute-start | bytes 6291464 | tf_op jit(solution)/shard_map/ppermute | solution.py:47
  260.1 26.3 %collective-permute-start.30 = (bf16[256,2048]{1,0:T(8,128)(2,1)}, bf16[256,2048]{1,0:T(8,128)(2,1)}, u32[]{:S(2)}, u32[]{:S(2)}) collective-permute-start(bf16[256,2048]{1,0:T(8,128)(2,1)} %copy-done.43), channel_id=1, source_target_pairs={{0,16},{16,0},{1,17},{17,1},{2,18},{18,2},{3,19},{19,3},{4,20},{20... | collective-permute-start | bytes 3145736 | tf_op jit(solution)/shard_map/ppermute | solution.py:47
  260.7 67.7 %collective-permute-start.33 = (bf16[2,256,2048]{2,1,0:T(8,128)(2,1)}, bf16[2,256,2048]{2,1,0:T(8,128)(2,1)}, u32[]{:S(2)}, u32[]{:S(2)}) collective-permute-start(bf16[2,256,2048]{2,1,0:T(8,128)(2,1)} %get-tuple-element.219), channel_id=1, source_target_pairs={{0,8},{4,12},{8,0},{12,4},{1,9},{5,13},{9,1},{13,5},{2,10},{6,14},... | collective-permute-start | bytes 6291464 | tf_op jit(solution)/shard_map/ppermute | solution.py:47
  280.7 56.6 %collective-permute-start.37 = (bf16[4,256,1024]{2,1,0:T(8,128)(2,1)}, bf16[4,256,1024]{2,1,0:T(8,128)(2,1)}, u32[]{:S(2)}, u32[]{:S(2)}) collective-permute-start(bf16[4,256,1024]{2,1,0:T(8,128)(2,1)} %bitcast.69), channel_id=1, source_target_pairs={{0,16},{16,0},{1,17},{17,1},{2,18},{18,2},{3,19},{19,3},{4,20},{20... | collective-permute-start | bytes 6291464 | tf_op jit(solution)/shard_map/ppermute | solution.py:47
  283.8 46.7 %collective-permute-start.34 = (bf16[1,256,2048]{2,1,0:T(8,128)(2,1)}, bf16[1,256,2048]{2,1,0:T(8,128)(2,1)S(1)}, u32[]{:S(2)}, u32[]{:S(2)}) collective-permute-start(bf16[1,256,2048]{2,1,0:T(8,128)(2,1)} %get-tuple-element.221), channel_id=1, source_target_pairs={{0,12},{4,8},{8,4},{12,0},{1,13},{5,9},{9,5},{13,1},{2,14},{6,10},... | collective-permute-start | bytes 3145736 | tf_op jit(solution)/shard_map/ppermute | solution.py:47
  291.1 39.3 %collective-permute-start.32 = (bf16[2,128,2048]{2,1,0:T(8,128)(2,1)}, bf16[2,128,2048]{2,1,0:T(8,128)(2,1)}, u32[]{:S(2)}, u32[]{:S(2)}) collective-permute-start(bf16[2,128,2048]{2,1,0:T(8,128)(2,1)} %pad_maximum_fusion.11), channel_id=1, source_target_pairs={{0,1},{1,0},{2,3},{3,2},{4,5},{5,4},{6,7},{7,6},{8,9},{9,8},{10,11... | collective-permute-start | bytes 3145736 | tf_op jit(solution)/shard_map/ppermute | solution.py:47
  346.9 37.0 %collective-permute-start.39 = (bf16[4,256,512]{2,1,0:T(8,128)(2,1)}, bf16[4,256,512]{2,1,0:T(8,128)(2,1)}, u32[]{:S(2)}, u32[]{:S(2)}) collective-permute-start(bf16[4,256,512]{2,1,0:T(8,128)(2,1)} %bitcast.73), channel_id=1, source_target_pairs={{0,16},{16,0},{1,17},{17,1},{2,18},{18,2},{3,19},{19,3},{4,20},{20... | collective-permute-start | bytes 3145736 | tf_op jit(solution)/shard_map/ppermute | solution.py:47
  348.4 36.9 %collective-permute-start.38 = (bf16[2,256,1024]{2,1,0:T(8,128)(2,1)}, bf16[2,256,1024]{2,1,0:T(8,128)(2,1)}, u32[]{:S(2)}, u32[]{:S(2)}) collective-permute-start(bf16[2,256,1024]{2,1,0:T(8,128)(2,1)} %pad_maximum_fusion.12), channel_id=1, source_target_pairs={{0,1},{1,0},{2,3},{3,2},{4,5},{5,4},{6,7},{7,6},{8,9},{9,8},{10,11... | collective-permute-start | bytes 3145736 | tf_op jit(solution)/shard_map/ppermute | solution.py:47
  352.6 30.6 %collective-permute-start.40 = (bf16[1,128,2048]{2,1,0:T(8,128)(2,1)}, bf16[1,128,2048]{2,1,0:T(8,128)(2,1)}, u32[]{:S(2)}, u32[]{:S(2)}) collective-permute-start(bf16[1,128,2048]{2,1,0:T(8,128)(2,1)} %get-tuple-element.399), channel_id=1, source_target_pairs={{0,2},{1,3},{2,0},{3,1},{4,6},{5,7},{6,4},{7,5},{8,10},{9,11},{10,... | collective-permute-start | bytes 1572872 | tf_op jit(solution)/shard_map/ppermute | solution.py:47
  363.8 50.2 %collective-permute-start.41 = (bf16[4,256,640]{2,1,0:T(8,128)(2,1)}, bf16[4,256,640]{2,1,0:T(8,128)(2,1)}, u32[]{:S(2)}, u32[]{:S(2)}) collective-permute-start(bf16[4,256,640]{2,1,0:T(8,128)(2,1)} %pad_maximum_fusion.3), channel_id=1, source_target_pairs={{0,16},{16,0},{1,17},{17,1},{2,18},{18,2},{3,19},{19,3},{4,20},{20... | collective-permute-start | bytes 3932168 | tf_op jit(solution)/shard_map/ppermute | solution.py:47
  383.2 36.4 %collective-permute-start.45 = (bf16[1,256,2048]{2,1,0:T(8,128)(2,1)}, bf16[1,256,2048]{2,1,0:T(8,128)(2,1)S(1)}, u32[]{:S(2)}, u32[]{:S(2)}) collective-permute-start(bf16[1,256,2048]{2,1,0:T(8,128)(2,1)} %get-tuple-element.246), channel_id=1, source_target_pairs={{0,12},{4,8},{8,4},{12,0},{1,13},{5,9},{9,5},{13,1},{2,14},{6,10},... | collective-permute-start | bytes 3145736 | tf_op jit(solution)/shard_map/ppermute | solution.py:47
  394.7 33.6 %collective-permute-start.47 = (bf16[1,256,1024]{2,1,0:T(8,128)(2,1)S(1)}, bf16[1,256,1024]{2,1,0:T(8,128)(2,1)S(1)}, u32[]{:S(2)}, u32[]{:S(2)}) collective-permute-start(bf16[1,256,1024]{2,1,0:T(8,128)(2,1)S(1)} %get-tuple-element.397), channel_id=1, source_target_pairs={{0,2},{1,3},{2,0},{3,1},{4,6},{5,7},{6,4},{7,5},{8,10},{9,11},{10,... | collective-permute-start | bytes 1572872 | tf_op jit(solution)/shard_map/ppermute | solution.py:47
  401.7 40.1 %collective-permute-start.46 = (bf16[256,2048]{1,0:T(8,128)(2,1)}, bf16[256,2048]{1,0:T(8,128)(2,1)S(1)}, u32[]{:S(2)}, u32[]{:S(2)}) collective-permute-start(bf16[256,2048]{1,0:T(8,128)(2,1)} %fusion.10), channel_id=1, source_target_pairs={{0,8},{4,12},{8,0},{12,4},{1,9},{5,13},{9,1},{13,5},{2,10},{6,14},... | collective-permute-start | bytes 3145736 | tf_op jit(solution)/shard_map/ppermute | solution.py:47
  417.1 24.7 %collective-permute-start.44 = (bf16[2,256,640]{2,1,0:T(8,128)(2,1)}, bf16[2,256,640]{2,1,0:T(8,128)(2,1)}, u32[]{:S(2)}, u32[]{:S(2)}) collective-permute-start(bf16[2,256,640]{2,1,0:T(8,128)(2,1)} %pad_maximum_fusion.13), channel_id=1, source_target_pairs={{0,1},{1,0},{2,3},{3,2},{4,5},{5,4},{6,7},{7,6},{8,9},{9,8},{10,11... | collective-permute-start | bytes 1966088 | tf_op jit(solution)/shard_map/ppermute | solution.py:47
  (113 other events, 1051.2 us)
Sparse Core Ops, SparseCore 0:
  31.5 34.6 all-gather.10
  67.8 26.9 all-gather.8
  96.3 45.4 all-gather.12
  143.8 79.4 all-gather.14

commit v4 on v3

--- a/solution.py
+++ b/solution.py
@@ -1219,9 +1219,7 @@
         out_shape=jax.ShapeDtypeStruct((LEVELS, tok, D), BF),
         name="mixed",
     )(here, theirs, ratio, tokens[0], *after(shares[:3] + third, right_sent))[:, None]
-    right_half, mixed, dxn_across = together(right_half, mixed, dxn_across)
-    right_kept = after(right_kept, mixed)
-    right_pair = fsdp_rest(right_kept, right_half)
+    mixed, dxn_across = together(mixed, dxn_across)
     dxn_own = near + dxn_across.astype(F32)
     grad_norm = jnp.sum(dxn_own * own_x * scale, axis=0)
     scaled = norm_gain * dxn_own
@@ -1229,6 +1227,8 @@
     dx = (dx + jnp.sum(after(cotangent, mixed)[:, 0].astype(F32), axis=0)).astype(BF)
     flat = jnp.concatenate([flat, grad_norm.reshape(-1, LANES)])
     flat = butterfly(flat, "dp")
+    right_half, flat, dx = together(right_half, flat, dx)
+    right_pair = fsdp_rest(right_kept, right_half)
 
     def whole_sum(pair):
         total = (pair[0].astype(F32) + pair[1].astype(F32)).astype(BF)
@@ -1237,8 +1237,8 @@
     z_pair, left_pair = together(z_pair, left_pair)
     early = jnp.concatenate([whole_sum(z_pair), whole_sum(left_pair)], axis=2)
     early_got = [picked(early, s)] + [swapped(picked(early, s ^ k), "seq", k) for k in range(1, ns)]
+    flat = butterfly(flat, "fsdp")
     early_got, right_pair, flat = together(early_got, right_pair, flat)
-    flat = butterfly(flat, "fsdp")
     late = whole_sum(right_pair)
     late_got = [picked(late, s)] + [swapped(picked(late, s ^ k), "seq", k) for k in range(1, ns)]
     early = jnp.stack(reordered_by_xor(early_got, s))

time: 501 us -> 530 us (1.058)
  waiting for transfers between devices: 129 us -> 158 us
    ppermute x62, waiting for transfers between devices: 86.5 us -> 116 us  [swapped(): return lax.ppermute(value, axis, pairs)]
  transfers between devices with their start and end apart: 66 -> 66, of which waited for: 23 -> 24; matrix products, arithmetic and copies ran while one was open for 19% -> 20% of each run, Pallas kernels for 32% -> 31%
where the time goes in v4:
time: 530 us; the launch traced here: 523 us
  Pallas kernels  164 us (31%)
  waiting for transfers between devices  158 us (30%)
  local copies, waits for them, and re-layouts  64.2 us (12%)
  other arithmetic  56.8 us (11%)
  starting transfers between devices  55.5 us (10%)
  between operations  15.7 us (3%)
  matrix products  8.89 us (2%)
    ppermute x62, waiting for transfers between devices, swapped(): return lax.ppermute(value, axis, pairs)  116 us
    ppermute x62, starting transfers between devices, swapped(): return lax.ppermute(value, axis, pairs)  55.3 us
    all_gather x4, waiting for transfers between devices, over_fsdp(): return lax.all_gather(chunk, 'fsdp', axis=0, tiled=False)  42.1 us
    pallas_call x1, Pallas kernels, scan_backward(): call(functools.partial(backward_kernel, heads), grid=(blocks,), in_specs=...  34.2 us
    pallas_call x7, Pallas kernels, row_terms(): call(functools.partial(terms_kernel, ns, nf), grid_spec=pltpu.PrefetchSca...  24.6 us
    unnamed x161, local copies, waits for them, and re-layouts  18 us
    pallas_call x1, Pallas kernels, shards(): call(functools.partial(products_kernel, where, plan, lanes, tok, ns, nd),...  16.4 us
    pallas_call x1, Pallas kernels, scan_forward(): call(functools.partial(forward_kernel, heads), grid=(blocks,), in_specs=i...  14.9 us
  transfers between devices with their start and end apart: 66, of which 24 were waited for; matrix products, arithmetic and copies ran while one was open for 20% of the time, Pallas kernels for 31%

profile of v4, /device:TPU:0, one launch (start us, length us, event | category | flops | bytes accessed | tf_op | source)
XLA Modules:
  0.0 522.7 jit_solution(2325589546651435408)
XLA Ops:
  24.9 5.6 %collective-permute-done.2.refs_3_ = bf16[64,2176]{1,0:T(8,128)(2,1)S(1)} collective-permute-done((bf16[64,2176]{1,0:T(8,128)(2,1)}, bf16[64,2176]{1,0:T(8,128)(2,1)S(1)}, u32[]{:S(2)}, u32[]{:S(2)}) %collective-permute-start.2) | collective-permute-done | bytes 278560 | tf_op jit(solution)/shard_map/ppermute | solution.py:47
  34.8 4.8 slice_bitcast_fusion
  40.4 4.5 slice_bitcast_fusion.2
  44.9 8.3 %collective-permute-done.4.refs_2_ = bf16[256,2048]{1,0:T(8,128)(2,1)} collective-permute-done((bf16[256,2048]{1,0:T(8,128)(2,1)}, bf16[256,2048]{1,0:T(8,128)(2,1)}, u32[]{:S(2)}, u32[]{:S(2)}) %collective-permute-start.4) | collective-permute-done | bytes 1048608 | tf_op jit(solution)/shard_map/ppermute | solution.py:47
  53.2 13.7 %all-gather.9.cloned.1.call-done = bf16[16,64,640]{2,1,0:T(8,128)(2,1)} async-done(((bf16[4,64,640]{2,1,0:T(8,128)(2,1)}), bf16[16,64,640]{2,1,0:T(8,128)(2,1)}) %all-gather.9.cloned.1.call-update) | async-done | bytes 1310736 | tf_op jit(solution)/shard_map/all_gather | solution.py:940
  75.4 20.0 %all-gather.11.cloned.1.call-done = bf16[16,64,512]{2,1,0:T(8,128)(2,1)} async-done(((bf16[4,64,512]{2,1,0:T(8,128)(2,1)}), bf16[16,64,512]{2,1,0:T(8,128)(2,1)}) %all-gather.11.cloned.1.call-update) | async-done | bytes 1048592 | tf_op jit(solution)/shard_map/all_gather | solution.py:940
  102.8 5.8 %filled.5 = bf16[4,256,2048]{2,1,0:T(8,128)(2,1)} custom-call(s32[4,3]{1,0:T(4,128)S(1)} %pad_add_fusion.index_ref, bf16[256,2048]{1,0:T(8,128)(2,1)} %fusion.2.refs_0_, bf16[256,2048]{1,0:T(8,128)(2,1)} %collective-permute-done.8.refs_1_, bf16[256,2048]{1,0:T(8,128)(2,1)} %collective-permute-done.4.refs_2_, bf16[256,2048]{1,0:T(8,128)(2,1)} %collective-permute-done.9.refs_3_), custom_call_target="tpu_custom_call" | custom-call | flops 1 | bytes 1 | tf_op jit(solution)/shard_map/filled/pallas_call | solution.py:116
  108.6 5.6 %convolution_convert_fusion.in_a_ref = bf16[1024,640]{1,0:T(8,128)(2,1)S(1)} fusion(bf16[1024,2048]{1,0:T(8,128)(2,1)} %bitcast.266, bf16[2048,640]{1,0:T(8,128)(2,1)S(1)} %bitcast.245), kind=kOutput, calls=%fused_computation.36 | convolution fusion | flops 2685009920 | bytes 8126464 | tf_op jit(solution)/shard_map/dot_general | solution.py:31
  120.2 6.4 %copy.203 = bf16[1024,2048]{0,1:T(8,128)(2,1)} copy(bf16[1024,2048]{1,0:T(8,128)(2,1)} %bitcast.267) | data formatting | bytes 8388608 | tf_op jit(solution)/shard_map/reshape | solution.py:965
  134.1 8.4 %all-gather.13.cloned.1.call-done = bf16[16,64,1024]{2,1,0:T(8,128)(2,1)} async-done(((bf16[4,64,1024]{2,1,0:T(8,128)(2,1)}), bf16[16,64,1024]{2,1,0:T(8,128)(2,1)}) %all-gather.13.cloned.1.call-update) | async-done | bytes 2097168 | tf_op jit(solution)/shard_map/all_gather | solution.py:940
  151.7 14.9 %scan_forward.1 = (f32[1024,1024]{1,0:T(8,128)}, f32[8,128,1024]{2,1,0:T(8,128)}) custom-call(s32[8]{0:T(128)S(1)} %pad_add_fusion.16.segp_ref, s32[1024,1]{1,0:T(8,128)S(1)} %copy-done.13, s32[1,1024]{1,0:T(1,128)S(1)} %bitcast.261, f32[1024,128]{1,0:T(8,128)S(1)} %pad.55.mask_ref, bf16[1024,640]{1,0:T(8,128)(2,1)S(1)} %convolution_convert_fusion.in_a_ref, ...), custom_call_target="tpu_custom_call" | custom-call | flops 1 | bytes 1 | tf_op jit(solution)/shard_map/scan_forward/pallas_call | solution.py:580
  166.6 3.8 collective-permute-done.16.refs_5_.refs_6_
  172.7 17.6 %collective-permute-done.17.refs_1_ = bf16[4,4,64,1024]{3,2,1,0:T(8,128)(2,1)} collective-permute-done((bf16[4,4,64,1024]{3,2,1,0:T(8,128)(2,1)}, bf16[4,4,64,1024]{3,2,1,0:T(8,128)(2,1)}, u32[]{:S(2)}, u32[]{:S(2)}) %collective-permute-start.17) | collective-permute-done | bytes 2097184 | tf_op jit(solution)/shard_map/ppermute | solution.py:47
  190.3 12.2 %gated.1 = (bf16[1024,1024]{1,0:T(8,128)(2,1)S(1)}, bf16[2048,1024]{1,0:T(8,128)(2,1)}, bf16[1024,1024]{1,0:T(8,128)(2,1)S(1)}, bf16[1024,1024]{1,0:T(8,128)(2,1)}, f32[8,1024]{1,0:T(8,128)S(1)}) custom-call(s32[2]{0:T(128)S(1)} %pad_add_fusion.15.here_ref, bf16[1024,2048]{1,0:T(8,128)(2,1)} %bitcast.268, f32[1024,1024]{1,0:T(8,128)} %get-tuple-element.178.y_ref, ...), custom_call_target="tpu_custom_call" | custom-call | flops 1 | bytes 1 | tf_op jit(solution)/shard_map/gated/pallas_call | solution.py:288
  207.4 5.3 %collective-permute-done.21 = f32[32,128]{1,0:T(8,128)S(1)} collective-permute-done((f32[32,128]{1,0:T(8,128)S(1)}, f32[32,128]{1,0:T(8,128)S(1)}, u32[]{:S(2)}, u32[]{:S(2)}) %collective-permute-start.21) | collective-permute-done | bytes 16416 | tf_op jit(solution)/shard_map/ppermute | solution.py:47
  212.7 3.8 collective-permute-start.24
  222.2 14.1 %upper.1 = (bf16[2,1024,2048]{2,1,0:T(8,128)(2,1)}, bf16[512,2048]{1,0:T(8,128)(2,1)}, bf16[256,2048]{1,0:T(8,128)(2,1)}, bf16[256,2048]{1,0:T(8,128)(2,1)S(1)}) custom-call(s32[2]{0:T(128)S(1)} %pad_add_fusion.15.here_ref, s32[2]{0:T(128)S(1)} %call_exported.0.range_ref, f32[2,4]{1,0:T(2,128)S(1)} %fusion.41.count_ref, f32[4,1024]{1,0:T(4,128)S(1)} %fusion.29.ratio_ref, ...), custom_call_target="tpu_custom_call" | custom-call | flops 1 | bytes 1 | tf_op jit(solution)/shard_map/upper/pallas_call | solution.py:1049
  239.1 16.4 %products.1 = (bf16[2,256,2048]{2,1,0:T(8,128)(2,1)}, bf16[2,256,2048]{2,1,0:T(8,128)(2,1)}, bf16[2,256,2048]{2,1,0:T(8,128)(2,1)}, bf16[2,256,2048]{2,1,0:T(8,1...) custom-call(s32[2]{0:T(128)S(1)} %pad_add_fusion.15.here_ref, f32[2,4]{1,0:T(2,128)S(1)} %fusion.41.count_ref, ...), custom_call_target="tpu_custom_call" | custom-call | flops 1 | bytes 1 | tf_op jit(solution)/shard_map/products/pallas_call | solution.py:1072
  266.5 12.3 %gate_backward.1 = (bf16[1024,1024]{1,0:T(8,128)(2,1)S(1)}, bf16[1024,1024]{1,0:T(8,128)(2,1)S(1)}, f32[8,1024]{1,0:T(8,128)S(1)}) custom-call(f32[2,4]{1,0:T(2,128)S(1)} %fusion.41.count_ref, bf16[2,1024,2048]{2,1,0:T(8,128)(2,1)} %get-tuple-element.201.upper_ref, bf16[1024,2048]{1,0:T(8,128)(2,1)} %get-tuple-element.202.w_ref, ...), custom_call_target="tpu_custom_call" | custom-call | flops 1 | bytes 1 | tf_op jit(solution)/shard_map/gate_backward/pallas_call | solution.py:1098
  280.2 6.2 %row_terms.7 = bf16[4,4,64,1024]{3,2,1,0:T(8,128)(2,1)} custom-call(s32[1]{0:T(128)} %bitcast.49.at_ref, bf16[2048,1024]{1,0:T(8,128)(2,1)} %bitcast.237, bf16[1024,1024]{1,0:T(8,128)(2,1)S(1)} %get-tuple-element.232.right_ref.dz_ref), custom_call_target="tpu_custom_call" | custom-call | flops 1 | bytes 1 | tf_op jit(solution)/shard_map/row_terms/pallas_call | solution.py:145
  295.3 34.2 %scan_backward.1 = (bf16[1024,1024]{1,0:T(8,128)(2,1)}, f32[1024,256]{1,0:T(8,128)S(1)}, f32[1024,128]{1,0:T(8,128)S(1)}, f32[1,128]{1,0:T(1,128)S(1)}, f32[8,1024]{1,0:T(8,128)S(1)}) custom-call(s32[8]{0:T(128)S(1)} %pad_add_fusion.16.segp_ref, s32[1024,1]{1,0:T(8,128)S(1)} %copy-done.14, s32[1,1024]{1,0:T(1,128)S(1)} %bitcast.262, ...), custom_call_target="tpu_custom_call" | custom-call | flops 1 | bytes 1 | tf_op jit(solution)/shard_map/scan_backward/pallas_call | solution.py:606
  336.2 4.9 row_terms.8
  341.1 3.5 add_convert_fusion.7
  346.6 3.9 row_terms.9
  364.6 13.7 %input_grad.1 = bf16[4,256,2048]{2,1,0:T(8,128)(2,1)} custom-call(bf16[1024,1024]{1,0:T(8,128)(2,1)S(1)} %copy-done.7, bf16[1024,1024]{1,0:T(8,128)(2,1)S(1)} %copy-done.2, bf16[1024,128]{1,0:T(8,128)(2,1)S(1)} %get-tuple-element.246.right_ref.dr_ref, bf16[2048,1024]{1,0:T(8,128)(2,1)} %get-tuple-element.241.wz_ref, bf16[2048,640]{1,0:T(8,128)(2,1)} %bitcast.246, ...), custom_call_target="tpu_custom_call" | custom-call | flops 1 | bytes 1 | tf_op jit(solution)/shard_map/input_grad/pallas_call | solution.py:219
  384.4 25.0 %collective-permute-done.41 = bf16[1,128,2048]{2,1,0:T(8,128)(2,1)} collective-permute-done((bf16[1,128,2048]{2,1,0:T(8,128)(2,1)}, bf16[1,128,2048]{2,1,0:T(8,128)(2,1)}, u32[]{:S(2)}, u32[]{:S(2)}) %collective-permute-start.41) | collective-permute-done | bytes 524320 | tf_op jit(solution)/shard_map/ppermute | solution.py:47
  409.4 4.9 row_terms.12
  425.8 11.4 %collective-permute-done.44 = bf16[2,256,512]{2,1,0:T(8,128)(2,1)S(1)} collective-permute-done((bf16[2,256,512]{2,1,0:T(8,128)(2,1)S(1)}, bf16[2,256,512]{2,1,0:T(8,128)(2,1)S(1)}, u32[]{:S(2)}, u32[]{:S(2)}) %collective-permute-start.44) | collective-permute-done | bytes 524320 | tf_op jit(solution)/shard_map/ppermute | solution.py:47
  444.5 7.8 %mixed.1 = bf16[4,256,2048]{2,1,0:T(8,128)(2,1)} custom-call(s32[2]{0:T(128)S(1)} %pad_add_fusion.15.here_ref, f32[4,8]{1,0:T(4,128)S(1)} %fusion.36.count_ref, f32[4,1024]{1,0:T(4,128)S(1)} %fusion.29.ratio_ref, bf16[256,2048]{1,0:T(8,128)(2,1)S(1)} %bitcast.244, bf16[2,256,2048]{2,1,0:T(8,128)(2,1)S(1)} %copy-done.32, ...), custom_call_target="tpu_custom_call" | custom-call | flops 1 | bytes 1 | tf_op jit(solution)/shard_map/mixed/pallas_call | solution.py:1202
  452.3 5.0 collective-permute-done.49
  470.6 3.5 fusion.8
  480.8 13.9 %collective-permute-done.55 = f32[72,128]{1,0:T(8,128)S(1)} collective-permute-done((f32[72,128]{1,0:T(8,128)S(1)}, f32[72,128]{1,0:T(8,128)S(1)}, u32[]{:S(2)}, u32[]{:S(2)}) %collective-permute-start.55) | collective-permute-done | bytes 36896 | tf_op jit(solution)/shard_map/ppermute | solution.py:47
  (491 shorter events, 185.4 us)
Async XLA Ops:
  7.2 59.7 %all-gather.9.cloned.1.call-start = ((), (), s32[]{:S(2)}) async-start(), calls=%async_computation | async-start | bytes 1638400 | tf_op jit(solution)/shard_map/all_gather | solution.py:940
  17.3 27.6 %collective-permute-start.3 = (bf16[128,2048]{1,0:T(8,128)(2,1)}, bf16[128,2048]{1,0:T(8,128)(2,1)}, u32[]{:S(2)}, u32[]{:S(2)}) collective-permute-start(bf16[128,2048]{1,0:T(8,128)(2,1)} %param.28), channel_id=1, source_target_pairs={{0,16},{16,0},{1,17},{17,1},{2,18},{18,2},{3,19},{19,3},{4,20},{20... | collective-permute-start | bytes 1572872 | tf_op jit(solution)/shard_map/ppermute | solution.py:47
  20.6 32.6 %collective-permute-start.4 = (bf16[256,2048]{1,0:T(8,128)(2,1)}, bf16[256,2048]{1,0:T(8,128)(2,1)}, u32[]{:S(2)}, u32[]{:S(2)}) collective-permute-start(bf16[256,2048]{1,0:T(8,128)(2,1)} %fusion.2.refs_0_), channel_id=1, source_target_pairs={{0,8},{4,12},{8,0},{12,4},{1,9},{5,13},{9,1},{13,5},{2,10},{6,14},... | collective-permute-start | bytes 3145736 | tf_op jit(solution)/shard_map/ppermute | solution.py:47
  32.1 63.3 %all-gather.11.cloned.1.call-start = ((), (), s32[]{:S(2)}) async-start(), calls=%async_computation.1 | async-start | bytes 1310720 | tf_op jit(solution)/shard_map/all_gather | solution.py:940
  40.4 102.1 %all-gather.13.cloned.1.call-start = ((), (), s32[]{:S(2)}) async-start(), calls=%async_computation.2 | async-start | bytes 2621440 | tf_op jit(solution)/shard_map/all_gather | solution.py:940
  66.9 31.5 %collective-permute-start.7 = (bf16[2,256,2048]{2,1,0:T(8,128)(2,1)}, bf16[2,256,2048]{2,1,0:T(8,128)(2,1)}, u32[]{:S(2)}, u32[]{:S(2)}) collective-permute-start(bf16[2,256,2048]{2,1,0:T(8,128)(2,1)} %get-tuple-element.151), channel_id=1, source_target_pairs={{0,4},{4,0},{8,12},{12,8},{1,5},{5,1},{9,13},{13,9},{2,6},{6,2},{1... | collective-permute-start | bytes 6291464 | tf_op jit(solution)/shard_map/ppermute | solution.py:47
  66.9 31.5 %collective-permute-start.5 = (bf16[4,4,64,640]{3,2,1,0:T(8,128)(2,1)}, bf16[4,4,64,640]{3,2,1,0:T(8,128)(2,1)}, u32[]{:S(2)}, u32[]{:S(2)}) collective-permute-start(bf16[4,4,64,640]{3,2,1,0:T(8,128)(2,1)} %bitcast.254), channel_id=1, source_target_pairs={{0,16},{16,0},{1,17},{17,1},{2,18},{18,2},{3,19},{19,3},{4,20},{20... | collective-permute-start | bytes 3932168 | tf_op jit(solution)/shard_map/ppermute | solution.py:47
  68.6 26.8 %collective-permute-start.9 = (bf16[256,2048]{1,0:T(8,128)(2,1)}, bf16[256,2048]{1,0:T(8,128)(2,1)}, u32[]{:S(2)}, u32[]{:S(2)}) collective-permute-start(bf16[256,2048]{1,0:T(8,128)(2,1)} %collective-permute-done.4.refs_2_), channel_id=1, source_target_pairs={{0,4},{4,0},{8,12},{12,8},{1,5},{5,1},{9,13},{13,9},{2,6},{6,2},{1... | collective-permute-start | bytes 3145736 | tf_op jit(solution)/shard_map/ppermute | solution.py:47
  68.9 26.5 %collective-permute-start.6 = (bf16[256,2048]{1,0:T(8,128)(2,1)}, bf16[256,2048]{1,0:T(8,128)(2,1)}, u32[]{:S(2)}, u32[]{:S(2)}) collective-permute-start(bf16[256,2048]{1,0:T(8,128)(2,1)} %get-tuple-element.149), channel_id=1, source_target_pairs={{0,8},{4,12},{8,0},{12,4},{1,9},{5,13},{9,1},{13,5},{2,10},{6,14},... | collective-permute-start | bytes 3145736 | tf_op jit(solution)/shard_map/ppermute | solution.py:47
  71.3 166.6 %all-gather.15.cloned.1.call-start = ((), (), s32[]{:S(2)}) async-start(), calls=%async_computation.3 | async-start | bytes 5242880 | tf_op jit(solution)/shard_map/all_gather | solution.py:940
  72.9 61.2 %collective-permute-start.13 = (bf16[2,256,2048]{2,1,0:T(8,128)(2,1)}, bf16[2,256,2048]{2,1,0:T(8,128)(2,1)}, u32[]{:S(2)}, u32[]{:S(2)}) collective-permute-start(bf16[2,256,2048]{2,1,0:T(8,128)(2,1)} %get-tuple-element.168), channel_id=1, source_target_pairs={{0,4},{4,0},{1,5},{5,1},{2,6},{6,2},{3,7},{7,3},{16,20},{20,16},{1... | collective-permute-start | bytes 6291464 | tf_op jit(solution)/shard_map/ppermute | solution.py:47
  98.4 28.2 %collective-permute-start.10 = (bf16[4,4,64,512]{3,2,1,0:T(8,128)(2,1)}, bf16[4,4,64,512]{3,2,1,0:T(8,128)(2,1)}, u32[]{:S(2)}, u32[]{:S(2)}) collective-permute-start(bf16[4,4,64,512]{3,2,1,0:T(8,128)(2,1)} %bitcast.256), channel_id=1, source_target_pairs={{0,16},{16,0},{1,17},{17,1},{2,18},{18,2},{3,19},{19,3},{4,20},{20... | collective-permute-start | bytes 3145736 | tf_op jit(solution)/shard_map/ppermute | solution.py:47
  114.3 28.2 %collective-permute-start.12 = (bf16[256,2048]{1,0:T(8,128)(2,1)}, bf16[256,2048]{1,0:T(8,128)(2,1)}, u32[]{:S(2)}, u32[]{:S(2)}) collective-permute-start(bf16[256,2048]{1,0:T(8,128)(2,1)} %collective-permute-done.6.refs_6_.refs_7_), channel_id=1, source_target_pairs={{0,4},{4,0},{8,12},{12,8},{1,5},{5,1},{9,13},{13,9},{2,6},{6,2},{1... | collective-permute-start | bytes 3145736 | tf_op jit(solution)/shard_map/ppermute | solution.py:47
  142.5 47.8 %collective-permute-start.17 = (bf16[4,4,64,1024]{3,2,1,0:T(8,128)(2,1)}, bf16[4,4,64,1024]{3,2,1,0:T(8,128)(2,1)}, u32[]{:S(2)}, u32[]{:S(2)}) collective-permute-start(bf16[4,4,64,1024]{3,2,1,0:T(8,128)(2,1)} %bitcast.279), channel_id=1, source_target_pairs={{0,16},{16,0},{1,17},{17,1},{2,18},{18,2},{3,19},{19,3},{4,20},{20... | collective-permute-start | bytes 6291464 | tf_op jit(solution)/shard_map/ppermute | solution.py:47
  148.6 56.6 %collective-permute-start.18 = (bf16[256,2048]{1,0:T(8,128)(2,1)S(1)}, bf16[256,2048]{1,0:T(8,128)(2,1)}, u32[]{:S(2)}, u32[]{:S(2)}) collective-permute-start(bf16[256,2048]{1,0:T(8,128)(2,1)S(1)} %copy-done.59), channel_id=1, source_target_pairs={{8,0},{12,4},{9,1},{13,5},{10,2},{14,6},{11,3},{15,7},{24,16},{28,... | collective-permute-start | bytes 3145736 | tf_op jit(solution)/shard_map/ppermute | solution.py:47
  170.4 46.2 %collective-permute-start.22 = (bf16[256,2048]{1,0:T(8,128)(2,1)}, bf16[256,2048]{1,0:T(8,128)(2,1)S(1)}, u32[]{:S(2)}, u32[]{:S(2)}) collective-permute-start(bf16[256,2048]{1,0:T(8,128)(2,1)} %get-tuple-element.186), channel_id=1, source_target_pairs={{8,0},{12,4},{9,1},{13,5},{10,2},{14,6},{11,3},{15,7},{24,16},{28,... | collective-permute-start | bytes 3145736 | tf_op jit(solution)/shard_map/ppermute | solution.py:47
  263.4 68.1 %collective-permute-start.33 = (bf16[2,256,2048]{2,1,0:T(8,128)(2,1)}, bf16[2,256,2048]{2,1,0:T(8,128)(2,1)}, u32[]{:S(2)}, u32[]{:S(2)}) collective-permute-start(bf16[2,256,2048]{2,1,0:T(8,128)(2,1)} %get-tuple-element.223), channel_id=1, source_target_pairs={{0,8},{4,12},{8,0},{12,4},{1,9},{5,13},{9,1},{13,5},{2,10},{6,14},... | collective-permute-start | bytes 6291464 | tf_op jit(solution)/shard_map/ppermute | solution.py:47
  286.5 54.7 %collective-permute-start.38 = (bf16[4,256,1024]{2,1,0:T(8,128)(2,1)}, bf16[4,256,1024]{2,1,0:T(8,128)(2,1)}, u32[]{:S(2)}, u32[]{:S(2)}) collective-permute-start(bf16[4,256,1024]{2,1,0:T(8,128)(2,1)} %bitcast.69), channel_id=1, source_target_pairs={{0,16},{16,0},{1,17},{17,1},{2,18},{18,2},{3,19},{19,3},{4,20},{20... | collective-permute-start | bytes 6291464 | tf_op jit(solution)/shard_map/ppermute | solution.py:47
  293.5 38.1 %collective-permute-start.32 = (bf16[2,128,2048]{2,1,0:T(8,128)(2,1)}, bf16[2,128,2048]{2,1,0:T(8,128)(2,1)}, u32[]{:S(2)}, u32[]{:S(2)}) collective-permute-start(bf16[2,128,2048]{2,1,0:T(8,128)(2,1)} %pad_maximum_fusion.11), channel_id=1, source_target_pairs={{0,1},{1,0},{2,3},{3,2},{4,5},{5,4},{6,7},{7,6},{8,9},{9,8},{10,11... | collective-permute-start | bytes 3145736 | tf_op jit(solution)/shard_map/ppermute | solution.py:47
  293.5 39.7 %collective-permute-start.34 = (bf16[1,256,2048]{2,1,0:T(8,128)(2,1)}, bf16[1,256,2048]{2,1,0:T(8,128)(2,1)S(1)}, u32[]{:S(2)}, u32[]{:S(2)}) collective-permute-start(bf16[1,256,2048]{2,1,0:T(8,128)(2,1)} %get-tuple-element.225), channel_id=1, source_target_pairs={{0,12},{4,8},{8,4},{12,0},{1,13},{5,9},{9,5},{13,1},{2,14},{6,10},... | collective-permute-start | bytes 3145736 | tf_op jit(solution)/shard_map/ppermute | solution.py:47
  345.7 63.7 %collective-permute-start.39 = (bf16[2,256,1024]{2,1,0:T(8,128)(2,1)}, bf16[2,256,1024]{2,1,0:T(8,128)(2,1)}, u32[]{:S(2)}, u32[]{:S(2)}) collective-permute-start(bf16[2,256,1024]{2,1,0:T(8,128)(2,1)} %pad_maximum_fusion.12), channel_id=1, source_target_pairs={{0,1},{1,0},{2,3},{3,2},{4,5},{5,4},{6,7},{7,6},{8,9},{9,8},{10,11... | collective-permute-start | bytes 3145736 | tf_op jit(solution)/shard_map/ppermute | solution.py:47
  350.5 58.9 %collective-permute-start.40 = (bf16[4,256,512]{2,1,0:T(8,128)(2,1)}, bf16[4,256,512]{2,1,0:T(8,128)(2,1)}, u32[]{:S(2)}, u32[]{:S(2)}) collective-permute-start(bf16[4,256,512]{2,1,0:T(8,128)(2,1)} %bitcast.73), channel_id=1, source_target_pairs={{0,16},{16,0},{1,17},{17,1},{2,18},{18,2},{3,19},{19,3},{4,20},{20... | collective-permute-start | bytes 3145736 | tf_op jit(solution)/shard_map/ppermute | solution.py:47
  381.5 40.0 %collective-permute-start.43 = (bf16[2,256,2048]{2,1,0:T(8,128)(2,1)}, bf16[2,256,2048]{2,1,0:T(8,128)(2,1)}, u32[]{:S(2)}, u32[]{:S(2)}) collective-permute-start(bf16[2,256,2048]{2,1,0:T(8,128)(2,1)} %pad_maximum_fusion.1), channel_id=1, source_target_pairs={{0,4},{4,0},{8,12},{12,8},{1,5},{5,1},{9,13},{13,9},{2,6},{6,2},{1... | collective-permute-start | bytes 6291464 | tf_op jit(solution)/shard_map/ppermute | solution.py:47
  382.6 26.8 %collective-permute-start.41 = (bf16[1,128,2048]{2,1,0:T(8,128)(2,1)}, bf16[1,128,2048]{2,1,0:T(8,128)(2,1)}, u32[]{:S(2)}, u32[]{:S(2)}) collective-permute-start(bf16[1,128,2048]{2,1,0:T(8,128)(2,1)} %get-tuple-element.401), channel_id=1, source_target_pairs={{0,2},{1,3},{2,0},{3,1},{4,6},{5,7},{6,4},{7,5},{8,10},{9,11},{10,... | collective-permute-start | bytes 1572872 | tf_op jit(solution)/shard_map/ppermute | solution.py:47
  383.4 53.8 %collective-permute-start.42 = (bf16[4,256,640]{2,1,0:T(8,128)(2,1)}, bf16[4,256,640]{2,1,0:T(8,128)(2,1)}, u32[]{:S(2)}, u32[]{:S(2)}) collective-permute-start(bf16[4,256,640]{2,1,0:T(8,128)(2,1)} %pad_maximum_fusion.3), channel_id=1, source_target_pairs={{0,16},{16,0},{1,17},{17,1},{2,18},{18,2},{3,19},{19,3},{4,20},{20... | collective-permute-start | bytes 3932168 | tf_op jit(solution)/shard_map/ppermute | solution.py:47
  409.4 35.1 %collective-permute-start.37 = (bf16[1,256,2048]{2,1,0:T(8,128)(2,1)}, bf16[1,256,2048]{2,1,0:T(8,128)(2,1)S(1)}, u32[]{:S(2)}, u32[]{:S(2)}) collective-permute-start(bf16[1,256,2048]{2,1,0:T(8,128)(2,1)} %get-tuple-element.230), channel_id=1, source_target_pairs={{0,12},{4,8},{8,4},{12,0},{1,13},{5,9},{9,5},{13,1},{2,14},{6,10},... | collective-permute-start | bytes 3145736 | tf_op jit(solution)/shard_map/ppermute | solution.py:47
  419.5 32.8 %collective-permute-start.48 = (bf16[1,256,1024]{2,1,0:T(8,128)(2,1)S(1)}, bf16[1,256,1024]{2,1,0:T(8,128)(2,1)S(1)}, u32[]{:S(2)}, u32[]{:S(2)}) collective-permute-start(bf16[1,256,1024]{2,1,0:T(8,128)(2,1)S(1)} %get-tuple-element.399), channel_id=1, source_target_pairs={{0,2},{1,3},{2,0},{3,1},{4,6},{5,7},{6,4},{7,5},{8,10},{9,11},{10,... | collective-permute-start | bytes 1572872 | tf_op jit(solution)/shard_map/ppermute | solution.py:47
  424.4 41.5 %collective-permute-start.45 = (bf16[256,2048]{1,0:T(8,128)(2,1)}, bf16[256,2048]{1,0:T(8,128)(2,1)S(1)}, u32[]{:S(2)}, u32[]{:S(2)}) collective-permute-start(bf16[256,2048]{1,0:T(8,128)(2,1)} %fusion.10), channel_id=1, source_target_pairs={{0,8},{4,12},{8,0},{12,4},{1,9},{5,13},{9,1},{13,5},{2,10},{6,14},... | collective-permute-start | bytes 3145736 | tf_op jit(solution)/shard_map/ppermute | solution.py:47
  442.0 32.1 %collective-permute-start.46 = (bf16[2,256,640]{2,1,0:T(8,128)(2,1)}, bf16[2,256,640]{2,1,0:T(8,128)(2,1)}, u32[]{:S(2)}, u32[]{:S(2)}) collective-permute-start(bf16[2,256,640]{2,1,0:T(8,128)(2,1)} %pad_maximum_fusion.13), channel_id=1, source_target_pairs={{0,1},{1,0},{2,3},{3,2},{4,5},{5,4},{6,7},{7,6},{8,9},{9,8},{10,11... | collective-permute-start | bytes 1966088 | tf_op jit(solution)/shard_map/ppermute | solution.py:47
  464.1 30.7 %collective-permute-start.50 = (bf16[64,1536]{0,1:T(8,128)(2,1)S(1)}, bf16[64,1536]{0,1:T(8,128)(2,1)S(1)}, u32[]{:S(2)}, u32[]{:S(2)}) collective-permute-start(bf16[64,1536]{0,1:T(8,128)(2,1)S(1)} %get-tuple-element.389), channel_id=1, source_target_pairs={{0,4},{4,0},{8,12},{12,8},{1,5},{5,1},{9,13},{13,9},{2,6},{6,2},{1... | collective-permute-start | bytes 589832 | tf_op jit(solution)/shard_map/ppermute | solution.py:47
  464.1 30.7 %collective-permute-start.51 = (bf16[64,1536]{0,1:T(8,128)(2,1)S(1)}, bf16[64,1536]{0,1:T(8,128)(2,1)S(1)}, u32[]{:S(2)}, u32[]{:S(2)}) collective-permute-start(bf16[64,1536]{0,1:T(8,128)(2,1)S(1)} %get-tuple-element.390), channel_id=1, source_target_pairs={{0,8},{4,12},{8,0},{12,4},{1,9},{5,13},{9,1},{13,5},{2,10},{6,14},... | collective-permute-start | bytes 589832 | tf_op jit(solution)/shard_map/ppermute | solution.py:47
  465.8 28.9 %collective-permute-start.52 = (bf16[64,1536]{0,1:T(8,128)(2,1)S(1)}, bf16[64,1536]{0,1:T(8,128)(2,1)S(1)}, u32[]{:S(2)}, u32[]{:S(2)}) collective-permute-start(bf16[64,1536]{0,1:T(8,128)(2,1)S(1)} %get-tuple-element.387), channel_id=1, source_target_pairs={{0,12},{4,8},{8,4},{12,0},{1,13},{5,9},{9,5},{13,1},{2,14},{6,10},... | collective-permute-start | bytes 589832 | tf_op jit(solution)/shard_map/ppermute | solution.py:47
  (113 other events, 1078.6 us)
Sparse Core Ops, SparseCore 0:
  32.2 34.6 all-gather.8
  68.5 26.9 all-gather.10
  97.0 45.4 all-gather.12
  144.5 79.4 all-gather.14

commit v5 on v3

--- a/solution.py
+++ b/solution.py
@@ -422,51 +422,58 @@
     return dot(high, ones) + dot(low, ones)
 
 
-def backward_kernel(
-    heads,
-    segp_ref,
-    segc_ref,
-    segr_ref,
-    mask_ref,
-    in_a_ref,
-    in_b_ref,
-    halo_ref,
-    weight_ref,
-    b_ref,
-    c_ref,
-    dt_ref,
-    rate_ref,
-    skip_ref,
-    y_ref,
-    prior_ref,
-    dy_ref,
-    din_ref,
-    dbc_ref,
-    ddt_ref,
-    drate_ref,
-    dsum_ref,
-    dcarry,
-    after_state,
-    keep_dy,
-    to_end_u,
-    slopes,
-    along,
-    ext,
-    dext,
-    wide_dt,
-    wide_keep,
-    wide_end,
-):
+def backward_kernel(heads, last, begins, *refs):
+    (
+        segp_ref,
+        segc_ref,
+        segr_ref,
+        mask_ref,
+        in_a_ref,
+        in_b_ref,
+        halo_ref,
+        weight_ref,
+        b_ref,
+        c_ref,
+        dt_ref,
+        rate_ref,
+        skip_ref,
+        y_ref,
+        prior_ref,
+        dy_ref,
+    ) = refs[:16]
+    rest = refs[16:] if begins else refs[24:]
+    din_ref, dbc_ref, ddt_ref, drate_ref, dsum_ref, carry_ref, tail_ref = rest[:7]
+    (
+        dcarry,
+        after_state,
+        keep_dy,
+        to_end_u,
+        slopes,
+        along,
+        ext,
+        dext,
+        wide_dt,
+        wide_keep,
+        wide_end,
+    ) = rest[7:]
     step = pl.program_id(0)
-    block = pl.num_programs(0) - 1 - step
+    block = last - step
 
     @pl.when(step == 0)
     def _():
-        dcarry[...] = jnp.zeros_like(dcarry)
-        after_state[...] = jnp.zeros_like(after_state)
-        drate_ref[...] = jnp.zeros_like(drate_ref)
-        dsum_ref[...] = jnp.zeros_like(dsum_ref)
-        dext[SPAN:] = jnp.zeros((HALO, dext.shape[1]), F32)
+        if begins:
+            dcarry[...] = jnp.zeros_like(dcarry)
+            after_state[...] = jnp.zeros_like(after_state)
+            drate_ref[...] = jnp.zeros_like(drate_ref)
+            dsum_ref[...] = jnp.zeros_like(dsum_ref)
+            dext[SPAN:] = jnp.zeros((HALO, dext.shape[1]), F32)
+        else:
+            drate_in, dsum_in, carry_in, tail_in, after_in = refs[16:21]
+            dcarry[...] = carry_in[...]
+            after_state[...] = after_in[0]
+            drate_ref[...] = drate_in[...]
+            dsum_ref[...] = dsum_in[...]
+            dext[SPAN:] = tail_in[...]
 
     ext[0:HALO] = halo_ref[0].astype(F32)
     half = in_b_ref.shape[1]
@@ -545,6 +552,11 @@
     dcarry[...] = wide_keep[SPAN - 1 : SPAN, :] * dcarry[...] + fresh
     after_state[...] = prior
 
+    @pl.when(step == pl.num_programs(0) - 1)
+    def _():
+        carry_ref[...] = dcarry[...]
+        tail_ref[...] = dext[SPAN:]
+
 
 def scan_specs(heads, at, in_widths):
     width = heads * HEADDIM
@@ -598,22 +610,43 @@
     )(*operands)
 
 
-def scan_backward(heads, blocks, operands, y, priors, dy):
+def scan_backward(heads, blocks, lowest, last, operands, y, priors, dy, before=None):
     rows, whole, ins, prior = scan_specs(
-        heads, lambda i: blocks - 1 - i, [operands[n].shape[1] for n in (4, 5)]
+        heads, lambda i: last - i, [operands[n].shape[1] for n in (4, 5)]
     )
     width = heads * HEADDIM
+    more, more_specs, aliases = [], [], {}
+    if before is not None:
+        more = list(before[3:]) + [priors] + list(before[:3])
+        more_specs = [
+            whole(1, LANES),
+            whole(8, width),
+            whole(STATE, width),
+            whole(HALO, width),
+            pl.BlockSpec((1, STATE, width), lambda i: (last + 1, 0, 0)),
+        ] + [pl.BlockSpec(memory_space=pl.ANY)] * 3
+        aliases = {len(ins) + 8 + n: n for n in range(3)}
     return call(
-        functools.partial(backward_kernel, heads),
-        grid=(blocks,),
-        in_specs=ins + [rows(width), prior, rows(width)],
-        out_specs=[rows(width), rows(2 * STATE), rows(LANES), whole(1, LANES), whole(8, width)],
+        functools.partial(backward_kernel, heads, last, before is None),
+        grid=(last - lowest + 1,),
+        in_specs=ins + [rows(width), prior, rows(width)] + more_specs,
+        out_specs=[
+            rows(width),
+            rows(2 * STATE),
+            rows(LANES),
+            whole(1, LANES),
+            whole(8, width),
+            whole(STATE, width),
+            whole(HALO, width),
+        ],
         out_shape=[
             jax.ShapeDtypeStruct((blocks * SPAN, width), BF),
             jax.ShapeDtypeStruct((blocks * SPAN, 2 * STATE), F32),
             jax.ShapeDtypeStruct((blocks * SPAN, LANES), F32),
             jax.ShapeDtypeStruct((1, LANES), F32),
             jax.ShapeDtypeStruct((8, width), F32),
+            jax.ShapeDtypeStruct((STATE, width), F32),
+            jax.ShapeDtypeStruct((HALO, width), F32),
         ],
         scratch_shapes=[
             pltpu.VMEM((STATE, width), F32),
@@ -628,8 +661,9 @@
             pltpu.VMEM((SPAN, width), F32),
             pltpu.VMEM((SPAN, width), F32),
         ],
+        input_output_aliases=aliases,
         name="scan_backward",
-    )(*operands, y, priors, dy)
+    )(*operands, y, priors, dy, *more)
 
 
 def as_columns(rows):
@@ -1133,9 +1167,15 @@
     dy = after(dy, out_sent)
     out_half = swapped(out_sent, "fsdp", 1)
 
-    dproj_s, dbc, ddt, drate, dsum = scan_backward(heads, blocks, operands, y, priors, dy)
-    dproj_s, dbc, out_half, shares[2], third = together(dproj_s, dbc, out_half, shares[2], third)
+    middle = blocks * 3 // 8
+    later = list(scan_backward(heads, blocks, middle, blocks - 1, operands, y, priors, dy))
+    carry, out_half = together(later[5], out_half)
     out_pair = fsdp_rest(out_kept, out_half)
+    later = later[:5] + [carry] + later[6:]
+    dproj_s, dbc, ddt, drate, dsum, _, _ = scan_backward(
+        heads, blocks, 0, middle - 1, operands, y, priors, dy, later
+    )
+    dproj_s, dbc, out_pair, shares[2], third = together(dproj_s, dbc, out_pair, shares[2], third)
 
     dbc = dbc.astype(BF)
     slices = reordered_by_xor([dbc[:, j * own_bc : (j + 1) * own_bc] for j in range(ns)], s)
@@ -1173,7 +1213,7 @@
     dxn = input_grad(dz, dproj_s, after(dproj_r, *right_other), full_z, full_a, full_b, ns, tok)
     pair = swapped(jnp.stack([picked(dxn, s ^ 1), picked(dxn, s ^ 3)]), "seq", 1)
 
-    dxn, z_half, left_got, out_pair = together(dxn, z_half, left_got, out_pair)
+    dxn, z_half, left_got = together(dxn, z_half, left_got)
     z_pair = fsdp_rest(z_kept, z_half)
     own_s = in_terms(after(dproj_s, dxn), d)
     left_kept, left_sent = fsdp_half(own_s[:, :, :half], left_got)

time: 501 us -> 524 us (1.046)
  waiting for transfers between devices: 129 us -> 159 us
  local copies, waits for them, and re-layouts: 64.7 us -> 59.1 us
    ppermute x62, waiting for transfers between devices: 86.5 us -> 116 us  [swapped(): return lax.ppermute(value, axis, pairs)]
    unnamed x161 -> x159, local copies, waits for them, and re-layouts: 21.4 us -> 16.8 us
    pallas_call x1 -> x2, Pallas kernels: 34.2 us -> 37.4 us  [scan_backward(): call(functools.partial(backward_kernel, heads, last, before is None), gri...]
  transfers between devices with their start and end apart: 66 -> 66, of which waited for: 23 -> 25; matrix products, arithmetic and copies ran while one was open for 19% -> 18% of each run, Pallas kernels for 32% -> 32%
where the time goes in v5:
time: 524 us; the launch traced here: 517 us
  Pallas kernels  167 us (32%)
  waiting for transfers between devices  159 us (30%)
  local copies, waits for them, and re-layouts  59.1 us (11%)
  other arithmetic  54 us (10%)
  starting transfers between devices  53.9 us (10%)
  between operations  15.9 us (3%)
  matrix products  8.88 us (2%)
    ppermute x62, waiting for transfers between devices, swapped(): return lax.ppermute(value, axis, pairs)  116 us
    ppermute x62, starting transfers between devices, swapped(): return lax.ppermute(value, axis, pairs)  53.7 us
    all_gather x4, waiting for transfers between devices, over_fsdp(): return lax.all_gather(chunk, 'fsdp', axis=0, tiled=False)  42.5 us
    pallas_call x2, Pallas kernels, scan_backward(): call(functools.partial(backward_kernel, heads, last, before is None), gri...  37.4 us
    pallas_call x7, Pallas kernels, row_terms(): call(functools.partial(terms_kernel, ns, nf), grid_spec=pltpu.PrefetchSca...  24.9 us
    unnamed x159, local copies, waits for them, and re-layouts  16.8 us
    pallas_call x1, Pallas kernels, shards(): call(functools.partial(products_kernel, where, plan, lanes, tok, ns, nd),...  16.4 us
    pallas_call x1, Pallas kernels, scan_forward(): call(functools.partial(forward_kernel, heads), grid=(blocks,), in_specs=i...  14.9 us
  transfers between devices with their start and end apart: 66, of which 25 were waited for; matrix products, arithmetic and copies ran while one was open for 18% of the time, Pallas kernels for 32%

profile of v5, /device:TPU:0, one launch (start us, length us, event | category | flops | bytes accessed | tf_op | source)
XLA Modules:
  0.0 517.3 jit_solution(17657369007647355953)
XLA Ops:
  24.2 5.6 %collective-permute-done.2.refs_3_ = bf16[64,2176]{1,0:T(8,128)(2,1)S(1)} collective-permute-done((bf16[64,2176]{1,0:T(8,128)(2,1)}, bf16[64,2176]{1,0:T(8,128)(2,1)S(1)}, u32[]{:S(2)}, u32[]{:S(2)}) %collective-permute-start.2) | collective-permute-done | bytes 278560 | tf_op jit(solution)/shard_map/ppermute | solution.py:47
  34.1 4.8 slice_bitcast_fusion
  39.8 4.5 slice_bitcast_fusion.2
  44.3 8.2 %collective-permute-done.4.refs_2_ = bf16[256,2048]{1,0:T(8,128)(2,1)S(1)} collective-permute-done((bf16[256,2048]{1,0:T(8,128)(2,1)}, bf16[256,2048]{1,0:T(8,128)(2,1)S(1)}, u32[]{:S(2)}, u32[]{:S(2)}) %collective-permute-start.4) | collective-permute-done | bytes 1048608 | tf_op jit(solution)/shard_map/ppermute | solution.py:47
  53.4 12.8 %all-gather.11.cloned.1.call-done = bf16[16,64,640]{2,1,0:T(8,128)(2,1)} async-done(((bf16[4,64,640]{2,1,0:T(8,128)(2,1)}), bf16[16,64,640]{2,1,0:T(8,128)(2,1)}) %all-gather.11.cloned.1.call-update) | async-done | bytes 1310736 | tf_op jit(solution)/shard_map/all_gather | solution.py:974
  74.5 20.3 %all-gather.9.cloned.1.call-done = bf16[16,64,512]{2,1,0:T(8,128)(2,1)} async-done(((bf16[4,64,512]{2,1,0:T(8,128)(2,1)}), bf16[16,64,512]{2,1,0:T(8,128)(2,1)}) %all-gather.9.cloned.1.call-update) | async-done | bytes 1048592 | tf_op jit(solution)/shard_map/all_gather | solution.py:974
  102.1 5.5 %filled.5 = bf16[4,256,2048]{2,1,0:T(8,128)(2,1)} custom-call(s32[4,3]{1,0:T(4,128)S(1)} %pad_add_fusion.index_ref, bf16[256,2048]{1,0:T(8,128)(2,1)} %fusion.2.refs_0_, bf16[256,2048]{1,0:T(8,128)(2,1)} %collective-permute-done.8.refs_1_, bf16[256,2048]{1,0:T(8,128)(2,1)S(1)} %copy-done.35, bf16[256,2048]{1,0:T(8,128)(2,1)} %collective-permute-done.9.refs_3_), custom_call_target="tpu_custom_call" | custom-call | flops 1 | bytes 1 | tf_op jit(solution)/shard_map/filled/pallas_call | solution.py:116
  107.6 5.6 %convolution_convert_fusion.in_a_ref.refs_4_ = bf16[1024,640]{1,0:T(8,128)(2,1)S(1)} fusion(bf16[1024,2048]{1,0:T(8,128)(2,1)} %bitcast.268, bf16[2048,640]{1,0:T(8,128)(2,1)S(1)} %bitcast.247), kind=kOutput, calls=%fused_computation.36 | convolution fusion | flops 2685009920 | bytes 8126464 | tf_op jit(solution)/shard_map/dot_general | solution.py:31
  118.3 6.4 %copy.211 = bf16[1024,2048]{0,1:T(8,128)(2,1)} copy(bf16[1024,2048]{1,0:T(8,128)(2,1)} %bitcast.269) | data formatting | bytes 8388608 | tf_op jit(solution)/shard_map/reshape | solution.py:999
  132.3 9.5 %all-gather.13.cloned.1.call-done = bf16[16,64,1024]{2,1,0:T(8,128)(2,1)} async-done(((bf16[4,64,1024]{2,1,0:T(8,128)(2,1)}), bf16[16,64,1024]{2,1,0:T(8,128)(2,1)}) %all-gather.13.cloned.1.call-update) | async-done | bytes 2097168 | tf_op jit(solution)/shard_map/all_gather | solution.py:974
  149.1 14.9 %scan_forward.1 = (f32[1024,1024]{1,0:T(8,128)}, f32[8,128,1024]{2,1,0:T(8,128)}) custom-call(s32[8]{0:T(128)S(1)} %pad_add_fusion.15.segp_ref.refs_0_, s32[1024,1]{1,0:T(8,128)S(1)} %copy.188.segc_ref.refs_1_, s32[1,1024]{1,0:T(1,128)S(1)} %bitcast.262, f32[1024,128]{1,0:T(8,128)S(1)} %pad.55.mask_ref.refs_3_, ...), custom_call_target="tpu_custom_call" | custom-call | flops 1 | bytes 1 | tf_op jit(solution)/shard_map/scan_forward/pallas_call | solution.py:592
  164.0 5.7 %collective-permute-done.16.refs_5_.refs_6_ = bf16[256,2048]{1,0:T(8,128)(2,1)} collective-permute-done((bf16[256,2048]{1,0:T(8,128)(2,1)}, bf16[256,2048]{1,0:T(8,128)(2,1)}, u32[]{:S(2)}, u32[]{:S(2)}) %collective-permute-start.16) | collective-permute-done | bytes 1048608 | tf_op jit(solution)/shard_map/ppermute | solution.py:47
  172.2 17.4 %collective-permute-done.17.refs_1_ = bf16[4,4,64,1024]{3,2,1,0:T(8,128)(2,1)} collective-permute-done((bf16[4,4,64,1024]{3,2,1,0:T(8,128)(2,1)}, bf16[4,4,64,1024]{3,2,1,0:T(8,128)(2,1)}, u32[]{:S(2)}, u32[]{:S(2)}) %collective-permute-start.17) | collective-permute-done | bytes 2097184 | tf_op jit(solution)/shard_map/ppermute | solution.py:47
  189.6 12.2 %gated.1 = (bf16[1024,1024]{1,0:T(8,128)(2,1)S(1)}, bf16[2048,1024]{1,0:T(8,128)(2,1)}, bf16[1024,1024]{1,0:T(8,128)(2,1)S(1)}, bf16[1024,1024]{1,0:T(8,128)(2,1)}, f32[8,1024]{1,0:T(8,128)S(1)}) custom-call(s32[2]{0:T(128)S(1)} %pad_add_fusion.16.here_ref, bf16[1024,2048]{1,0:T(8,128)(2,1)} %bitcast.270, f32[1024,1024]{1,0:T(8,128)} %get-tuple-element.184.y_ref.refs_13_, ...), custom_call_target="tpu_custom_call" | custom-call | flops 1 | bytes 1 | tf_op jit(solution)/shard_map/gated/pallas_call | solution.py:288
  208.8 4.8 collective-permute-done.20
  219.3 13.7 %upper.1 = (bf16[2,1024,2048]{2,1,0:T(8,128)(2,1)}, bf16[512,2048]{1,0:T(8,128)(2,1)}, bf16[256,2048]{1,0:T(8,128)(2,1)S(1)}, bf16[256,2048]{1,0:T(8,128)(2,1)}) custom-call(s32[2]{0:T(128)S(1)} %pad_add_fusion.16.here_ref, s32[2]{0:T(128)S(1)} %call_exported.0.range_ref, f32[2,4]{1,0:T(2,128)S(1)} %fusion.42.count_ref, f32[4,1024]{1,0:T(4,128)S(1)} %fusion.30.ratio_ref, ...), custom_call_target="tpu_custom_call" | custom-call | flops 1 | bytes 1 | tf_op jit(solution)/shard_map/upper/pallas_call | solution.py:1083
  234.9 16.4 %products.1 = (bf16[2,256,2048]{2,1,0:T(8,128)(2,1)}, bf16[2,256,2048]{2,1,0:T(8,128)(2,1)}, bf16[2,256,2048]{2,1,0:T(8,128)(2,1)}, bf16[2,256,2048]{2,1,0:T(8,1...) custom-call(s32[2]{0:T(128)S(1)} %pad_add_fusion.16.here_ref, f32[2,4]{1,0:T(2,128)S(1)} %fusion.42.count_ref, ...), custom_call_target="tpu_custom_call" | custom-call | flops 1 | bytes 1 | tf_op jit(solution)/shard_map/products/pallas_call | solution.py:1106
  259.2 12.3 %gate_backward.1 = (bf16[1024,1024]{1,0:T(8,128)(2,1)S(1)}, bf16[1024,1024]{1,0:T(8,128)(2,1)S(1)}, f32[8,1024]{1,0:T(8,128)S(1)}) custom-call(f32[2,4]{1,0:T(2,128)S(1)} %fusion.42.count_ref, bf16[2,1024,2048]{2,1,0:T(8,128)(2,1)} %get-tuple-element.205.upper_ref, bf16[1024,2048]{1,0:T(8,128)(2,1)} %get-tuple-element.208.w_ref, ...), custom_call_target="tpu_custom_call" | custom-call | flops 1 | bytes 1 | tf_op jit(solution)/shard_map/gate_backward/pallas_call | solution.py:1132
  272.8 6.3 %row_terms.7 = bf16[4,4,64,1024]{3,2,1,0:T(8,128)(2,1)} custom-call(s32[1]{0:T(128)} %bitcast.49.at_ref, bf16[2048,1024]{1,0:T(8,128)(2,1)} %bitcast.238, bf16[1024,1024]{1,0:T(8,128)(2,1)S(1)} %get-tuple-element.241.right_ref.dz_ref), custom_call_target="tpu_custom_call" | custom-call | flops 1 | bytes 1 | tf_op jit(solution)/shard_map/row_terms/pallas_call | solution.py:145
  279.1 5.4 %collective-permute-done.30 = bf16[256,2048]{1,0:T(8,128)(2,1)} collective-permute-done((bf16[256,2048]{1,0:T(8,128)(2,1)}, bf16[256,2048]{1,0:T(8,128)(2,1)}, u32[]{:S(2)}, u32[]{:S(2)}) %collective-permute-start.30) | collective-permute-done | bytes 1048608 | tf_op jit(solution)/shard_map/ppermute | solution.py:47
  291.2 22.5 %scan_backward.2 = (bf16[1024,1024]{1,0:T(8,128)(2,1)}, f32[1024,256]{1,0:T(8,128)S(1)}, f32[1024,128]{1,0:T(8,128)S(1)}, f32[1,128]{1,0:T(1,128)S(1)}, f32[8,10...) custom-call(s32[8]{0:T(128)S(1)} %pad_add_fusion.15.segp_ref.refs_0_, s32[1024,1]{1,0:T(8,128)S(1)} %copy-done.14, ...), custom_call_target="tpu_custom_call" | custom-call | flops 1 | bytes 1 | tf_op jit(solution)/shard_map/scan_backward/pallas_call | solution.py:629
  316.8 14.9 %scan_backward.3 = (bf16[1024,1024]{1,0:T(8,128)(2,1)}, f32[1024,256]{1,0:T(8,128)S(1)}, f32[1024,128]{1,0:T(8,128)S(1)}, f32[1,128]{1,0:T(1,128)S(1)}, f32[8,10...) custom-call(s32[8]{0:T(128)S(1)} %pad_add_fusion.15.segp_ref.refs_0_, ...), custom_call_target="tpu_custom_call", output_to_operand_aliasing={{0}: (21, {}), {1}: (22, {}), {2}: (23, {})} | custom-call | flops 1 | bytes 1 | tf_op jit(solution)/shard_map/scan_backward/pallas_call | solution.py:629
  331.7 4.5 collective-permute-done.34.refs_2_
  336.2 19.9 %collective-permute-done.35.refs_3_ = bf16[1,256,2048]{2,1,0:T(8,128)(2,1)S(1)} collective-permute-done((bf16[1,256,2048]{2,1,0:T(8,128)(2,1)}, bf16[1,256,2048]{2,1,0:T(8,128)(2,1)S(1)}, u32[]{:S(2)}, u32[]{:S(2)}) %collective-permute-start.35) | collective-permute-done | bytes 1048608 | tf_op jit(solution)/shard_map/ppermute | solution.py:47
  359.7 4.9 row_terms.8
  385.9 13.6 %input_grad.1 = bf16[4,256,2048]{2,1,0:T(8,128)(2,1)} custom-call(bf16[1024,1024]{1,0:T(8,128)(2,1)S(1)} %copy-done.6, bf16[1024,1024]{1,0:T(8,128)(2,1)S(1)} %copy-done.2, bf16[1024,128]{1,0:T(8,128)(2,1)S(1)} %get-tuple-element.254.right_ref.dr_ref, bf16[2048,1024]{1,0:T(8,128)(2,1)} %get-tuple-element.250.wz_ref, bf16[2048,640]{1,0:T(8,128)(2,1)} %bitcast.248, ...), custom_call_target="tpu_custom_call" | custom-call | flops 1 | bytes 1 | tf_op jit(solution)/shard_map/input_grad/pallas_call | solution.py:219
  407.1 4.9 row_terms.12
  422.5 12.7 %collective-permute-done.43 = bf16[2,256,512]{2,1,0:T(8,128)(2,1)S(1)} collective-permute-done((bf16[2,256,512]{2,1,0:T(8,128)(2,1)S(1)}, bf16[2,256,512]{2,1,0:T(8,128)(2,1)S(1)}, u32[]{:S(2)}, u32[]{:S(2)}) %collective-permute-start.43) | collective-permute-done | bytes 524320 | tf_op jit(solution)/shard_map/ppermute | solution.py:47
  440.2 8.2 %mixed.1 = bf16[4,256,2048]{2,1,0:T(8,128)(2,1)} custom-call(s32[2]{0:T(128)S(1)} %pad_add_fusion.16.here_ref, f32[4,8]{1,0:T(4,128)S(1)} %fusion.37.count_ref, f32[4,1024]{1,0:T(4,128)S(1)} %fusion.30.ratio_ref, bf16[256,2048]{1,0:T(8,128)(2,1)S(1)} %bitcast.245, bf16[2,256,2048]{2,1,0:T(8,128)(2,1)S(1)} %copy-done.29, ...), custom_call_target="tpu_custom_call" | custom-call | flops 1 | bytes 1 | tf_op jit(solution)/shard_map/mixed/pallas_call | solution.py:1242
  450.4 4.7 collective-permute-done.48
  475.8 5.8 %collective-permute-done.51 = bf16[64,1536]{0,1:T(8,128)(2,1)S(1)} collective-permute-done((bf16[64,1536]{0,1:T(8,128)(2,1)S(1)}, bf16[64,1536]{0,1:T(8,128)(2,1)S(1)}, u32[]{:S(2)}, u32[]{:S(2)}) %collective-permute-start.51) | collective-permute-done | bytes 196640 | tf_op jit(solution)/shard_map/ppermute | solution.py:47
  481.5 5.0 collective-permute-done.52
  (491 shorter events, 187.7 us)
Async XLA Ops:
  7.2 59.0 %all-gather.11.cloned.1.call-start = ((), (), s32[]{:S(2)}) async-start(), calls=%async_computation.1 | async-start | bytes 1638400 | tf_op jit(solution)/shard_map/all_gather | solution.py:974
  18.3 34.2 %collective-permute-start.4 = (bf16[256,2048]{1,0:T(8,128)(2,1)}, bf16[256,2048]{1,0:T(8,128)(2,1)S(1)}, u32[]{:S(2)}, u32[]{:S(2)}) collective-permute-start(bf16[256,2048]{1,0:T(8,128)(2,1)} %fusion.2.refs_0_), channel_id=1, source_target_pairs={{0,8},{4,12},{8,0},{12,4},{1,9},{5,13},{9,1},{13,5},{2,10},{6,14},... | collective-permute-start | bytes 3145736 | tf_op jit(solution)/shard_map/ppermute | solution.py:47
  20.0 24.2 %collective-permute-start.3 = (bf16[128,2048]{1,0:T(8,128)(2,1)}, bf16[128,2048]{1,0:T(8,128)(2,1)}, u32[]{:S(2)}, u32[]{:S(2)}) collective-permute-start(bf16[128,2048]{1,0:T(8,128)(2,1)} %param.28), channel_id=1, source_target_pairs={{0,16},{16,0},{1,17},{17,1},{2,18},{18,2},{3,19},{19,3},{4,20},{20... | collective-permute-start | bytes 1572872 | tf_op jit(solution)/shard_map/ppermute | solution.py:47
  31.4 63.3 %all-gather.9.cloned.1.call-start = ((), (), s32[]{:S(2)}) async-start(), calls=%async_computation | async-start | bytes 1310720 | tf_op jit(solution)/shard_map/all_gather | solution.py:974
  39.7 102.1 %all-gather.13.cloned.1.call-start = ((), (), s32[]{:S(2)}) async-start(), calls=%async_computation.2 | async-start | bytes 2621440 | tf_op jit(solution)/shard_map/all_gather | solution.py:974
  66.2 31.5 %collective-permute-start.7 = (bf16[2,256,2048]{2,1,0:T(8,128)(2,1)}, bf16[2,256,2048]{2,1,0:T(8,128)(2,1)}, u32[]{:S(2)}, u32[]{:S(2)}) collective-permute-start(bf16[2,256,2048]{2,1,0:T(8,128)(2,1)} %get-tuple-element.157), channel_id=1, source_target_pairs={{0,4},{4,0},{8,12},{12,8},{1,5},{5,1},{9,13},{13,9},{2,6},{6,2},{1... | collective-permute-start | bytes 6291464 | tf_op jit(solution)/shard_map/ppermute | solution.py:47
  66.2 31.5 %collective-permute-start.5 = (bf16[4,4,64,640]{3,2,1,0:T(8,128)(2,1)}, bf16[4,4,64,640]{3,2,1,0:T(8,128)(2,1)}, u32[]{:S(2)}, u32[]{:S(2)}) collective-permute-start(bf16[4,4,64,640]{3,2,1,0:T(8,128)(2,1)} %bitcast.255), channel_id=1, source_target_pairs={{0,16},{16,0},{1,17},{17,1},{2,18},{18,2},{3,19},{19,3},{4,20},{20... | collective-permute-start | bytes 3932168 | tf_op jit(solution)/shard_map/ppermute | solution.py:47
  67.9 26.8 %collective-permute-start.9 = (bf16[256,2048]{1,0:T(8,128)(2,1)}, bf16[256,2048]{1,0:T(8,128)(2,1)}, u32[]{:S(2)}, u32[]{:S(2)}) collective-permute-start(bf16[256,2048]{1,0:T(8,128)(2,1)} %copy-done.34), channel_id=1, source_target_pairs={{0,4},{4,0},{8,12},{12,8},{1,5},{5,1},{9,13},{13,9},{2,6},{6,2},{1... | collective-permute-start | bytes 3145736 | tf_op jit(solution)/shard_map/ppermute | solution.py:47
  68.2 26.5 %collective-permute-start.6 = (bf16[256,2048]{1,0:T(8,128)(2,1)}, bf16[256,2048]{1,0:T(8,128)(2,1)}, u32[]{:S(2)}, u32[]{:S(2)}) collective-permute-start(bf16[256,2048]{1,0:T(8,128)(2,1)} %get-tuple-element.155), channel_id=1, source_target_pairs={{0,8},{4,12},{8,0},{12,4},{1,9},{5,13},{9,1},{13,5},{2,10},{6,14},... | collective-permute-start | bytes 3145736 | tf_op jit(solution)/shard_map/ppermute | solution.py:47
  70.5 163.1 %all-gather.15.cloned.1.call-start = ((), (), s32[]{:S(2)}) async-start(), calls=%async_computation.3 | async-start | bytes 5242880 | tf_op jit(solution)/shard_map/all_gather | solution.py:974
  72.2 60.1 %collective-permute-start.13 = (bf16[2,256,2048]{2,1,0:T(8,128)(2,1)}, bf16[2,256,2048]{2,1,0:T(8,128)(2,1)}, u32[]{:S(2)}, u32[]{:S(2)}) collective-permute-start(bf16[2,256,2048]{2,1,0:T(8,128)(2,1)} %get-tuple-element.174), channel_id=1, source_target_pairs={{0,4},{4,0},{1,5},{5,1},{2,6},{6,2},{3,7},{7,3},{16,20},{20,16},{1... | collective-permute-start | bytes 6291464 | tf_op jit(solution)/shard_map/ppermute | solution.py:47
  97.7 27.0 %collective-permute-start.10 = (bf16[4,4,64,512]{3,2,1,0:T(8,128)(2,1)}, bf16[4,4,64,512]{3,2,1,0:T(8,128)(2,1)}, u32[]{:S(2)}, u32[]{:S(2)}) collective-permute-start(bf16[4,4,64,512]{3,2,1,0:T(8,128)(2,1)} %bitcast.257), channel_id=1, source_target_pairs={{0,16},{16,0},{1,17},{17,1},{2,18},{18,2},{3,19},{19,3},{4,20},{20... | collective-permute-start | bytes 3145736 | tf_op jit(solution)/shard_map/ppermute | solution.py:47
  113.2 28.6 %collective-permute-start.12 = (bf16[256,2048]{1,0:T(8,128)(2,1)}, bf16[256,2048]{1,0:T(8,128)(2,1)}, u32[]{:S(2)}, u32[]{:S(2)}) collective-permute-start(bf16[256,2048]{1,0:T(8,128)(2,1)} %collective-permute-done.6.refs_6_.refs_7_), channel_id=1, source_target_pairs={{0,4},{4,0},{8,12},{12,8},{1,5},{5,1},{9,13},{13,9},{2,6},{6,2},{1... | collective-permute-start | bytes 3145736 | tf_op jit(solution)/shard_map/ppermute | solution.py:47
  141.8 47.8 %collective-permute-start.17 = (bf16[4,4,64,1024]{3,2,1,0:T(8,128)(2,1)}, bf16[4,4,64,1024]{3,2,1,0:T(8,128)(2,1)}, u32[]{:S(2)}, u32[]{:S(2)}) collective-permute-start(bf16[4,4,64,1024]{3,2,1,0:T(8,128)(2,1)} %bitcast.281), channel_id=1, source_target_pairs={{0,16},{16,0},{1,17},{17,1},{2,18},{18,2},{3,19},{19,3},{4,20},{20... | collective-permute-start | bytes 6291464 | tf_op jit(solution)/shard_map/ppermute | solution.py:47
  143.3 26.4 %collective-permute-start.16 = (bf16[256,2048]{1,0:T(8,128)(2,1)}, bf16[256,2048]{1,0:T(8,128)(2,1)}, u32[]{:S(2)}, u32[]{:S(2)}) collective-permute-start(bf16[256,2048]{1,0:T(8,128)(2,1)} %get-tuple-element.183), channel_id=1, source_target_pairs={{0,8},{4,12},{8,0},{12,4},{1,9},{5,13},{9,1},{13,5},{2,10},{6,14},... | collective-permute-start | bytes 3145736 | tf_op jit(solution)/shard_map/ppermute | solution.py:47
  147.0 57.4 %collective-permute-start.18 = (bf16[256,2048]{1,0:T(8,128)(2,1)S(1)}, bf16[256,2048]{1,0:T(8,128)(2,1)}, u32[]{:S(2)}, u32[]{:S(2)}) collective-permute-start(bf16[256,2048]{1,0:T(8,128)(2,1)S(1)} %copy-done.55), channel_id=1, source_target_pairs={{8,0},{12,4},{9,1},{13,5},{10,2},{14,6},{11,3},{15,7},{24,16},{28,... | collective-permute-start | bytes 3145736 | tf_op jit(solution)/shard_map/ppermute | solution.py:47
  169.7 44.0 %collective-permute-start.22 = (bf16[256,2048]{1,0:T(8,128)(2,1)}, bf16[256,2048]{1,0:T(8,128)(2,1)S(1)}, u32[]{:S(2)}, u32[]{:S(2)}) collective-permute-start(bf16[256,2048]{1,0:T(8,128)(2,1)} %get-tuple-element.195), channel_id=1, source_target_pairs={{8,0},{12,4},{9,1},{13,5},{10,2},{14,6},{11,3},{15,7},{24,16},{28,... | collective-permute-start | bytes 3145736 | tf_op jit(solution)/shard_map/ppermute | solution.py:47
  233.0 25.6 %collective-permute-start.29 = (bf16[256,2048]{1,0:T(8,128)(2,1)S(1)}, bf16[256,2048]{1,0:T(8,128)(2,1)}, u32[]{:S(2)}, u32[]{:S(2)}) collective-permute-start(bf16[256,2048]{1,0:T(8,128)(2,1)S(1)} %get-tuple-element.211), channel_id=1, source_target_pairs={{0,16},{16,0},{1,17},{17,1},{2,18},{18,2},{3,19},{19,3},{4,20},{20... | collective-permute-start | bytes 3145736 | tf_op jit(solution)/shard_map/ppermute | solution.py:47
  258.6 25.9 %collective-permute-start.31 = (bf16[2,256,2048]{2,1,0:T(8,128)(2,1)}, bf16[2,256,2048]{2,1,0:T(8,128)(2,1)}, u32[]{:S(2)}, u32[]{:S(2)}) collective-permute-start(bf16[2,256,2048]{2,1,0:T(8,128)(2,1)} %get-tuple-element.218), channel_id=1, source_target_pairs={{0,4},{4,0},{8,12},{12,8},{1,5},{5,1},{9,13},{13,9},{2,6},{6,2},{1... | collective-permute-start | bytes 6291464 | tf_op jit(solution)/shard_map/ppermute | solution.py:47
  258.6 25.9 %collective-permute-start.30 = (bf16[256,2048]{1,0:T(8,128)(2,1)}, bf16[256,2048]{1,0:T(8,128)(2,1)}, u32[]{:S(2)}, u32[]{:S(2)}) collective-permute-start(bf16[256,2048]{1,0:T(8,128)(2,1)} %get-tuple-element.216), channel_id=1, source_target_pairs={{0,16},{16,0},{1,17},{17,1},{2,18},{18,2},{3,19},{19,3},{4,20},{20... | collective-permute-start | bytes 3145736 | tf_op jit(solution)/shard_map/ppermute | solution.py:47
  287.3 26.4 %collective-permute-start.32 = (bf16[2,128,2048]{2,1,0:T(8,128)(2,1)S(1)}, bf16[2,128,2048]{2,1,0:T(8,128)(2,1)S(1)}, u32[]{:S(2)}, u32[]{:S(2)}) collective-permute-start(bf16[2,128,2048]{2,1,0:T(8,128)(2,1)S(1)} %pad_maximum_fusion.11), channel_id=1, source_target_pairs={{0,1},{1,0},{2,3},{3,2},{4,5},{5,4},{6,7},{7,6},{8,9},{9,8},{10,11... | collective-permute-start | bytes 3145736 | tf_op jit(solution)/shard_map/ppermute | solution.py:47
  287.4 48.8 %collective-permute-start.34 = (bf16[2,256,2048]{2,1,0:T(8,128)(2,1)}, bf16[2,256,2048]{2,1,0:T(8,128)(2,1)S(1)}, u32[]{:S(2)}, u32[]{:S(2)}) collective-permute-start(bf16[2,256,2048]{2,1,0:T(8,128)(2,1)} %get-tuple-element.236), channel_id=1, source_target_pairs={{0,8},{4,12},{8,0},{12,4},{1,9},{5,13},{9,1},{13,5},{2,10},{6,14},... | collective-permute-start | bytes 6291464 | tf_op jit(solution)/shard_map/ppermute | solution.py:47
  290.4 74.2 %collective-permute-start.38 = (bf16[4,256,1024]{2,1,0:T(8,128)(2,1)}, bf16[4,256,1024]{2,1,0:T(8,128)(2,1)}, u32[]{:S(2)}, u32[]{:S(2)}) collective-permute-start(bf16[4,256,1024]{2,1,0:T(8,128)(2,1)} %bitcast.69), channel_id=1, source_target_pairs={{0,16},{16,0},{1,17},{17,1},{2,18},{18,2},{3,19},{19,3},{4,20},{20... | collective-permute-start | bytes 6291464 | tf_op jit(solution)/shard_map/ppermute | solution.py:47
  291.0 65.1 %collective-permute-start.35 = (bf16[1,256,2048]{2,1,0:T(8,128)(2,1)}, bf16[1,256,2048]{2,1,0:T(8,128)(2,1)S(1)}, u32[]{:S(2)}, u32[]{:S(2)}) collective-permute-start(bf16[1,256,2048]{2,1,0:T(8,128)(2,1)} %get-tuple-element.238), channel_id=1, source_target_pairs={{0,12},{4,8},{8,4},{12,0},{1,13},{5,9},{9,5},{13,1},{2,14},{6,10},... | collective-permute-start | bytes 3145736 | tf_op jit(solution)/shard_map/ppermute | solution.py:47
  315.1 41.1 %collective-permute-start.33 = (bf16[1,128,2048]{2,1,0:T(8,128)(2,1)S(1)}, bf16[1,128,2048]{2,1,0:T(8,128)(2,1)S(1)}, u32[]{:S(2)}, u32[]{:S(2)}) collective-permute-start(bf16[1,128,2048]{2,1,0:T(8,128)(2,1)S(1)} %get-tuple-element.415), channel_id=1, source_target_pairs={{0,2},{1,3},{2,0},{3,1},{4,6},{5,7},{6,4},{7,5},{8,10},{9,11},{10,... | collective-permute-start | bytes 1572872 | tf_op jit(solution)/shard_map/ppermute | solution.py:47
  375.2 31.8 %collective-permute-start.40 = (bf16[4,256,512]{2,1,0:T(8,128)(2,1)}, bf16[4,256,512]{2,1,0:T(8,128)(2,1)}, u32[]{:S(2)}, u32[]{:S(2)}) collective-permute-start(bf16[4,256,512]{2,1,0:T(8,128)(2,1)} %bitcast.75), channel_id=1, source_target_pairs={{0,16},{16,0},{1,17},{17,1},{2,18},{18,2},{3,19},{19,3},{4,20},{20... | collective-permute-start | bytes 3145736 | tf_op jit(solution)/shard_map/ppermute | solution.py:47
  375.8 31.3 %collective-permute-start.39 = (bf16[2,256,1024]{2,1,0:T(8,128)(2,1)}, bf16[2,256,1024]{2,1,0:T(8,128)(2,1)}, u32[]{:S(2)}, u32[]{:S(2)}) collective-permute-start(bf16[2,256,1024]{2,1,0:T(8,128)(2,1)} %pad_maximum_fusion.12), channel_id=1, source_target_pairs={{0,1},{1,0},{2,3},{3,2},{4,5},{5,4},{6,7},{7,6},{8,9},{9,8},{10,11... | collective-permute-start | bytes 3145736 | tf_op jit(solution)/shard_map/ppermute | solution.py:47
  403.8 31.5 %collective-permute-start.41 = (bf16[4,256,640]{2,1,0:T(8,128)(2,1)}, bf16[4,256,640]{2,1,0:T(8,128)(2,1)}, u32[]{:S(2)}, u32[]{:S(2)}) collective-permute-start(bf16[4,256,640]{2,1,0:T(8,128)(2,1)} %pad_maximum_fusion.3), channel_id=1, source_target_pairs={{0,16},{16,0},{1,17},{17,1},{2,18},{18,2},{3,19},{19,3},{4,20},{20... | collective-permute-start | bytes 3932168 | tf_op jit(solution)/shard_map/ppermute | solution.py:47
  405.4 34.8 %collective-permute-start.45 = (bf16[1,256,2048]{2,1,0:T(8,128)(2,1)}, bf16[1,256,2048]{2,1,0:T(8,128)(2,1)}, u32[]{:S(2)}, u32[]{:S(2)}) collective-permute-start(bf16[1,256,2048]{2,1,0:T(8,128)(2,1)} %get-tuple-element.262), channel_id=1, source_target_pairs={{0,12},{4,8},{8,4},{12,0},{1,13},{5,9},{9,5},{13,1},{2,14},{6,10},... | collective-permute-start | bytes 3145736 | tf_op jit(solution)/shard_map/ppermute | solution.py:47
  417.6 32.8 %collective-permute-start.47 = (bf16[1,256,1024]{2,1,0:T(8,128)(2,1)S(1)}, bf16[1,256,1024]{2,1,0:T(8,128)(2,1)S(1)}, u32[]{:S(2)}, u32[]{:S(2)}) collective-permute-start(bf16[1,256,1024]{2,1,0:T(8,128)(2,1)S(1)} %get-tuple-element.413), channel_id=1, source_target_pairs={{0,2},{1,3},{2,0},{3,1},{4,6},{5,7},{6,4},{7,5},{8,10},{9,11},{10,... | collective-permute-start | bytes 1572872 | tf_op jit(solution)/shard_map/ppermute | solution.py:47
  422.2 43.2 %collective-permute-start.46 = (bf16[256,2048]{1,0:T(8,128)(2,1)}, bf16[256,2048]{1,0:T(8,128)(2,1)S(1)}, u32[]{:S(2)}, u32[]{:S(2)}) collective-permute-start(bf16[256,2048]{1,0:T(8,128)(2,1)} %fusion.10), channel_id=1, source_target_pairs={{0,8},{4,12},{8,0},{12,4},{1,9},{5,13},{9,1},{13,5},{2,10},{6,14},... | collective-permute-start | bytes 3145736 | tf_op jit(solution)/shard_map/ppermute | solution.py:47
  439.3 26.1 %collective-permute-start.44 = (bf16[2,256,640]{2,1,0:T(8,128)(2,1)}, bf16[2,256,640]{2,1,0:T(8,128)(2,1)}, u32[]{:S(2)}, u32[]{:S(2)}) collective-permute-start(bf16[2,256,640]{2,1,0:T(8,128)(2,1)} %pad_maximum_fusion.13), channel_id=1, source_target_pairs={{0,1},{1,0},{2,3},{3,2},{4,5},{5,4},{6,7},{7,6},{8,9},{9,8},{10,11... | collective-permute-start | bytes 1966088 | tf_op jit(solution)/shard_map/ppermute | solution.py:47
  (112 other events, 903.3 us)
Sparse Core Ops, SparseCore 0:
  31.5 34.6 all-gather.10
  67.8 26.9 all-gather.8
  96.3 45.4 all-gather.12
  143.8 79.4 all-gather.14

commit v6 on v5

--- a/solution.py
+++ b/solution.py
@@ -1169,13 +1169,13 @@
 
     middle = blocks * 3 // 8
     later = list(scan_backward(heads, blocks, middle, blocks - 1, operands, y, priors, dy))
-    carry, out_half = together(later[5], out_half)
+    carry, out_half, shares[2] = together(later[5], out_half, shares[2])
     out_pair = fsdp_rest(out_kept, out_half)
     later = later[:5] + [carry] + later[6:]
     dproj_s, dbc, ddt, drate, dsum, _, _ = scan_backward(
         heads, blocks, 0, middle - 1, operands, y, priors, dy, later
     )
-    dproj_s, dbc, out_pair, shares[2], third = together(dproj_s, dbc, out_pair, shares[2], third)
+    dproj_s, dbc, out_pair = together(dproj_s, dbc, out_pair)
 
     dbc = dbc.astype(BF)
     slices = reordered_by_xor([dbc[:, j * own_bc : (j + 1) * own_bc] for j in range(ns)], s)
@@ -1213,7 +1213,7 @@
     dxn = input_grad(dz, dproj_s, after(dproj_r, *right_other), full_z, full_a, full_b, ns, tok)
     pair = swapped(jnp.stack([picked(dxn, s ^ 1), picked(dxn, s ^ 3)]), "seq", 1)
 
-    dxn, z_half, left_got = together(dxn, z_half, left_got)
+    dxn, z_half, left_got, third[0] = together(dxn, z_half, left_got, third[0])
     z_pair = fsdp_rest(z_kept, z_half)
     own_s = in_terms(after(dproj_s, dxn), d)
     left_kept, left_sent = fsdp_half(own_s[:, :, :half], left_got)

time: 524 us -> 505 us (0.964)
  waiting for transfers between devices: 159 us -> 144 us
    ppermute x62, waiting for transfers between devices: 116 us -> 101 us  [swapped(): return lax.ppermute(value, axis, pairs)]
    unnamed x159 -> x153, local copies, waits for them, and re-layouts: 16.8 us -> 15.4 us
  transfers between devices with their start and end apart: 66 -> 66, of which waited for: 25 -> 25; matrix products, arithmetic and copies ran while one was open for 18% -> 20% of each run, Pallas kernels for 32% -> 33%
where the time goes in v6:
time: 505 us; the launch traced here: 498 us
  Pallas kernels  167 us (33%)
  waiting for transfers between devices  144 us (29%)
  local copies, waits for them, and re-layouts  57.5 us (11%)
  other arithmetic  53.8 us (11%)
  starting transfers between devices  51.9 us (10%)
  between operations  15.9 us (3%)
  matrix products  8.89 us (2%)
    ppermute x62, waiting for transfers between devices, swapped(): return lax.ppermute(value, axis, pairs)  101 us
    ppermute x62, starting transfers between devices, swapped(): return lax.ppermute(value, axis, pairs)  51.7 us
    all_gather x4, waiting for transfers between devices, over_fsdp(): return lax.all_gather(chunk, 'fsdp', axis=0, tiled=False)  42.5 us
    pallas_call x2, Pallas kernels, scan_backward(): call(functools.partial(backward_kernel, heads, last, before is None), gri...  37.4 us
    pallas_call x7, Pallas kernels, row_terms(): call(functools.partial(terms_kernel, ns, nf), grid_spec=pltpu.PrefetchSca...  24.8 us
    pallas_call x1, Pallas kernels, shards(): call(functools.partial(products_kernel, where, plan, lanes, tok, ns, nd),...  16.4 us
    unnamed x153, local copies, waits for them, and re-layouts  15.4 us
    pallas_call x1, Pallas kernels, scan_forward(): call(functools.partial(forward_kernel, heads), grid=(blocks,), in_specs=i...  14.9 us
  transfers between devices with their start and end apart: 66, of which 25 were waited for; matrix products, arithmetic and copies ran while one was open for 20% of the time, Pallas kernels for 33%

profile of v6, /device:TPU:0, one launch (start us, length us, event | category | flops | bytes accessed | tf_op | source)
XLA Modules:
  0.0 498.1 jit_solution(7556396191048487000)
XLA Ops:
  24.2 5.6 %collective-permute-done.2.refs_3_ = bf16[64,2176]{1,0:T(8,128)(2,1)S(1)} collective-permute-done((bf16[64,2176]{1,0:T(8,128)(2,1)}, bf16[64,2176]{1,0:T(8,128)(2,1)S(1)}, u32[]{:S(2)}, u32[]{:S(2)}) %collective-permute-start.2) | collective-permute-done | bytes 278560 | tf_op jit(solution)/shard_map/ppermute | solution.py:47
  34.1 4.8 slice_bitcast_fusion
  39.7 4.5 slice_bitcast_fusion.2
  44.3 8.2 %collective-permute-done.4.refs_2_ = bf16[256,2048]{1,0:T(8,128)(2,1)S(1)} collective-permute-done((bf16[256,2048]{1,0:T(8,128)(2,1)}, bf16[256,2048]{1,0:T(8,128)(2,1)S(1)}, u32[]{:S(2)}, u32[]{:S(2)}) %collective-permute-start.4) | collective-permute-done | bytes 1048608 | tf_op jit(solution)/shard_map/ppermute | solution.py:47
  53.4 12.7 %all-gather.11.cloned.1.call-done = bf16[16,64,640]{2,1,0:T(8,128)(2,1)} async-done(((bf16[4,64,640]{2,1,0:T(8,128)(2,1)}), bf16[16,64,640]{2,1,0:T(8,128)(2,1)}) %all-gather.11.cloned.1.call-update) | async-done | bytes 1310736 | tf_op jit(solution)/shard_map/all_gather | solution.py:974
  74.4 20.3 %all-gather.9.cloned.1.call-done = bf16[16,64,512]{2,1,0:T(8,128)(2,1)} async-done(((bf16[4,64,512]{2,1,0:T(8,128)(2,1)}), bf16[16,64,512]{2,1,0:T(8,128)(2,1)}) %all-gather.9.cloned.1.call-update) | async-done | bytes 1048592 | tf_op jit(solution)/shard_map/all_gather | solution.py:974
  102.1 5.5 %filled.5 = bf16[4,256,2048]{2,1,0:T(8,128)(2,1)} custom-call(s32[4,3]{1,0:T(4,128)S(1)} %pad_add_fusion.index_ref, bf16[256,2048]{1,0:T(8,128)(2,1)} %fusion.2.refs_0_, bf16[256,2048]{1,0:T(8,128)(2,1)} %collective-permute-done.8.refs_1_, bf16[256,2048]{1,0:T(8,128)(2,1)S(1)} %copy-done.33, bf16[256,2048]{1,0:T(8,128)(2,1)} %collective-permute-done.9.refs_3_), custom_call_target="tpu_custom_call" | custom-call | flops 1 | bytes 1 | tf_op jit(solution)/shard_map/filled/pallas_call | solution.py:116
  107.6 5.6 %convolution_convert_fusion.in_a_ref.refs_4_ = bf16[1024,640]{1,0:T(8,128)(2,1)S(1)} fusion(bf16[1024,2048]{1,0:T(8,128)(2,1)} %bitcast.268, bf16[2048,640]{1,0:T(8,128)(2,1)S(1)} %bitcast.247), kind=kOutput, calls=%fused_computation.36 | convolution fusion | flops 2685009920 | bytes 8126464 | tf_op jit(solution)/shard_map/dot_general | solution.py:31
  118.3 6.4 %copy.211 = bf16[1024,2048]{0,1:T(8,128)(2,1)} copy(bf16[1024,2048]{1,0:T(8,128)(2,1)} %bitcast.269) | data formatting | bytes 8388608 | tf_op jit(solution)/shard_map/reshape | solution.py:999
  132.3 9.5 %all-gather.13.cloned.1.call-done = bf16[16,64,1024]{2,1,0:T(8,128)(2,1)} async-done(((bf16[4,64,1024]{2,1,0:T(8,128)(2,1)}), bf16[16,64,1024]{2,1,0:T(8,128)(2,1)}) %all-gather.13.cloned.1.call-update) | async-done | bytes 2097168 | tf_op jit(solution)/shard_map/all_gather | solution.py:974
  149.1 14.9 %scan_forward.1 = (f32[1024,1024]{1,0:T(8,128)}, f32[8,128,1024]{2,1,0:T(8,128)}) custom-call(s32[8]{0:T(128)S(1)} %pad_add_fusion.15.segp_ref.refs_0_, s32[1024,1]{1,0:T(8,128)S(1)} %copy.188.segc_ref.refs_1_, s32[1,1024]{1,0:T(1,128)S(1)} %bitcast.262, f32[1024,128]{1,0:T(8,128)S(1)} %pad.55.mask_ref.refs_3_, ...), custom_call_target="tpu_custom_call" | custom-call | flops 1 | bytes 1 | tf_op jit(solution)/shard_map/scan_forward/pallas_call | solution.py:592
  164.0 5.7 %collective-permute-done.16.refs_5_.refs_6_ = bf16[256,2048]{1,0:T(8,128)(2,1)} collective-permute-done((bf16[256,2048]{1,0:T(8,128)(2,1)}, bf16[256,2048]{1,0:T(8,128)(2,1)}, u32[]{:S(2)}, u32[]{:S(2)}) %collective-permute-start.16) | collective-permute-done | bytes 1048608 | tf_op jit(solution)/shard_map/ppermute | solution.py:47
  172.2 17.4 %collective-permute-done.17.refs_1_ = bf16[4,4,64,1024]{3,2,1,0:T(8,128)(2,1)} collective-permute-done((bf16[4,4,64,1024]{3,2,1,0:T(8,128)(2,1)}, bf16[4,4,64,1024]{3,2,1,0:T(8,128)(2,1)}, u32[]{:S(2)}, u32[]{:S(2)}) %collective-permute-start.17) | collective-permute-done | bytes 2097184 | tf_op jit(solution)/shard_map/ppermute | solution.py:47
  189.5 12.2 %gated.1 = (bf16[1024,1024]{1,0:T(8,128)(2,1)S(1)}, bf16[2048,1024]{1,0:T(8,128)(2,1)}, bf16[1024,1024]{1,0:T(8,128)(2,1)S(1)}, bf16[1024,1024]{1,0:T(8,128)(2,1)}, f32[8,1024]{1,0:T(8,128)S(1)}) custom-call(s32[2]{0:T(128)S(1)} %pad_add_fusion.16.here_ref, bf16[1024,2048]{1,0:T(8,128)(2,1)} %bitcast.270, f32[1024,1024]{1,0:T(8,128)} %get-tuple-element.183.y_ref.refs_13_, ...), custom_call_target="tpu_custom_call" | custom-call | flops 1 | bytes 1 | tf_op jit(solution)/shard_map/gated/pallas_call | solution.py:288
  208.8 4.8 collective-permute-done.20
  219.3 13.7 %upper.1 = (bf16[2,1024,2048]{2,1,0:T(8,128)(2,1)}, bf16[512,2048]{1,0:T(8,128)(2,1)}, bf16[256,2048]{1,0:T(8,128)(2,1)S(1)}, bf16[256,2048]{1,0:T(8,128)(2,1)}) custom-call(s32[2]{0:T(128)S(1)} %pad_add_fusion.16.here_ref, s32[2]{0:T(128)S(1)} %call_exported.0.range_ref, f32[2,4]{1,0:T(2,128)S(1)} %fusion.42.count_ref, f32[4,1024]{1,0:T(4,128)S(1)} %fusion.30.ratio_ref, ...), custom_call_target="tpu_custom_call" | custom-call | flops 1 | bytes 1 | tf_op jit(solution)/shard_map/upper/pallas_call | solution.py:1083
  234.9 16.4 %products.1 = (bf16[2,256,2048]{2,1,0:T(8,128)(2,1)}, bf16[2,256,2048]{2,1,0:T(8,128)(2,1)}, bf16[2,256,2048]{2,1,0:T(8,128)(2,1)}, bf16[2,256,2048]{2,1,0:T(8,1...) custom-call(s32[2]{0:T(128)S(1)} %pad_add_fusion.16.here_ref, f32[2,4]{1,0:T(2,128)S(1)} %fusion.42.count_ref, ...), custom_call_target="tpu_custom_call" | custom-call | flops 1 | bytes 1 | tf_op jit(solution)/shard_map/products/pallas_call | solution.py:1106
  259.2 12.3 %gate_backward.1 = (bf16[1024,1024]{1,0:T(8,128)(2,1)S(1)}, bf16[1024,1024]{1,0:T(8,128)(2,1)S(1)}, f32[8,1024]{1,0:T(8,128)S(1)}) custom-call(f32[2,4]{1,0:T(2,128)S(1)} %fusion.42.count_ref, bf16[2,1024,2048]{2,1,0:T(8,128)(2,1)} %get-tuple-element.204.upper_ref, bf16[1024,2048]{1,0:T(8,128)(2,1)} %get-tuple-element.207.w_ref, ...), custom_call_target="tpu_custom_call" | custom-call | flops 1 | bytes 1 | tf_op jit(solution)/shard_map/gate_backward/pallas_call | solution.py:1132
  272.8 6.3 %row_terms.7 = bf16[4,4,64,1024]{3,2,1,0:T(8,128)(2,1)} custom-call(s32[1]{0:T(128)} %bitcast.49.at_ref, bf16[2048,1024]{1,0:T(8,128)(2,1)} %bitcast.238, bf16[1024,1024]{1,0:T(8,128)(2,1)S(1)} %get-tuple-element.238.right_ref.dz_ref), custom_call_target="tpu_custom_call" | custom-call | flops 1 | bytes 1 | tf_op jit(solution)/shard_map/row_terms/pallas_call | solution.py:145
  279.1 5.4 %collective-permute-done.30 = bf16[256,2048]{1,0:T(8,128)(2,1)} collective-permute-done((bf16[256,2048]{1,0:T(8,128)(2,1)}, bf16[256,2048]{1,0:T(8,128)(2,1)}, u32[]{:S(2)}, u32[]{:S(2)}) %collective-permute-start.30) | collective-permute-done | bytes 1048608 | tf_op jit(solution)/shard_map/ppermute | solution.py:47
  289.1 22.5 %scan_backward.2 = (bf16[1024,1024]{1,0:T(8,128)(2,1)}, f32[1024,256]{1,0:T(8,128)S(1)}, f32[1024,128]{1,0:T(8,128)S(1)}, f32[1,128]{1,0:T(1,128)S(1)}, f32[8,10...) custom-call(s32[8]{0:T(128)S(1)} %pad_add_fusion.15.segp_ref.refs_0_, s32[1024,1]{1,0:T(8,128)S(1)} %copy-done.14, ...), custom_call_target="tpu_custom_call" | custom-call | flops 1 | bytes 1 | tf_op jit(solution)/shard_map/scan_backward/pallas_call | solution.py:629
  316.1 14.9 %scan_backward.3 = (bf16[1024,1024]{1,0:T(8,128)(2,1)}, f32[1024,256]{1,0:T(8,128)S(1)}, f32[1024,128]{1,0:T(8,128)S(1)}, f32[1,128]{1,0:T(1,128)S(1)}, f32[8,10...) custom-call(s32[8]{0:T(128)S(1)} %pad_add_fusion.15.segp_ref.refs_0_, ...), custom_call_target="tpu_custom_call", output_to_operand_aliasing={{0}: (21, {}), {1}: (22, {}), {2}: (23, {})} | custom-call | flops 1 | bytes 1 | tf_op jit(solution)/shard_map/scan_backward/pallas_call | solution.py:629
  331.0 7.6 %collective-permute-done.34 = bf16[1,128,2048]{2,1,0:T(8,128)(2,1)S(1)} collective-permute-done((bf16[1,128,2048]{2,1,0:T(8,128)(2,1)S(1)}, bf16[1,128,2048]{2,1,0:T(8,128)(2,1)S(1)}, u32[]{:S(2)}, u32[]{:S(2)}) %collective-permute-start.34) | collective-permute-done | bytes 524320 | tf_op jit(solution)/shard_map/ppermute | solution.py:47
  340.8 4.9 row_terms.8
  351.9 4.1 row_terms.9
  365.4 13.6 %input_grad.1 = bf16[4,256,2048]{2,1,0:T(8,128)(2,1)} custom-call(bf16[1024,1024]{1,0:T(8,128)(2,1)S(1)} %copy-done.6, bf16[1024,1024]{1,0:T(8,128)(2,1)S(1)} %copy-done.2, bf16[1024,128]{1,0:T(8,128)(2,1)S(1)} %get-tuple-element.253.right_ref.dr_ref, bf16[2048,1024]{1,0:T(8,128)(2,1)} %get-tuple-element.247.wz_ref, bf16[2048,640]{1,0:T(8,128)(2,1)} %bitcast.248, ...), custom_call_target="tpu_custom_call" | custom-call | flops 1 | bytes 1 | tf_op jit(solution)/shard_map/input_grad/pallas_call | solution.py:219
  386.5 4.9 row_terms.12
  402.3 12.4 %collective-permute-done.43 = bf16[2,256,512]{2,1,0:T(8,128)(2,1)S(1)} collective-permute-done((bf16[2,256,512]{2,1,0:T(8,128)(2,1)S(1)}, bf16[2,256,512]{2,1,0:T(8,128)(2,1)S(1)}, u32[]{:S(2)}, u32[]{:S(2)}) %collective-permute-start.43) | collective-permute-done | bytes 524320 | tf_op jit(solution)/shard_map/ppermute | solution.py:47
  420.3 8.2 %mixed.1 = bf16[4,256,2048]{2,1,0:T(8,128)(2,1)} custom-call(s32[2]{0:T(128)S(1)} %pad_add_fusion.16.here_ref, f32[4,8]{1,0:T(4,128)S(1)} %fusion.37.count_ref, f32[4,1024]{1,0:T(4,128)S(1)} %fusion.30.ratio_ref, bf16[256,2048]{1,0:T(8,128)(2,1)S(1)} %bitcast.245, bf16[2,256,2048]{2,1,0:T(8,128)(2,1)S(1)} %copy-done.29, ...), custom_call_target="tpu_custom_call" | custom-call | flops 1 | bytes 1 | tf_op jit(solution)/shard_map/mixed/pallas_call | solution.py:1242
  431.5 4.7 collective-permute-done.48
  456.3 6.2 %collective-permute-done.51 = bf16[64,1536]{0,1:T(8,128)(2,1)S(1)} collective-permute-done((bf16[64,1536]{0,1:T(8,128)(2,1)S(1)}, bf16[64,1536]{0,1:T(8,128)(2,1)S(1)}, u32[]{:S(2)}, u32[]{:S(2)}) %collective-permute-start.51) | collective-permute-done | bytes 196640 | tf_op jit(solution)/shard_map/ppermute | solution.py:47
  462.6 4.8 collective-permute-done.52
  (485 shorter events, 181.3 us)
Async XLA Ops:
  7.2 59.0 %all-gather.11.cloned.1.call-start = ((), (), s32[]{:S(2)}) async-start(), calls=%async_computation.1 | async-start | bytes 1638400 | tf_op jit(solution)/shard_map/all_gather | solution.py:974
  18.3 34.2 %collective-permute-start.4 = (bf16[256,2048]{1,0:T(8,128)(2,1)}, bf16[256,2048]{1,0:T(8,128)(2,1)S(1)}, u32[]{:S(2)}, u32[]{:S(2)}) collective-permute-start(bf16[256,2048]{1,0:T(8,128)(2,1)} %fusion.2.refs_0_), channel_id=1, source_target_pairs={{0,8},{4,12},{8,0},{12,4},{1,9},{5,13},{9,1},{13,5},{2,10},{6,14},... | collective-permute-start | bytes 3145736 | tf_op jit(solution)/shard_map/ppermute | solution.py:47
  20.0 24.2 %collective-permute-start.3 = (bf16[128,2048]{1,0:T(8,128)(2,1)}, bf16[128,2048]{1,0:T(8,128)(2,1)}, u32[]{:S(2)}, u32[]{:S(2)}) collective-permute-start(bf16[128,2048]{1,0:T(8,128)(2,1)} %param.28), channel_id=1, source_target_pairs={{0,16},{16,0},{1,17},{17,1},{2,18},{18,2},{3,19},{19,3},{4,20},{20... | collective-permute-start | bytes 1572872 | tf_op jit(solution)/shard_map/ppermute | solution.py:47
  31.4 63.3 %all-gather.9.cloned.1.call-start = ((), (), s32[]{:S(2)}) async-start(), calls=%async_computation | async-start | bytes 1310720 | tf_op jit(solution)/shard_map/all_gather | solution.py:974
  39.7 102.1 %all-gather.13.cloned.1.call-start = ((), (), s32[]{:S(2)}) async-start(), calls=%async_computation.2 | async-start | bytes 2621440 | tf_op jit(solution)/shard_map/all_gather | solution.py:974
  66.2 31.5 %collective-permute-start.7 = (bf16[2,256,2048]{2,1,0:T(8,128)(2,1)}, bf16[2,256,2048]{2,1,0:T(8,128)(2,1)}, u32[]{:S(2)}, u32[]{:S(2)}) collective-permute-start(bf16[2,256,2048]{2,1,0:T(8,128)(2,1)} %get-tuple-element.156), channel_id=1, source_target_pairs={{0,4},{4,0},{8,12},{12,8},{1,5},{5,1},{9,13},{13,9},{2,6},{6,2},{1... | collective-permute-start | bytes 6291464 | tf_op jit(solution)/shard_map/ppermute | solution.py:47
  66.2 31.5 %collective-permute-start.5 = (bf16[4,4,64,640]{3,2,1,0:T(8,128)(2,1)}, bf16[4,4,64,640]{3,2,1,0:T(8,128)(2,1)}, u32[]{:S(2)}, u32[]{:S(2)}) collective-permute-start(bf16[4,4,64,640]{3,2,1,0:T(8,128)(2,1)} %bitcast.255), channel_id=1, source_target_pairs={{0,16},{16,0},{1,17},{17,1},{2,18},{18,2},{3,19},{19,3},{4,20},{20... | collective-permute-start | bytes 3932168 | tf_op jit(solution)/shard_map/ppermute | solution.py:47
  67.9 26.8 %collective-permute-start.9 = (bf16[256,2048]{1,0:T(8,128)(2,1)}, bf16[256,2048]{1,0:T(8,128)(2,1)}, u32[]{:S(2)}, u32[]{:S(2)}) collective-permute-start(bf16[256,2048]{1,0:T(8,128)(2,1)} %copy-done.32), channel_id=1, source_target_pairs={{0,4},{4,0},{8,12},{12,8},{1,5},{5,1},{9,13},{13,9},{2,6},{6,2},{1... | collective-permute-start | bytes 3145736 | tf_op jit(solution)/shard_map/ppermute | solution.py:47
  68.2 26.5 %collective-permute-start.6 = (bf16[256,2048]{1,0:T(8,128)(2,1)}, bf16[256,2048]{1,0:T(8,128)(2,1)}, u32[]{:S(2)}, u32[]{:S(2)}) collective-permute-start(bf16[256,2048]{1,0:T(8,128)(2,1)} %get-tuple-element.154), channel_id=1, source_target_pairs={{0,8},{4,12},{8,0},{12,4},{1,9},{5,13},{9,1},{13,5},{2,10},{6,14},... | collective-permute-start | bytes 3145736 | tf_op jit(solution)/shard_map/ppermute | solution.py:47
  70.5 163.1 %all-gather.15.cloned.1.call-start = ((), (), s32[]{:S(2)}) async-start(), calls=%async_computation.3 | async-start | bytes 5242880 | tf_op jit(solution)/shard_map/all_gather | solution.py:974
  72.2 60.1 %collective-permute-start.13 = (bf16[2,256,2048]{2,1,0:T(8,128)(2,1)}, bf16[2,256,2048]{2,1,0:T(8,128)(2,1)}, u32[]{:S(2)}, u32[]{:S(2)}) collective-permute-start(bf16[2,256,2048]{2,1,0:T(8,128)(2,1)} %get-tuple-element.173), channel_id=1, source_target_pairs={{0,4},{4,0},{1,5},{5,1},{2,6},{6,2},{3,7},{7,3},{16,20},{20,16},{1... | collective-permute-start | bytes 6291464 | tf_op jit(solution)/shard_map/ppermute | solution.py:47
  97.7 27.0 %collective-permute-start.10 = (bf16[4,4,64,512]{3,2,1,0:T(8,128)(2,1)}, bf16[4,4,64,512]{3,2,1,0:T(8,128)(2,1)}, u32[]{:S(2)}, u32[]{:S(2)}) collective-permute-start(bf16[4,4,64,512]{3,2,1,0:T(8,128)(2,1)} %bitcast.257), channel_id=1, source_target_pairs={{0,16},{16,0},{1,17},{17,1},{2,18},{18,2},{3,19},{19,3},{4,20},{20... | collective-permute-start | bytes 3145736 | tf_op jit(solution)/shard_map/ppermute | solution.py:47
  113.2 28.6 %collective-permute-start.12 = (bf16[256,2048]{1,0:T(8,128)(2,1)}, bf16[256,2048]{1,0:T(8,128)(2,1)}, u32[]{:S(2)}, u32[]{:S(2)}) collective-permute-start(bf16[256,2048]{1,0:T(8,128)(2,1)} %collective-permute-done.6.refs_6_.refs_7_), channel_id=1, source_target_pairs={{0,4},{4,0},{8,12},{12,8},{1,5},{5,1},{9,13},{13,9},{2,6},{6,2},{1... | collective-permute-start | bytes 3145736 | tf_op jit(solution)/shard_map/ppermute | solution.py:47
  141.8 47.8 %collective-permute-start.17 = (bf16[4,4,64,1024]{3,2,1,0:T(8,128)(2,1)}, bf16[4,4,64,1024]{3,2,1,0:T(8,128)(2,1)}, u32[]{:S(2)}, u32[]{:S(2)}) collective-permute-start(bf16[4,4,64,1024]{3,2,1,0:T(8,128)(2,1)} %bitcast.281), channel_id=1, source_target_pairs={{0,16},{16,0},{1,17},{17,1},{2,18},{18,2},{3,19},{19,3},{4,20},{20... | collective-permute-start | bytes 6291464 | tf_op jit(solution)/shard_map/ppermute | solution.py:47
  143.3 26.4 %collective-permute-start.16 = (bf16[256,2048]{1,0:T(8,128)(2,1)}, bf16[256,2048]{1,0:T(8,128)(2,1)}, u32[]{:S(2)}, u32[]{:S(2)}) collective-permute-start(bf16[256,2048]{1,0:T(8,128)(2,1)} %get-tuple-element.182), channel_id=1, source_target_pairs={{0,8},{4,12},{8,0},{12,4},{1,9},{5,13},{9,1},{13,5},{2,10},{6,14},... | collective-permute-start | bytes 3145736 | tf_op jit(solution)/shard_map/ppermute | solution.py:47
  147.0 57.4 %collective-permute-start.18 = (bf16[256,2048]{1,0:T(8,128)(2,1)S(1)}, bf16[256,2048]{1,0:T(8,128)(2,1)}, u32[]{:S(2)}, u32[]{:S(2)}) collective-permute-start(bf16[256,2048]{1,0:T(8,128)(2,1)S(1)} %copy-done.52), channel_id=1, source_target_pairs={{8,0},{12,4},{9,1},{13,5},{10,2},{14,6},{11,3},{15,7},{24,16},{28,... | collective-permute-start | bytes 3145736 | tf_op jit(solution)/shard_map/ppermute | solution.py:47
  169.7 44.0 %collective-permute-start.22 = (bf16[256,2048]{1,0:T(8,128)(2,1)}, bf16[256,2048]{1,0:T(8,128)(2,1)S(1)}, u32[]{:S(2)}, u32[]{:S(2)}) collective-permute-start(bf16[256,2048]{1,0:T(8,128)(2,1)} %get-tuple-element.194), channel_id=1, source_target_pairs={{8,0},{12,4},{9,1},{13,5},{10,2},{14,6},{11,3},{15,7},{24,16},{28,... | collective-permute-start | bytes 3145736 | tf_op jit(solution)/shard_map/ppermute | solution.py:47
  233.0 25.6 %collective-permute-start.29 = (bf16[256,2048]{1,0:T(8,128)(2,1)S(1)}, bf16[256,2048]{1,0:T(8,128)(2,1)}, u32[]{:S(2)}, u32[]{:S(2)}) collective-permute-start(bf16[256,2048]{1,0:T(8,128)(2,1)S(1)} %get-tuple-element.210), channel_id=1, source_target_pairs={{0,16},{16,0},{1,17},{17,1},{2,18},{18,2},{3,19},{19,3},{4,20},{20... | collective-permute-start | bytes 3145736 | tf_op jit(solution)/shard_map/ppermute | solution.py:47
  258.6 25.9 %collective-permute-start.31 = (bf16[2,256,2048]{2,1,0:T(8,128)(2,1)}, bf16[2,256,2048]{2,1,0:T(8,128)(2,1)}, u32[]{:S(2)}, u32[]{:S(2)}) collective-permute-start(bf16[2,256,2048]{2,1,0:T(8,128)(2,1)} %get-tuple-element.217), channel_id=1, source_target_pairs={{0,4},{4,0},{8,12},{12,8},{1,5},{5,1},{9,13},{13,9},{2,6},{6,2},{1... | collective-permute-start | bytes 6291464 | tf_op jit(solution)/shard_map/ppermute | solution.py:47
  258.6 25.9 %collective-permute-start.30 = (bf16[256,2048]{1,0:T(8,128)(2,1)}, bf16[256,2048]{1,0:T(8,128)(2,1)}, u32[]{:S(2)}, u32[]{:S(2)}) collective-permute-start(bf16[256,2048]{1,0:T(8,128)(2,1)} %get-tuple-element.215), channel_id=1, source_target_pairs={{0,16},{16,0},{1,17},{17,1},{2,18},{18,2},{3,19},{19,3},{4,20},{20... | collective-permute-start | bytes 3145736 | tf_op jit(solution)/shard_map/ppermute | solution.py:47
  259.2 52.4 %collective-permute-start.33 = (bf16[2,256,2048]{2,1,0:T(8,128)(2,1)}, bf16[2,256,2048]{2,1,0:T(8,128)(2,1)}, u32[]{:S(2)}, u32[]{:S(2)}) collective-permute-start(bf16[2,256,2048]{2,1,0:T(8,128)(2,1)} %get-tuple-element.227), channel_id=1, source_target_pairs={{0,8},{4,12},{8,0},{12,4},{1,9},{5,13},{9,1},{13,5},{2,10},{6,14},... | collective-permute-start | bytes 6291464 | tf_op jit(solution)/shard_map/ppermute | solution.py:47
  287.4 24.9 %collective-permute-start.32 = (bf16[2,128,2048]{2,1,0:T(8,128)(2,1)S(1)}, bf16[2,128,2048]{2,1,0:T(8,128)(2,1)S(1)}, u32[]{:S(2)}, u32[]{:S(2)}) collective-permute-start(bf16[2,128,2048]{2,1,0:T(8,128)(2,1)S(1)} %pad_maximum_fusion.11), channel_id=1, source_target_pairs={{0,1},{1,0},{2,3},{3,2},{4,5},{5,4},{6,7},{7,6},{8,9},{9,8},{10,11... | collective-permute-start | bytes 3145736 | tf_op jit(solution)/shard_map/ppermute | solution.py:47
  288.3 57.4 %collective-permute-start.37 = (bf16[4,256,1024]{2,1,0:T(8,128)(2,1)}, bf16[4,256,1024]{2,1,0:T(8,128)(2,1)}, u32[]{:S(2)}, u32[]{:S(2)}) collective-permute-start(bf16[4,256,1024]{2,1,0:T(8,128)(2,1)} %bitcast.69), channel_id=1, source_target_pairs={{0,16},{16,0},{1,17},{17,1},{2,18},{18,2},{3,19},{19,3},{4,20},{20... | collective-permute-start | bytes 6291464 | tf_op jit(solution)/shard_map/ppermute | solution.py:47
  313.5 25.1 %collective-permute-start.34 = (bf16[1,128,2048]{2,1,0:T(8,128)(2,1)S(1)}, bf16[1,128,2048]{2,1,0:T(8,128)(2,1)S(1)}, u32[]{:S(2)}, u32[]{:S(2)}) collective-permute-start(bf16[1,128,2048]{2,1,0:T(8,128)(2,1)S(1)} %get-tuple-element.413), channel_id=1, source_target_pairs={{0,2},{1,3},{2,0},{3,1},{4,6},{5,7},{6,4},{7,5},{8,10},{9,11},{10,... | collective-permute-start | bytes 1572872 | tf_op jit(solution)/shard_map/ppermute | solution.py:47
  316.1 68.7 %collective-permute-start.40 = (bf16[1,256,2048]{2,1,0:T(8,128)(2,1)}, bf16[1,256,2048]{2,1,0:T(8,128)(2,1)}, u32[]{:S(2)}, u32[]{:S(2)}) collective-permute-start(bf16[1,256,2048]{2,1,0:T(8,128)(2,1)} %get-tuple-element.249), channel_id=1, source_target_pairs={{0,12},{4,8},{8,4},{12,0},{1,13},{5,9},{9,5},{13,1},{2,14},{6,10},... | collective-permute-start | bytes 3145736 | tf_op jit(solution)/shard_map/ppermute | solution.py:47
  356.0 30.5 %collective-permute-start.39 = (bf16[4,256,512]{2,1,0:T(8,128)(2,1)}, bf16[4,256,512]{2,1,0:T(8,128)(2,1)}, u32[]{:S(2)}, u32[]{:S(2)}) collective-permute-start(bf16[4,256,512]{2,1,0:T(8,128)(2,1)} %bitcast.75), channel_id=1, source_target_pairs={{0,16},{16,0},{1,17},{17,1},{2,18},{18,2},{3,19},{19,3},{4,20},{20... | collective-permute-start | bytes 3145736 | tf_op jit(solution)/shard_map/ppermute | solution.py:47
  357.0 29.5 %collective-permute-start.38 = (bf16[2,256,1024]{2,1,0:T(8,128)(2,1)}, bf16[2,256,1024]{2,1,0:T(8,128)(2,1)}, u32[]{:S(2)}, u32[]{:S(2)}) collective-permute-start(bf16[2,256,1024]{2,1,0:T(8,128)(2,1)} %pad_maximum_fusion.12), channel_id=1, source_target_pairs={{0,1},{1,0},{2,3},{3,2},{4,5},{5,4},{6,7},{7,6},{8,9},{9,8},{10,11... | collective-permute-start | bytes 3145736 | tf_op jit(solution)/shard_map/ppermute | solution.py:47
  383.6 31.3 %collective-permute-start.41 = (bf16[4,256,640]{2,1,0:T(8,128)(2,1)}, bf16[4,256,640]{2,1,0:T(8,128)(2,1)}, u32[]{:S(2)}, u32[]{:S(2)}) collective-permute-start(bf16[4,256,640]{2,1,0:T(8,128)(2,1)} %pad_maximum_fusion.3), channel_id=1, source_target_pairs={{0,16},{16,0},{1,17},{17,1},{2,18},{18,2},{3,19},{19,3},{4,20},{20... | collective-permute-start | bytes 3932168 | tf_op jit(solution)/shard_map/ppermute | solution.py:47
  384.8 35.5 %collective-permute-start.45 = (bf16[1,256,2048]{2,1,0:T(8,128)(2,1)}, bf16[1,256,2048]{2,1,0:T(8,128)(2,1)S(1)}, u32[]{:S(2)}, u32[]{:S(2)}) collective-permute-start(bf16[1,256,2048]{2,1,0:T(8,128)(2,1)} %get-tuple-element.260), channel_id=1, source_target_pairs={{0,12},{4,8},{8,4},{12,0},{1,13},{5,9},{9,5},{13,1},{2,14},{6,10},... | collective-permute-start | bytes 3145736 | tf_op jit(solution)/shard_map/ppermute | solution.py:47
  398.7 32.8 %collective-permute-start.47 = (bf16[1,256,1024]{2,1,0:T(8,128)(2,1)S(1)}, bf16[1,256,1024]{2,1,0:T(8,128)(2,1)S(1)}, u32[]{:S(2)}, u32[]{:S(2)}) collective-permute-start(bf16[1,256,1024]{2,1,0:T(8,128)(2,1)S(1)} %get-tuple-element.411), channel_id=1, source_target_pairs={{0,2},{1,3},{2,0},{3,1},{4,6},{5,7},{6,4},{7,5},{8,10},{9,11},{10,... | collective-permute-start | bytes 1572872 | tf_op jit(solution)/shard_map/ppermute | solution.py:47
  402.0 44.5 %collective-permute-start.46 = (bf16[256,2048]{1,0:T(8,128)(2,1)}, bf16[256,2048]{1,0:T(8,128)(2,1)S(1)}, u32[]{:S(2)}, u32[]{:S(2)}) collective-permute-start(bf16[256,2048]{1,0:T(8,128)(2,1)} %fusion.10), channel_id=1, source_target_pairs={{0,8},{4,12},{8,0},{12,4},{1,9},{5,13},{9,1},{13,5},{2,10},{6,14},... | collective-permute-start | bytes 3145736 | tf_op jit(solution)/shard_map/ppermute | solution.py:47
  420.3 26.3 %collective-permute-start.44 = (bf16[2,256,640]{2,1,0:T(8,128)(2,1)}, bf16[2,256,640]{2,1,0:T(8,128)(2,1)}, u32[]{:S(2)}, u32[]{:S(2)}) collective-permute-start(bf16[2,256,640]{2,1,0:T(8,128)(2,1)} %pad_maximum_fusion.13), channel_id=1, source_target_pairs={{0,1},{1,0},{2,3},{3,2},{4,5},{5,4},{6,7},{7,6},{8,9},{9,8},{10,11... | collective-permute-start | bytes 1966088 | tf_op jit(solution)/shard_map/ppermute | solution.py:47
  (109 other events, 835.9 us)
Sparse Core Ops, SparseCore 0:
  31.5 34.6 all-gather.10
  67.8 26.9 all-gather.8
  96.3 45.4 all-gather.12
  143.8 79.4 all-gather.14
